TPU v7x, 32 devices: a whole 2x2x4 slice. The times are simulated.
32 devices in a mesh: modes: 8 (over y, x, core), tiles: 4 (over z).
Axes of the slice: x: 2, y: 2, z: 4, core: 2. Of those that a mesh axis runs over, the one named last changes fastest.
Arguments:
- solution_modes: float32 [512, 16, 8, 128], P('modes', 'tiles'), may hold values from -6 to 6
- coefficient_modes: float32 [128, 16, 8, 128], P('modes', 'tiles'), may hold values from 0.5 to 4
- coupling: float32 [16, 32, 32, 32], P('modes'), may hold values from -0.03125 to 0.03125
- source_block: int32 [16, 32], P('modes'), may hold values from 0 to 15
- expansion_index: int32 [16, 32], P('modes'), may hold values from 0 to 127
Outputs:
- applied: float32 [512, 16, 8, 128], P('modes', 'tiles')
All inputs are finite; a program needn't handle non-finite values.
Results may differ from a plain program's by a relative error of at most 0.0003.
Values sent between devices are 32-bit elements; how exact they have to be, the bound alone decides.
No kernel may reach another device: no remote copies, remote signals or barrier semaphores. Data moves between devices by JAX's collectives and lax.ppermute only.
A program may use at most 128 MiB of HBM per device.

v0:
```python
import jax
import jax.numpy as jnp
from jax import lax
from jax.sharding import PartitionSpec as P


def with_halo(value, sides, width):
    for axis, dim in sides:
        count, length = (lax.axis_size(axis), value.shape[dim])
        up = [(i, (i + 1) % count) for i in range(count - 1)]
        down = [(j, i) for i, j in up]
        last = lax.slice_in_dim(value, length - width, length, axis=dim)
        initial = lax.slice_in_dim(value, 0, width, axis=dim)
        before = lax.ppermute(last, axis, up)
        after = lax.ppermute(initial, axis, down)
        value = jnp.concatenate([before, value, after], axis=dim)
    return value


def face_means(coefficient):
    along_first = 0.5 * (coefficient[:, :-1, 1:-1, 1:-1] + coefficient[:, 1:, 1:-1, 1:-1])
    along_second = 0.5 * (coefficient[:, 1:-1, :-1, 1:-1] + coefficient[:, 1:-1, 1:, 1:-1])
    along_third = 0.5 * (coefficient[:, 1:-1, 1:-1, :-1] + coefficient[:, 1:-1, 1:-1, 1:])
    return (along_first, along_second, along_third)


def divergence(blended, along_first, along_second, along_third):
    flux_first = along_first * (blended[:, :-1, 1:-1, 1:-1] - blended[:, 1:, 1:-1, 1:-1])
    flux_second = along_second * (blended[:, 1:-1, :-1, 1:-1] - blended[:, 1:-1, 1:, 1:-1])
    flux_third = along_third * (blended[:, 1:-1, 1:-1, :-1] - blended[:, 1:-1, 1:-1, 1:])
    result = flux_first[:, 1:] - flux_first[:, :-1]
    result = result + flux_second[:, :, 1:] - flux_second[:, :, :-1]
    return result + flux_third[:, :, :, 1:] - flux_third[:, :, :, :-1]


def slot_term(padded_u, faces, block_matrix, offset, expansion, width):
    first_faces, second_faces, third_faces = faces
    source_modes = lax.dynamic_slice_in_dim(padded_u, offset * width, width, 0)
    blended = jnp.einsum(
        "ij,jxyz->ixyz", block_matrix, source_modes, precision=lax.Precision.HIGHEST
    )
    return divergence(
        blended,
        lax.dynamic_index_in_dim(first_faces, expansion, 0, keepdims=False),
        lax.dynamic_index_in_dim(second_faces, expansion, 0, keepdims=False),
        lax.dynamic_index_in_dim(third_faces, expansion, 0, keepdims=False),
    )


def block_output(padded_u, faces, coupling_rows, source_rows, expansion_rows, width):
    shape = (width, padded_u.shape[1] - 2, padded_u.shape[2] - 2, padded_u.shape[3] - 2)

    def advance(running, slot_index):
        source = source_rows[slot_index]
        expansion = expansion_rows[slot_index]
        term = slot_term(padded_u, faces, coupling_rows[slot_index], source, expansion, width)
        return (running + term, None)

    start = jnp.zeros(shape, jnp.float32)
    total, _ = lax.scan(advance, start, jnp.arange(source_rows.shape[0], dtype=jnp.int32))
    return total


def on_device(solution_modes, coefficient_modes, coupling, source_block, expansion_index):
    local_solution = solution_modes.shape[0]
    local_coefficient = coefficient_modes.shape[0]
    width = coupling.shape[2]
    groups = lax.axis_size("modes")
    padding = ((0, 0), (0, 0), (1, 1), (1, 1))
    stacked = jnp.concatenate([solution_modes, coefficient_modes], axis=0)
    rimmed = with_halo(stacked, (("tiles", 1),), 1)
    everyone = lax.all_gather(rimmed, "modes", axis=0, tiled=True)
    trailing = everyone.shape[1:]
    shaped = everyone.reshape((groups, local_solution + local_coefficient) + trailing)
    all_solution = shaped[:, :local_solution].reshape((groups * local_solution,) + trailing)
    all_coefficient = shaped[:, local_solution:].reshape((groups * local_coefficient,) + trailing)
    padded_u = jnp.pad(all_solution, padding)
    padded_a = jnp.pad(all_coefficient, padding)
    faces = face_means(padded_a)
    outputs = []
    for block_index in range(source_block.shape[0]):
        outputs.append(
            block_output(
                padded_u,
                faces,
                coupling[block_index],
                source_block[block_index],
                expansion_index[block_index],
                width,
            )
        )
    return jnp.concatenate(outputs, axis=0)


def solution(mesh):
    placed = (
        P("modes", "tiles", None, None),
        P("modes", "tiles", None, None),
        P("modes", None, None, None),
        P("modes", None),
        P("modes", None),
    )
    return jax.shard_map(
        on_device,
        mesh=mesh,
        in_specs=placed,
        out_specs=P("modes", "tiles", None, None),
        check_vma=False,
    )
```

profile of v0, /device:TPU:0, one launch (start us, length us, event | category | flops | bytes accessed | tf_op | source)
XLA Modules:
  0.0 1238.7 jit_solution(8265272524221648106)
XLA Ops:
  10.2 5.7 collective-permute-start
  15.9 5.6 collective-permute-done.1
  25.4 86.8 %all-gather.2.cloned.1.call-done = f32[640,6,8,128]{3,2,1,0:T(8,128)} async-done(((f32[80,6,8,128]{3,2,1,0:T(8,128)}), f32[640,6,8,128]{3,2,1,0:T(8,128)}) %all-gather.2.cloned.1.call-update) | async-done | bytes 15728656 | tf_op jit(solution)/shard_map/all_gather | solution.py:72
  114.3 10.2 slice.191
  132.1 13.2 %copy.9 = f32[8,64,6,8,128]{4,1,0,3,2:T(8,128)} copy(f32[8,64,6,8,128]{4,3,2,1,0:T(8,128)} %slice.191) | data formatting | bytes 25165824 | tf_op jit(solution)/shard_map/slice | solution.py:75
  145.3 15.0 %pad.8 = f32[512,6,10,130]{3,0,2,1:T(8,128)} pad(f32[512,6,8,128]{3,0,2,1:T(8,128)} %bitcast.78, f32[]{:T(128)} %constant.51.clone.1), padding=0_0x0_0x1_1x1_1 | pad | bytes 28557316 | tf_op jit(solution)/shard_map/jit(_pad)/pad | solution.py:77
  160.3 533.9 %while.23 = (s32[]{:T(128)}, f32[32,4,8,128]{3,0,2,1:T(8,128)}, s32[32]{0:T(128)S(1)}, s32[32]{0:T(128)S(1)}, f32[128,5,8,128]{3,2,1,0:T(8,128)}, /*index=5*/f32...) while((s32[]{:T(128)}, f32[32,4,8,128]{3,0,2,1:T(8,128)}, ...), condition=%wide.region_3.4_spmd.clone, body=%wide.region_2.3_spmd.clone.sunk | while | flops 97650696 | bytes 12662481 | solution.py:60
  197.3 3.3 fusion.47
  214.0 3.3 fusion.47
  230.7 3.3 fusion.47
  264.1 3.3 fusion.47
  280.8 3.3 fusion.47
  297.4 3.3 fusion.47
  330.8 3.3 fusion.47
  347.5 3.3 fusion.47
  364.2 3.3 fusion.47
  397.6 3.3 fusion.47
  414.3 3.3 fusion.47
  431.0 3.3 fusion.47
  481.0 3.3 fusion.47
  497.7 3.3 fusion.47
  547.8 3.3 fusion.47
  564.5 3.3 fusion.47
  597.8 3.3 fusion.47
  614.5 3.3 fusion.47
  631.2 3.3 fusion.47
  664.6 3.3 fusion.47
  681.3 3.3 fusion.47
  696.3 532.1 %while.22 = (s32[]{:T(128)}, f32[32,4,8,128]{3,0,2,1:T(8,128)}, s32[32]{0:T(128)S(1)}, s32[32]{0:T(128)S(1)}, f32[128,5,8,128]{3,2,1,0:T(8,128)}, /*index=5*/f32...) while((s32[]{:T(128)}, f32[32,4,8,128]{3,0,2,1:T(8,128)}, ...), condition=%wide.region_1.2_spmd.clone, body=%wide.region_0.1_spmd.clone.sunk | while | flops 97650696 | bytes 12662481 | solution.py:60
  700.1 3.3 fusion.40
  716.6 3.3 fusion.40
  733.2 3.3 fusion.40
  (707 shorter events, 716.8 us)
Async XLA Ops:
  6.5 105.6 %all-gather.2.cloned.1.call-start = ((), (), s32[]{:S(2)}) async-start(), calls=%async_computation | async-start | bytes 17694720 | tf_op jit(solution)/shard_map/all_gather | solution.py:72
  8.9 12.6 %collective-permute-start.1 = (f32[80,1,8,128]{3,2,1,0:T(8,128)S(1)}, f32[80,1,8,128]{3,2,1,0:T(8,128)S(1)}, u32[]{:S(2)}, u32[]{:S(2)}) collective-permute-start(f32[80,1,8,128]{3,2,1,0:T(8,128)S(1)} %get-tuple-element.218), channel_id=1, source_target_pairs={{1,0},{2,1},{3,2},{5,4},{6,5},{7,6},{9,8},{10,9},{11,10},{13,12},{... | collective-permute-start | bytes 983048 | tf_op jit(solution)/shard_map/ppermute | solution.py:15
  10.2 14.1 %copy-start.1 = (s32[2,32]{1,0:T(2,128)S(1)}, s32[2,32]{1,0:T(2,128)}, u32[]{:S(2)}) copy-start(s32[2,32]{1,0:T(2,128)} %param.12) | copy-start | bytes 772
  10.2 14.1 %copy-start.2 = (s32[2,32]{1,0:T(2,128)S(1)}, s32[2,32]{1,0:T(2,128)}, u32[]{:S(2)}) copy-start(s32[2,32]{1,0:T(2,128)} %param.13) | copy-start | bytes 772
  10.2 14.1 %copy-start = (f32[2,32,32,32]{3,2,1,0:T(8,128)S(1)}, f32[2,32,32,32]{3,2,1,0:T(8,128)}, u32[]{:S(2)}) copy-start(f32[2,32,32,32]{3,2,1,0:T(8,128)} %param.11) | copy-start | bytes 786436
  10.2 12.6 %collective-permute-start = (f32[80,1,8,128]{3,2,1,0:T(8,128)S(1)}, f32[80,1,8,128]{3,2,1,0:T(8,128)S(1)}, u32[]{:S(2)}, u32[]{:S(2)}) collective-permute-start(f32[80,1,8,128]{3,2,1,0:T(8,128)S(1)} %get-tuple-element.217), channel_id=1, source_target_pairs={{0,1},{1,2},{2,3},{4,5},{5,6},{6,7},{8,9},{9,10},{10,11},{12,13},{... | collective-permute-start | bytes 983048 | tf_op jit(solution)/shard_map/ppermute | solution.py:14
Sparse Core Ops, SparseCore 0:
  24.4 87.7 all-gather.1
where the time goes:
time: 1260 us; the launch traced here: 1240 us
  other arithmetic  315 us (25%)
  local copies, waits for them, and re-layouts  305 us (24%)
  loops' own time  292 us (23%)
  matrix products  212 us (17%)
  waiting for transfers between devices  93.7 us (7%)
  between operations  13.5 us (1%)
    another operation x2, loops' own time, block_output(): lax.scan(advance, start, jnp.arange(source_rows.shape[0], dtype=jnp.int32))  292 us
    dot_general x64, matrix products, slot_term(): jnp.einsum('ij,jxyz->ixyz', block_matrix, source_modes, precision=lax.Pre...  212 us
    add x64, other arithmetic, advance(): return (running + term, None)  170 us
    all_gather x1, waiting for transfers between devices, on_device(): everyone = lax.all_gather(rimmed, 'modes', axis=0, tiled=True)  86.8 us
    mul x64, other arithmetic, divergence(): along_third * (blended[:, 1:-1, 1:-1, :-1] - blended[:, 1:-1, 1:-1, 1:])  84.7 us
    mul x64, local copies, waits for them, and re-layouts, divergence(): along_third * (blended[:, 1:-1, 1:-1, :-1] - blended[:, 1:-1, 1:-1, 1:])  49 us
    mul x64, local copies, waits for them, and re-layouts, divergence(): along_second * (blended[:, 1:-1, :-1, 1:-1] - blended[:, 1:-1, 1:, 1:-1])  48.6 us
    mul x64, local copies, waits for them, and re-layouts, divergence(): along_first * (blended[:, :-1, 1:-1, 1:-1] - blended[:, 1:, 1:-1, 1:-1])  47.1 us
  transfers between devices with their start and end apart: 3, of which 3 were waited for; matrix products, arithmetic and copies ran while one was open for 0% of the time, Pallas kernels for 0%

commit v1 on v0

v1 whole, which is shorter than its diff:
```python
import functools

import jax
import jax.numpy as jnp
from jax import lax
from jax.experimental import pallas as pl
from jax.experimental.pallas import tpu as pltpu
from jax.sharding import PartitionSpec as P

VMEM_LIMIT = 56 * 1024 * 1024
CHUNK = 4


def lane_index(rows):
    return lax.broadcasted_iota(jnp.int32, (rows, 128), 1)


def swap_lanes(tiles, depth, lanes):
    tiles = list(tiles)
    size = len(tiles)
    step = 1
    while step < size:
        width = step * depth
        upper = (lanes & width) != 0
        for low in range(size):
            if low & step:
                continue
            high = low | step
            first, second = tiles[low], tiles[high]
            tiles[low] = jnp.where(upper, pltpu.roll(second, width, 1), first)
            tiles[high] = jnp.where(upper, second, pltpu.roll(first, 128 - width, 1))
        step *= 2
    return tiles


def turn(value, shift):
    shift = shift % 128
    return value if shift == 0 else pltpu.roll(value, shift, 1)


def pack_kernel(
    geometry, chip_ref, u_ref, a_ref, coupling_ref, index_ref, *rest
):
    layers, halves, ny, depth, chips = geometry
    sends, packs, stage = rest[:chips], rest[chips], rest[chips + 1]
    me = chip_ref[0]
    lanes = lane_index(8)
    place = lanes % depth
    row = 0
    for ref in (u_ref, a_ref):
        modes = ref.shape[0] // (layers * ny)

        def group(g, carry, ref=ref, row=row):
            target = pl.multiple_of(row + g * 8, 8)
            by_layer = []
            for x in range(layers):
                tiles = [
                    ref[pl.ds(g * 8 * layers * ny + x * ny + y, 8, stride=layers * ny), :]
                    for y in range(ny)
                ]
                tiles = swap_lanes(tiles, depth, lanes)
                by_layer.append(tiles)
                for d in range(ny):
                    stage[d // halves, x * halves + d % halves, pl.ds(target, 8), :] = tiles[d]
            for chip in range(chips):
                rim = jnp.zeros((8, 128), jnp.float32)
                left, right = chip * halves - 1, (chip + 1) * halves
                for x in range(layers):
                    if left >= 0:
                        rim = jnp.where(place == x, turn(by_layer[x][left], x + 1 - depth), rim)
                    if right < ny:
                        at = depth // 2 + x
                        rim = jnp.where(place == at, turn(by_layer[x][right], at), rim)
                stage[chip, layers * halves, pl.ds(target, 8), :] = rim
            return carry

        lax.fori_loop(0, modes // 8, group, 0)
        row += modes
    for e in range(chips):
        sends[e][...] = stage[e ^ me]
    blocks, slots, width, _ = coupling_ref.shape
    per = 128 // width
    groups = slots // per
    for block in range(blocks):

        def gather(g, carry, block=block):
            packs[block * groups + g] = jnp.concatenate(
                [coupling_ref[block, g * per + q] for q in range(per)], axis=1
            )
            return carry

        lax.fori_loop(0, groups, gather, 0)
    packs[blocks * groups] = index_ref[...]


def laplacian(tile, low, high, rim, geometry, rows):
    layers, halves, ny, depth, _ = geometry
    lanes = lane_index(rows)
    place = lanes % depth
    first_row, last_row = lanes < depth, lanes >= 128 - depth
    result = []
    for x in range(layers):
        result.append([])
        for h in range(halves):
            c = tile[x][h]
            before = tile[x - 1][h] if x else low[h]
            after = tile[x + 1][h] if x + 1 < layers else high[h]
            up = jnp.where(first_row, 0.0, turn(c, depth))
            down = jnp.where(last_row, 0.0, turn(c, -depth))
            edge = turn(tile[x][h - 1], 1 - depth) if h else turn(rim, -x)
            left = jnp.where(place == 0, edge, turn(c, 1))
            if h + 1 < halves:
                edge = turn(tile[x][h + 1], depth - 1)
            else:
                edge = turn(rim, depth - 1 - depth // 2 - x)
            right = jnp.where(place == depth - 1, edge, turn(c, -1))
            result[-1].append(((before + after) + (up + down)) + ((left + right) - 6.0 * c))
    return result


def halves_of(value):
    upper = value.astype(jnp.bfloat16)
    lower = (value - upper.astype(jnp.float32)).astype(jnp.bfloat16)
    return upper, lower


def apply_kernel(geometry, sizes, where_ref, source_ref, expansion_ref, *rest):
    layers, halves, ny, depth, chips = geometry
    blocks, width, slots, local_u, local_a = sizes
    tiles = layers * halves
    chunks = tiles // CHUNK
    span = CHUNK * 128
    rim_at = chunks * 2 * span
    take = lambda n: (rest[:n], rest[n:])
    bodies, rest = take(2 * chips)
    lows, rest = take(2)
    highs, rest = take(2)
    packs, rest = take(chips)
    out_ref, sources, fields, mix, product, cross = rest
    chip, core = where_ref[0], where_ref[1]

    def columns(t):
        base = (t // CHUNK) * 2 * span + (t % CHUNK) * 128
        return base, base + span

    def load(body, low, high, e, start, rows):
        part = pl.ds(start, rows)
        tile = [[body[x * halves + h, part, :] for h in range(halves)] for x in range(layers)]
        below = [low[e, h, part, :] for h in range(halves)]
        above = [high[e, h, part, :] for h in range(halves)]
        return tile, below, above, body[tiles, part, :]

    for side in range(2):
        for e in range(chips):
            body, low, high = bodies[side * chips + e], lows[side], highs[side]
            device = (chip ^ e) * 2 + (core ^ side)

            def prepare_u(g, carry, body=body, low=low, high=high, e=e, device=device):
                start = pl.multiple_of(g * 16, 16)
                tile, below, above, rim = load(body, low, high, e, start, 16)
                lap = laplacian(tile, below, above, rim, geometry, 16)
                block = device * (local_u // width) + (g * 16) // width
                row = pl.multiple_of((g * 16) % width, 16)

                def put(value, at):
                    upper, lower = halves_of(value)
                    where = pl.ds(at, 128)
                    sources[block, pl.ds(row, 16), where] = upper
                    sources[block, pl.ds(width + row, 16), where] = lower
                    sources[block, pl.ds(2 * width + row, 16), where] = upper

                for t in range(tiles):
                    x, h = t // halves, t % halves
                    put(tile[x][h], columns(t)[0])
                    put(lap[x][h], columns(t)[1])
                for h in range(halves):
                    put(below[h], rim_at + h * 128)
                    put(above[h], rim_at + (halves + h) * 128)
                put(rim, rim_at + 2 * halves * 128)
                return carry

            lax.fori_loop(0, local_u // 16, prepare_u, 0)
            tile, below, above, rim = load(body, low, high, e, local_u, local_a)
            lap = laplacian(tile, below, above, rim, geometry, local_a)
            rows = pl.ds(pl.multiple_of(device * local_a, local_a), local_a)
            for t in range(tiles):
                x, h = t // halves, t % halves
                fields[rows, pl.ds(columns(t)[0], 128)] = tile[x][h]
                fields[rows, pl.ds(columns(t)[1], 128)] = lap[x][h]
            for h in range(halves):
                fields[rows, pl.ds(rim_at + h * 128, 128)] = below[h]
                fields[rows, pl.ds(rim_at + (halves + h) * 128, 128)] = above[h]
            fields[rows, pl.ds(rim_at + 2 * halves * 128, 128)] = rim

    per = 128 // width
    groups = slots // per
    for e in range(chips):

        def spread(n, carry, e=e):
            value = packs[e][n]
            upper = value.astype(jnp.bfloat16).astype(jnp.float32)
            lower = value - upper
            for q in range(per):
                lanes = slice(q * width, (q + 1) * width)
                part = jnp.concatenate([upper[:, lanes], upper[:, lanes], lower[:, lanes]], axis=1)
                mix[e * blocks * slots + n * per + q] = part.astype(jnp.bfloat16)
            return carry

        lax.fori_loop(0, blocks * groups, spread, 0)

    rims = (2 * halves + 1) * 128

    def one_block(n, carry):
        for chunk in range(chunks):
            base = chunk * 2 * span

            def step(s, totals, base=base):
                total, rest_total = totals
                at = n * slots + s
                j, k = source_ref[at], expansion_ref[at]
                mixed = jnp.dot(
                    mix[at],
                    sources[j, :, base : base + 2 * span],
                    preferred_element_type=jnp.float32,
                )
                field = fields[pl.ds(k, 1), base : base + span]
                bent = fields[pl.ds(k, 1), base + span : base + 2 * span]
                value, curve = mixed[:, :span], mixed[:, span:]
                return total + field * value, rest_total + (bent * value - field * curve)

            zero = jnp.zeros((width, span), jnp.float32)
            total, rest_total = lax.fori_loop(0, slots, step, (zero, zero), unroll=4)
            for i in range(CHUNK):
                product[chunk * CHUNK + i] = total[:, i * 128 : (i + 1) * 128]
                cross[chunk * CHUNK + i] = rest_total[:, i * 128 : (i + 1) * 128]

        def rim_step(s, total):
            at = n * slots + s
            j, k = source_ref[at], expansion_ref[at]
            mixed = jnp.dot(
                mix[at],
                sources[j, :, rim_at : rim_at + rims],
                preferred_element_type=jnp.float32,
            )
            return total + fields[pl.ds(k, 1), rim_at : rim_at + rims] * mixed

        total = lax.fori_loop(0, slots, rim_step, jnp.zeros((width, rims), jnp.float32), unroll=4)
        for i in range(2 * halves + 1):
            product[tiles + i] = total[:, i * 128 : (i + 1) * 128]

        for r in range(0, width, 8):
            part = slice(r, r + 8)
            tile = [[product[x * halves + h, part, :] for h in range(halves)] for x in range(layers)]
            low = [product[tiles + h, part, :] for h in range(halves)]
            high = [product[tiles + halves + h, part, :] for h in range(halves)]
            rim = product[tiles + 2 * halves, part, :]
            lap = laplacian(tile, low, high, rim, geometry, 8)
            for t in range(tiles):
                row = pl.multiple_of((n % blocks) * width + r, 8)
                out_ref[n // blocks, t, pl.ds(row, 8), :] = 0.5 * (
                    cross[t, part, :] - lap[t // halves][t % halves]
                )
        return carry

    lax.fori_loop(0, chips * blocks, one_block, 0)


def unpack_kernel(geometry, chip_ref, *rest):
    layers, halves, ny, depth, chips = geometry
    parts, out_ref, stage = rest[:chips], rest[chips], rest[chips + 1]
    me = chip_ref[0]
    for e in range(chips):
        stage[e ^ me] = parts[e][...]
    lanes = lane_index(8)
    modes = out_ref.shape[0] // (layers * ny)

    def group(g, carry):
        source = pl.multiple_of(g * 8, 8)
        for x in range(layers):
            tiles = [
                stage[d // halves, x * halves + d % halves, pl.ds(source, 8), :] for d in range(ny)
            ]
            tiles = swap_lanes(tiles, depth, lanes)
            for y in range(ny):
                out_ref[pl.ds(g * 8 * layers * ny + x * ny + y, 8, stride=layers * ny), :] = tiles[y]
        return carry

    lax.fori_loop(0, modes // 8, group, 0)


def vmem(count):
    return [pl.BlockSpec(memory_space=pltpu.VMEM)] * count


def smem(count):
    return [pl.BlockSpec(memory_space=pltpu.SMEM)] * count


def on_device(solution_modes, coefficient_modes, coupling, source_block, expansion_index):
    local_u, layers, ny, nz = solution_modes.shape
    local_a = coefficient_modes.shape[0]
    blocks, slots, width = coupling.shape[:3]
    count = lax.axis_size("modes")
    chips = count // 2
    depth = 128 // ny
    halves = (nz // depth) // chips
    geometry = (layers, halves, ny, depth, chips)
    tiles = layers * halves
    modes = local_u + local_a
    me = lax.axis_index("modes")
    chip, core = me // 2, me % 2
    f32 = jnp.float32
    params = pltpu.CompilerParams(vmem_limit_bytes=VMEM_LIMIT)

    flat = jnp.stack([source_block, expansion_index]).astype(f32).reshape(-1)
    indices = jnp.zeros((width * 128,), f32).at[: flat.size].set(flat).reshape(width, 128)
    per = 128 // width
    groups = slots // per
    packed = pl.pallas_call(
        functools.partial(pack_kernel, geometry),
        out_shape=[jax.ShapeDtypeStruct((tiles + 1, modes, 128), f32)] * chips
        + [jax.ShapeDtypeStruct((blocks * groups + 1, width, 128), f32)],
        in_specs=smem(1) + vmem(4),
        out_specs=vmem(chips + 1),
        scratch_shapes=[pltpu.VMEM((chips, tiles + 1, modes, 128), f32)],
        compiler_params=params,
        name="pack",
    )(
        chip[None],
        solution_modes.reshape(-1, nz),
        coefficient_modes.reshape(-1, nz),
        coupling,
        indices,
    )
    sends, pack = packed[:chips], packed[chips]

    def trade(value, e):
        return lax.ppermute(value, "modes", [(i, i ^ (2 * e)) for i in range(count)])

    def sibling(value):
        return lax.ppermute(value, "modes", [(i, i ^ 1) for i in range(count)])

    packs = [pack] + [trade(pack, e) for e in range(1, chips)]
    bodies = [sends[0]] + [trade(sends[e], e) for e in range(1, chips)]
    n_tiles = lax.axis_size("tiles")
    up = [(i, i + 1) for i in range(n_tiles - 1)]
    down = [(i + 1, i) for i in range(n_tiles - 1)]
    bottom = jnp.stack([body[:halves] for body in bodies])
    top = jnp.stack([body[tiles - halves : tiles] for body in bodies])
    low, high = lax.ppermute(top, "tiles", up), lax.ppermute(bottom, "tiles", down)
    bodies = bodies + [sibling(body) for body in bodies]
    low_other, high_other = sibling(low), sibling(high)

    numbers = jnp.stack([p[blocks * groups] for p in packs]).reshape(chips, -1)
    numbers = numbers[:, : 2 * blocks * slots].astype(jnp.int32).reshape(chips, 2, blocks * slots)
    sources = numbers[:, 0].reshape(-1)
    expansions = numbers[:, 1].reshape(-1)

    ncol = 2 * tiles * 128 + (2 * halves + 1) * 128
    n_blocks = chips * 2 * (local_u // width)
    result = pl.pallas_call(
        functools.partial(
            apply_kernel, geometry, (blocks, width, slots, local_u, local_a)
        ),
        out_shape=jax.ShapeDtypeStruct((chips, tiles, local_u, 128), f32),
        in_specs=smem(3) + vmem(2 * chips + 4 + chips),
        out_specs=pl.BlockSpec(memory_space=pltpu.VMEM),
        scratch_shapes=[
            pltpu.VMEM((n_blocks, 3 * width, ncol), jnp.bfloat16),
            pltpu.VMEM((chips * 2 * local_a, ncol), f32),
            pltpu.VMEM((chips * blocks * slots, width, 3 * width), jnp.bfloat16),
            pltpu.VMEM((tiles + 2 * halves + 1, width, 128), f32),
            pltpu.VMEM((tiles, width, 128), f32),
        ],
        compiler_params=params,
        name="apply",
    )(
        jnp.stack([chip, core]),
        sources,
        expansions,
        *bodies,
        low,
        low_other,
        high,
        high_other,
        *packs,
    )
    parts = [result[0]] + [trade(result[e], e) for e in range(1, chips)]
    out = pl.pallas_call(
        functools.partial(unpack_kernel, geometry),
        out_shape=jax.ShapeDtypeStruct((local_u * layers * ny, nz), f32),
        in_specs=smem(1) + vmem(chips),
        out_specs=pl.BlockSpec(memory_space=pltpu.VMEM),
        scratch_shapes=[pltpu.VMEM((chips, tiles, local_u, 128), f32)],
        compiler_params=params,
        name="unpack",
    )(chip[None], *parts)
    return out.reshape(solution_modes.shape)


def solution(mesh):
    placed = (
        P("modes", "tiles", None, None),
        P("modes", "tiles", None, None),
        P("modes", None, None, None),
        P("modes", None),
        P("modes", None),
    )
    return jax.shard_map(
        on_device,
        mesh=mesh,
        in_specs=placed,
        out_specs=P("modes", "tiles", None, None),
        check_vma=False,
    )
```

time: 1260 us -> 150 us (0.12); the launches traced: 1240 us -> 150 us
  other arithmetic: 315 us -> 2.29 us
  local copies, waits for them, and re-layouts: 305 us -> 9.33 us
  loops' own time: 292 us -> 0 us
  matrix products: 212 us -> 0 us
  Pallas kernels: 0 us -> 76.4 us
  waiting for transfers between devices: 93.7 us -> 41.4 us
  between operations: 13.5 us -> 0.17 us
  starting transfers between devices: 7 us -> 20 us
    another operation x2 -> x0, loops' own time: 292 us -> none  [block_output(): lax.scan(advance, start, jnp.arange(source_rows.shape[0], dtype=jnp.int32))]
    dot_general x64 -> x0, matrix products: 212 us -> none  [slot_term(): jnp.einsum('ij,jxyz->ixyz', block_matrix, source_modes, precision=lax.Pre...]
    add x64 -> x0, other arithmetic: 170 us -> none  [advance(): return (running + term, None)]
    mul x192 -> x0, local copies, waits for them, and re-layouts: 145 us -> none  [the longest x64 49 us: divergence(): along_third * (blended[:, 1:-1, 1:-1, :-1] - blended[:, 1:-1, 1:-1, 1:])]
    mul x195 -> x0, other arithmetic: 142 us -> none  [the longest x64 84.7 us: divergence(): along_third * (blended[:, 1:-1, 1:-1, :-1] - blended[:, 1:-1, 1:-1, 1:])]
    dynamic_slice x192 -> x0, local copies, waits for them, and re-layouts: 112 us -> none  [the longest x64 37.7 us: advance(): expansion = expansion_rows[slot_index]]
    all_gather x1 -> x0, waiting for transfers between devices: 86.8 us -> none  [on_device(): everyone = lax.all_gather(rimmed, 'modes', axis=0, tiled=True)]
    pallas_call x0 -> x3, Pallas kernels: none -> 76.4 us  [the longest x1 64.5 us: on_device(): pl.pallas_call(functools.partial(apply_kernel, geometry, (blocks, width,...]
  transfers between devices with their start and end apart: 3 -> 17, of which waited for: 3 -> 7; matrix products, arithmetic and copies ran while one was open for 0% -> 4% of each run, Pallas kernels for 0% -> 0%
where the time goes in v1:
time: 150 us
  Pallas kernels  76.4 us (51%)
  waiting for transfers between devices  41.4 us (28%)
  starting transfers between devices  20 us (13%)
  local copies, waits for them, and re-layouts  9.33 us (6%)
  other arithmetic  2.29 us (2%)
    pallas_call x1, Pallas kernels, on_device(): pl.pallas_call(functools.partial(apply_kernel, geometry, (blocks, width,...  64.5 us
    ppermute x9, waiting for transfers between devices, trade(): return lax.ppermute(value, 'modes', [(i, i ^ 2 * e) for i in range(count)])  34.1 us
    ppermute x9, starting transfers between devices, trade(): return lax.ppermute(value, 'modes', [(i, i ^ 2 * e) for i in range(count)])  14.5 us
    pallas_call x1, Pallas kernels, on_device(): pl.pallas_call(functools.partial(pack_kernel, geometry), out_shape=[jax.S...  7.44 us
    ppermute x1, waiting for transfers between devices, on_device(): lax.ppermute(bottom, 'tiles', down)  4.77 us
    pallas_call x1, Pallas kernels, on_device(): pl.pallas_call(functools.partial(unpack_kernel, geometry), out_shape=jax....  4.42 us
    ppermute x1, starting transfers between devices, on_device(): lax.ppermute(top, 'tiles', up)  3.49 us
  transfers between devices with their start and end apart: 17, of which 7 were waited for; matrix products, arithmetic and copies ran while one was open for 4% of the time, Pallas kernels for 0%

profile of v1, /device:TPU:0, one launch (start us, length us, event | category | flops | bytes accessed | tf_op | source)
XLA Modules:
  0.0 149.5 jit_solution(1732021801597354099)
XLA Ops:
  0.0 0.7 copy-done.16
  0.8 0.6 pad_bitcast_fusion.index_ref
  1.4 7.4 %pack.1 = (f32[9,80,128]{2,1,0:T(8,128)}, f32[9,80,128]{2,1,0:T(8,128)}, f32[9,80,128]{2,1,0:T(8,128)}, f32[9,80,128]{2,1,0:T(8,128)}, f32[17,32,128]{2,1,0:T(8,128)}) custom-call(s32[1]{0:T(128)} %bitcast.chip_ref, f32[2048,128]{1,0:T(8,128)} %bitcast.38, f32[512,128]{1,0:T(8,128)} %bitcast.39, f32[2,32,32,32]{3,2,1,0:T(8,128)} %coupling_ref.1, ...), custom_call_target="tpu_custom_call" | custom-call | tf_op jit(solution)/shard_map/pack/pallas_call | solution.py:319
  8.8 2.9 %collective-permute-start.3 = (f32[9,80,128]{2,1,0:T(8,128)}, f32[9,80,128]{2,1,0:T(8,128)S(1)}, u32[]{:S(2)}, u32[]{:S(2)}) collective-permute-start(f32[9,80,128]{2,1,0:T(8,128)} %get-tuple-element.24), channel_id=1, source_target_pairs={{0,8},{4,12},{8,0},{12,4},{16,24},{20,28},{24,16},{28,20},{1,9},{5... | collective-permute-start | bytes 1105928 | tf_op jit(solution)/shard_map/ppermute | solution.py:338
  11.8 1.5 collective-permute-start.2
  13.3 2.0 %collective-permute-start = (f32[17,32,128]{2,1,0:T(8,128)}, f32[17,32,128]{2,1,0:T(8,128)}, u32[]{:S(2)}, u32[]{:S(2)}) collective-permute-start(f32[17,32,128]{2,1,0:T(8,128)} %get-tuple-element.22.rest_12_), channel_id=1, source_target_pairs={{0,8},{4,12},{8,0},{12,4},{16,24},{20,28},{24,16},{28,20},{1,9},{5... | collective-permute-start | bytes 835592 | tf_op jit(solution)/shard_map/ppermute | solution.py:338
  15.3 1.5 %collective-permute-start.4 = (f32[9,80,128]{2,1,0:T(8,128)}, f32[9,80,128]{2,1,0:T(8,128)S(1)}, u32[]{:S(2)}, u32[]{:S(2)}) collective-permute-start(f32[9,80,128]{2,1,0:T(8,128)} %get-tuple-element.25), channel_id=1, source_target_pairs={{0,16},{4,20},{8,24},{12,28},{16,0},{20,4},{24,8},{28,12},{1,17},{... | collective-permute-start | bytes 1105928 | tf_op jit(solution)/shard_map/ppermute | solution.py:338
  16.8 0.9 slice_bitcast_fusion.10
  17.7 3.7 %collective-permute-done.3.rest_1_ = f32[9,80,128]{2,1,0:T(8,128)S(1)} collective-permute-done((f32[9,80,128]{2,1,0:T(8,128)}, f32[9,80,128]{2,1,0:T(8,128)S(1)}, u32[]{:S(2)}, u32[]{:S(2)}) %collective-permute-start.3) | collective-permute-done | bytes 368672 | tf_op jit(solution)/shard_map/ppermute | solution.py:338
  21.4 3.0 %collective-permute-start.5 = (f32[9,80,128]{2,1,0:T(8,128)}, f32[9,80,128]{2,1,0:T(8,128)S(1)}, u32[]{:S(2)}, u32[]{:S(2)}) collective-permute-start(f32[9,80,128]{2,1,0:T(8,128)} %get-tuple-element.26), channel_id=1, source_target_pairs={{0,24},{4,28},{8,16},{12,20},{16,8},{20,12},{24,0},{28,4},{1,25},{... | collective-permute-start | bytes 1105928 | tf_op jit(solution)/shard_map/ppermute | solution.py:338
  24.4 18.6 %collective-permute-done.4.rest_2_ = f32[9,80,128]{2,1,0:T(8,128)S(1)} collective-permute-done((f32[9,80,128]{2,1,0:T(8,128)}, f32[9,80,128]{2,1,0:T(8,128)S(1)}, u32[]{:S(2)}, u32[]{:S(2)}) %collective-permute-start.4) | collective-permute-done | bytes 368672 | tf_op jit(solution)/shard_map/ppermute | solution.py:338
  43.2 0.9 pad_maximum_fusion
  44.0 3.5 %collective-permute-start.10 = (f32[4,2,80,128]{3,2,1,0:T(8,128)}, f32[4,2,80,128]{3,2,1,0:T(8,128)S(1)}, u32[]{:S(2)}, u32[]{:S(2)}) collective-permute-start(f32[4,2,80,128]{3,2,1,0:T(8,128)} %pad_maximum_fusion), channel_id=1, source_target_pairs={{0,1},{1,2},{2,3},{4,5},{5,6},{6,7},{8,9},{9,10},{10,11},{12,13},{... | collective-permute-start | bytes 983048 | tf_op jit(solution)/shard_map/ppermute | solution.py:350
  47.5 0.8 pad_maximum_fusion.1
  48.3 1.3 collective-permute-start.12
  49.6 0.7 slice.68
  50.3 0.7 pad_add_fusion.where_ref
  51.0 0.7 copy-done.11
  51.7 0.7 slice.87
  53.2 2.2 %collective-permute-done.10.rest_8_ = f32[4,2,80,128]{3,2,1,0:T(8,128)S(1)} collective-permute-done((f32[4,2,80,128]{3,2,1,0:T(8,128)}, f32[4,2,80,128]{3,2,1,0:T(8,128)S(1)}, u32[]{:S(2)}, u32[]{:S(2)}) %collective-permute-start.10) | collective-permute-done | bytes 327712 | tf_op jit(solution)/shard_map/ppermute | solution.py:350
  55.4 4.8 %collective-permute-done.12.rest_10_ = f32[4,2,80,128]{3,2,1,0:T(8,128)S(1)} collective-permute-done((f32[4,2,80,128]{3,2,1,0:T(8,128)}, f32[4,2,80,128]{3,2,1,0:T(8,128)S(1)}, u32[]{:S(2)}, u32[]{:S(2)}) %collective-permute-start.12) | collective-permute-done | bytes 327712 | tf_op jit(solution)/shard_map/ppermute | solution.py:350
  60.3 0.7 reshape_squeeze.7.expansion_ref
  60.9 0.6 reshape_squeeze.6.source_ref
  62.5 64.5 %apply.1 = f32[4,8,64,128]{3,2,1,0:T(8,128)} custom-call(s32[2]{0:T(128)} %pad_add_fusion.where_ref, s32[256]{0:T(256)} %reshape_squeeze.6.source_ref, s32[256]{0:T(256)} %reshape_squeeze.7.expansion_ref, f32[9,80,128]{2,1,0:T(8,128)} %get-tuple-element.23.rest_0_, f32[9,80,128]{2,1,0:T(8,128)} %copy-done.1, f32[9,80,128]{2,1,0:T(8,128)} %copy-done.2, ...), custom_call_target="tpu_custom_call" | custom-call | tf_op jit(solution)/shard_map/apply/pallas_call | solution.py:361
  127.1 2.0 %slice_bitcast_fusion = (f32[8,64,128]{2,1,0:T(8,128)S(1)}, f32[8,64,128]{2,1,0:T(8,128)S(1)}, f32[8,64,128]{2,1,0:T(8,128)S(1)}, f32[8,64,128]{2,1,0:T(8,128)}) fusion(f32[4,8,64,128]{3,2,1,0:T(8,128)} %apply.1), kind=kLoop, calls=%fused_computation.2 | loop fusion | bytes 2097152 | tf_op jit(solution)/shard_map/squeeze | solution.py:388
  129.1 1.4 collective-permute-start.16
  130.5 1.5 %collective-permute-start.15 = (f32[8,64,128]{2,1,0:T(8,128)S(1)}, f32[8,64,128]{2,1,0:T(8,128)S(1)}, u32[]{:S(2)}, u32[]{:S(2)}) collective-permute-start(f32[8,64,128]{2,1,0:T(8,128)S(1)} %get-tuple-element.30), channel_id=1, source_target_pairs={{0,16},{4,20},{8,24},{12,28},{16,0},{20,4},{24,8},{28,12},{1,17},{... | collective-permute-start | bytes 786440 | tf_op jit(solution)/shard_map/ppermute | solution.py:338
  132.0 0.5 collective-permute-start.14
  132.6 6.5 %collective-permute-done.16.rest_3_ = f32[8,64,128]{2,1,0:T(8,128)S(1)} collective-permute-done((f32[8,64,128]{2,1,0:T(8,128)S(1)}, f32[8,64,128]{2,1,0:T(8,128)S(1)}, u32[]{:S(2)}, u32[]{:S(2)}) %collective-permute-start.16) | collective-permute-done | bytes 262176 | tf_op jit(solution)/shard_map/ppermute | solution.py:338
  139.1 5.2 %collective-permute-done.15.rest_2_ = f32[8,64,128]{2,1,0:T(8,128)S(1)} collective-permute-done((f32[8,64,128]{2,1,0:T(8,128)S(1)}, f32[8,64,128]{2,1,0:T(8,128)S(1)}, u32[]{:S(2)}, u32[]{:S(2)}) %collective-permute-start.15) | collective-permute-done | bytes 262176 | tf_op jit(solution)/shard_map/ppermute | solution.py:338
  144.3 0.7 copy-done.13
  145.1 4.4 %unpack.1 = f32[2048,128]{1,0:T(8,128)} custom-call(s32[1]{0:T(128)} %bitcast.chip_ref, f32[8,64,128]{2,1,0:T(8,128)} %get-tuple-element.32.rest_0_, f32[8,64,128]{2,1,0:T(8,128)} %copy-done.14, f32[8,64,128]{2,1,0:T(8,128)} %copy-done.13, f32[8,64,128]{2,1,0:T(8,128)} %copy-done.12), custom_call_target="tpu_custom_call" | custom-call | tf_op jit(solution)/shard_map/unpack/pallas_call | solution.py:389
  (61 shorter events, 2.2 us)
Async XLA Ops:
  8.8 34.3 %copy-start = (f32[9,80,128]{2,1,0:T(8,128)S(1)}, f32[9,80,128]{2,1,0:T(8,128)}, u32[]{:S(2)}) copy-start(f32[9,80,128]{2,1,0:T(8,128)} %get-tuple-element.23.rest_0_) | copy-start | bytes 1105924
  8.8 12.6 %collective-permute-start.3 = (f32[9,80,128]{2,1,0:T(8,128)}, f32[9,80,128]{2,1,0:T(8,128)S(1)}, u32[]{:S(2)}, u32[]{:S(2)}) collective-permute-start(f32[9,80,128]{2,1,0:T(8,128)} %get-tuple-element.24), channel_id=1, source_target_pairs={{0,8},{4,12},{8,0},{12,4},{16,24},{20,28},{24,16},{28,20},{1,9},{5... | collective-permute-start | bytes 1105928 | tf_op jit(solution)/shard_map/ppermute | solution.py:338
  11.8 36.5 %collective-permute-start.2 = (f32[17,32,128]{2,1,0:T(8,128)}, f32[17,32,128]{2,1,0:T(8,128)S(1)}, u32[]{:S(2)}, u32[]{:S(2)}) collective-permute-start(f32[17,32,128]{2,1,0:T(8,128)} %get-tuple-element.22.rest_12_), channel_id=1, source_target_pairs={{0,24},{4,28},{8,16},{12,20},{16,8},{20,12},{24,0},{28,4},{1,25},{... | collective-permute-start | bytes 835592 | tf_op jit(solution)/shard_map/ppermute | solution.py:338
  13.3 37.7 %collective-permute-start.1 = (f32[17,32,128]{2,1,0:T(8,128)}, f32[17,32,128]{2,1,0:T(8,128)S(1)}, u32[]{:S(2)}, u32[]{:S(2)}) collective-permute-start(f32[17,32,128]{2,1,0:T(8,128)} %get-tuple-element.22.rest_12_), channel_id=1, source_target_pairs={{0,16},{4,20},{8,24},{12,28},{16,0},{20,4},{24,8},{28,12},{1,17},{... | collective-permute-start | bytes 835592 | tf_op jit(solution)/shard_map/ppermute | solution.py:338
  13.3 37.7 %collective-permute-start = (f32[17,32,128]{2,1,0:T(8,128)}, f32[17,32,128]{2,1,0:T(8,128)}, u32[]{:S(2)}, u32[]{:S(2)}) collective-permute-start(f32[17,32,128]{2,1,0:T(8,128)} %get-tuple-element.22.rest_12_), channel_id=1, source_target_pairs={{0,8},{4,12},{8,0},{12,4},{16,24},{20,28},{24,16},{28,20},{1,9},{5... | collective-permute-start | bytes 835592 | tf_op jit(solution)/shard_map/ppermute | solution.py:338
  15.3 27.8 %collective-permute-start.4 = (f32[9,80,128]{2,1,0:T(8,128)}, f32[9,80,128]{2,1,0:T(8,128)S(1)}, u32[]{:S(2)}, u32[]{:S(2)}) collective-permute-start(f32[9,80,128]{2,1,0:T(8,128)} %get-tuple-element.25), channel_id=1, source_target_pairs={{0,16},{4,20},{8,24},{12,28},{16,0},{20,4},{24,8},{28,12},{1,17},{... | collective-permute-start | bytes 1105928 | tf_op jit(solution)/shard_map/ppermute | solution.py:338
  21.4 31.0 %copy-start.1 = (f32[9,80,128]{2,1,0:T(8,128)}, f32[9,80,128]{2,1,0:T(8,128)S(1)}, u32[]{:S(2)}) copy-start(f32[9,80,128]{2,1,0:T(8,128)S(1)} %collective-permute-done.3.rest_1_) | copy-start | bytes 1105924
  21.4 21.7 %collective-permute-start.5 = (f32[9,80,128]{2,1,0:T(8,128)}, f32[9,80,128]{2,1,0:T(8,128)S(1)}, u32[]{:S(2)}, u32[]{:S(2)}) collective-permute-start(f32[9,80,128]{2,1,0:T(8,128)} %get-tuple-element.26), channel_id=1, source_target_pairs={{0,24},{4,28},{8,16},{12,20},{16,8},{20,12},{24,0},{28,4},{1,25},{... | collective-permute-start | bytes 1105928 | tf_op jit(solution)/shard_map/ppermute | solution.py:338
  43.1 9.5 %copy-start.2 = (f32[9,80,128]{2,1,0:T(8,128)}, f32[9,80,128]{2,1,0:T(8,128)S(1)}, u32[]{:S(2)}) copy-start(f32[9,80,128]{2,1,0:T(8,128)S(1)} %collective-permute-done.4.rest_2_) | copy-start | bytes 1105924
  43.1 9.8 %collective-permute-start.6 = (f32[9,80,128]{2,1,0:T(8,128)S(1)}, f32[9,80,128]{2,1,0:T(8,128)S(1)}, u32[]{:S(2)}, u32[]{:S(2)}) collective-permute-start(f32[9,80,128]{2,1,0:T(8,128)S(1)} %copy-done), channel_id=1, source_target_pairs={{0,4},{4,0},{8,12},{12,8},{16,20},{20,16},{24,28},{28,24},{1,5},{5... | collective-permute-start | bytes 1105928 | tf_op jit(solution)/shard_map/ppermute | solution.py:341
  43.1 9.8 %copy-start.3 = (f32[9,80,128]{2,1,0:T(8,128)}, f32[9,80,128]{2,1,0:T(8,128)S(1)}, u32[]{:S(2)}) copy-start(f32[9,80,128]{2,1,0:T(8,128)S(1)} %collective-permute-done.5.rest_3_) | copy-start | bytes 1105924
  44.0 11.4 %collective-permute-start.10 = (f32[4,2,80,128]{3,2,1,0:T(8,128)}, f32[4,2,80,128]{3,2,1,0:T(8,128)S(1)}, u32[]{:S(2)}, u32[]{:S(2)}) collective-permute-start(f32[4,2,80,128]{3,2,1,0:T(8,128)} %pad_maximum_fusion), channel_id=1, source_target_pairs={{0,1},{1,2},{2,3},{4,5},{5,6},{6,7},{8,9},{9,10},{10,11},{12,13},{... | collective-permute-start | bytes 983048 | tf_op jit(solution)/shard_map/ppermute | solution.py:350
  48.3 13.6 %copy-start.10 = (f32[17,32,128]{2,1,0:T(8,128)}, f32[17,32,128]{2,1,0:T(8,128)S(1)}, u32[]{:S(2)}) copy-start(f32[17,32,128]{2,1,0:T(8,128)S(1)} %collective-permute-done.2.rest_15_) | copy-start | bytes 835588
  48.3 11.9 %collective-permute-start.12 = (f32[4,2,80,128]{3,2,1,0:T(8,128)}, f32[4,2,80,128]{3,2,1,0:T(8,128)S(1)}, u32[]{:S(2)}, u32[]{:S(2)}) collective-permute-start(f32[4,2,80,128]{3,2,1,0:T(8,128)} %pad_maximum_fusion.1), channel_id=1, source_target_pairs={{1,0},{2,1},{3,2},{5,4},{6,5},{7,6},{9,8},{10,9},{11,10},{13,12},{... | collective-permute-start | bytes 983048 | tf_op jit(solution)/shard_map/ppermute | solution.py:350
  51.0 0.7 copy-start.11
  52.4 9.2 %collective-permute-start.7 = (f32[9,80,128]{2,1,0:T(8,128)S(1)}, f32[9,80,128]{2,1,0:T(8,128)S(1)}, u32[]{:S(2)}, u32[]{:S(2)}) collective-permute-start(f32[9,80,128]{2,1,0:T(8,128)S(1)} %collective-permute-done.3.rest_1_), channel_id=1, source_target_pairs={{0,4},{4,0},{8,12},{12,8},{16,20},{20,16},{24,28},{28,24},{1,5},{5... | collective-permute-start | bytes 1105928 | tf_op jit(solution)/shard_map/ppermute | solution.py:341
  52.6 9.0 %collective-permute-start.8 = (f32[9,80,128]{2,1,0:T(8,128)S(1)}, f32[9,80,128]{2,1,0:T(8,128)S(1)}, u32[]{:S(2)}, u32[]{:S(2)}) collective-permute-start(f32[9,80,128]{2,1,0:T(8,128)S(1)} %collective-permute-done.4.rest_2_), channel_id=1, source_target_pairs={{0,4},{4,0},{8,12},{12,8},{16,20},{20,16},{24,28},{28,24},{1,5},{5... | collective-permute-start | bytes 1105928 | tf_op jit(solution)/shard_map/ppermute | solution.py:341
  52.9 9.0 %copy-start.4 = (f32[9,80,128]{2,1,0:T(8,128)}, f32[9,80,128]{2,1,0:T(8,128)S(1)}, u32[]{:S(2)}) copy-start(f32[9,80,128]{2,1,0:T(8,128)S(1)} %collective-permute-done.6.rest_4_) | copy-start | bytes 1105924
  52.9 8.7 %collective-permute-start.9 = (f32[9,80,128]{2,1,0:T(8,128)S(1)}, f32[9,80,128]{2,1,0:T(8,128)S(1)}, u32[]{:S(2)}, u32[]{:S(2)}) collective-permute-start(f32[9,80,128]{2,1,0:T(8,128)S(1)} %collective-permute-done.5.rest_3_), channel_id=1, source_target_pairs={{0,4},{4,0},{8,12},{12,8},{16,20},{20,16},{24,28},{28,24},{1,5},{5... | collective-permute-start | bytes 1105928 | tf_op jit(solution)/shard_map/ppermute | solution.py:341
  55.4 6.5 %copy-start.8 = (f32[4,2,80,128]{3,2,1,0:T(8,128)}, f32[4,2,80,128]{3,2,1,0:T(8,128)S(1)}, u32[]{:S(2)}) copy-start(f32[4,2,80,128]{3,2,1,0:T(8,128)S(1)} %collective-permute-done.10.rest_8_) | copy-start | bytes 983044
  55.4 6.2 %collective-permute-start.11 = (f32[4,2,80,128]{3,2,1,0:T(8,128)S(1)}, f32[4,2,80,128]{3,2,1,0:T(8,128)}, u32[]{:S(2)}, u32[]{:S(2)}) collective-permute-start(f32[4,2,80,128]{3,2,1,0:T(8,128)S(1)} %collective-permute-done.10.rest_8_), channel_id=1, source_target_pairs={{0,4},{4,0},{8,12},{12,8},{16,20},{20,16},{24,28},{28,24},{1,5},{5... | collective-permute-start | bytes 983048 | tf_op jit(solution)/shard_map/ppermute | solution.py:341
  60.2 1.8 %copy-start.9 = (f32[4,2,80,128]{3,2,1,0:T(8,128)}, f32[4,2,80,128]{3,2,1,0:T(8,128)S(1)}, u32[]{:S(2)}) copy-start(f32[4,2,80,128]{3,2,1,0:T(8,128)S(1)} %collective-permute-done.12.rest_10_) | copy-start | bytes 983044
  60.2 1.8 %collective-permute-start.13 = (f32[4,2,80,128]{3,2,1,0:T(8,128)S(1)}, f32[4,2,80,128]{3,2,1,0:T(8,128)}, u32[]{:S(2)}, u32[]{:S(2)}) collective-permute-start(f32[4,2,80,128]{3,2,1,0:T(8,128)S(1)} %collective-permute-done.12.rest_10_), channel_id=1, source_target_pairs={{0,4},{4,0},{8,12},{12,8},{16,20},{20,16},{24,28},{28,24},{1,5},{5... | collective-permute-start | bytes 983048 | tf_op jit(solution)/shard_map/ppermute | solution.py:341
  61.5 0.7 copy-start.5
  61.6 0.9 copy-start.6
  61.6 1.0 copy-start.7
  129.1 10.0 %collective-permute-start.16 = (f32[8,64,128]{2,1,0:T(8,128)S(1)}, f32[8,64,128]{2,1,0:T(8,128)S(1)}, u32[]{:S(2)}, u32[]{:S(2)}) collective-permute-start(f32[8,64,128]{2,1,0:T(8,128)S(1)} %get-tuple-element.29), channel_id=1, source_target_pairs={{0,24},{4,28},{8,16},{12,20},{16,8},{20,12},{24,0},{28,4},{1,25},{... | collective-permute-start | bytes 786440 | tf_op jit(solution)/shard_map/ppermute | solution.py:338
  130.5 13.8 %collective-permute-start.15 = (f32[8,64,128]{2,1,0:T(8,128)S(1)}, f32[8,64,128]{2,1,0:T(8,128)S(1)}, u32[]{:S(2)}, u32[]{:S(2)}) collective-permute-start(f32[8,64,128]{2,1,0:T(8,128)S(1)} %get-tuple-element.30), channel_id=1, source_target_pairs={{0,16},{4,20},{8,24},{12,28},{16,0},{20,4},{24,8},{28,12},{1,17},{... | collective-permute-start | bytes 786440 | tf_op jit(solution)/shard_map/ppermute | solution.py:338
  132.0 12.3 %collective-permute-start.14 = (f32[8,64,128]{2,1,0:T(8,128)S(1)}, f32[8,64,128]{2,1,0:T(8,128)S(1)}, u32[]{:S(2)}, u32[]{:S(2)}) collective-permute-start(f32[8,64,128]{2,1,0:T(8,128)S(1)} %get-tuple-element.31), channel_id=1, source_target_pairs={{0,8},{4,12},{8,0},{12,4},{16,24},{20,28},{24,16},{28,20},{1,9},{5... | collective-permute-start | bytes 786440 | tf_op jit(solution)/shard_map/ppermute | solution.py:338
  139.1 5.2 %copy-start.12 = (f32[8,64,128]{2,1,0:T(8,128)}, f32[8,64,128]{2,1,0:T(8,128)S(1)}, u32[]{:S(2)}) copy-start(f32[8,64,128]{2,1,0:T(8,128)S(1)} %collective-permute-done.16.rest_3_) | copy-start | bytes 786436
  144.3 0.7 copy-start.13
  144.3 0.8 copy-start.14
  (2 other events, 1.4 us)

commit v2 on v1

v2 whole, which is shorter than its diff:
```python
import functools

import jax
import jax.numpy as jnp
from jax import lax
from jax.experimental import pallas as pl
from jax.experimental.pallas import tpu as pltpu
from jax.sharding import PartitionSpec as P

PACK_LIMIT = 16
PREPARE_LIMIT = 24
APPLY_LIMIT = 24
CHUNK = 4


def lane_index(rows):
    return lax.broadcasted_iota(jnp.int32, (rows, 128), 1)


def swap_lanes(tiles, depth, lanes):
    tiles = list(tiles)
    size = len(tiles)
    step = 1
    while step < size:
        width = step * depth
        upper = (lanes & width) != 0
        for low in range(size):
            if low & step:
                continue
            high = low | step
            first, second = tiles[low], tiles[high]
            tiles[low] = jnp.where(upper, pltpu.roll(second, width, 1), first)
            tiles[high] = jnp.where(upper, second, pltpu.roll(first, 128 - width, 1))
        step *= 2
    return tiles


def turn(value, shift):
    shift = shift % 128
    return value if shift == 0 else pltpu.roll(value, shift, 1)


def pack_fields(geometry, u_ref, a_ref, *rest):
    layers, halves, ny, depth, chips = geometry
    sends, stage = rest[:chips], rest[chips]
    me = lax.axis_index("modes") // 2
    lanes = lane_index(8)
    place = lanes % depth
    row = 0
    for ref in (u_ref, a_ref):
        modes = ref.shape[0] // (layers * ny)

        def group(g, carry, ref=ref, row=row):
            target = pl.multiple_of(row + g * 8, 8)
            by_layer = []
            for x in range(layers):
                tiles = [
                    ref[pl.ds(g * 8 * layers * ny + x * ny + y, 8, stride=layers * ny), :]
                    for y in range(ny)
                ]
                tiles = swap_lanes(tiles, depth, lanes)
                by_layer.append(tiles)
                for d in range(ny):
                    stage[d // halves, x * halves + d % halves, pl.ds(target, 8), :] = tiles[d]
            for chip in range(chips):
                rim = jnp.zeros((8, 128), jnp.float32)
                left, right = chip * halves - 1, (chip + 1) * halves
                for x in range(layers):
                    if left >= 0:
                        rim = jnp.where(place == x, turn(by_layer[x][left], x + 1 - depth), rim)
                    if right < ny:
                        at = depth // 2 + x
                        rim = jnp.where(place == at, turn(by_layer[x][right], at), rim)
                stage[chip, layers * halves, pl.ds(target, 8), :] = rim
            return carry

        lax.fori_loop(0, modes // 8, group, 0)
        row += modes
    for e in range(chips):
        sends[e][...] = stage[e ^ me]


def pack_coupling(coupling_ref, source_ref, expansion_ref, out_ref):
    blocks, slots, width, _ = coupling_ref.shape
    per = 128 // width
    groups = slots // per
    for block in range(blocks):
        for g in range(groups):
            rows = slice((block * groups + g) * width, (block * groups + g + 1) * width)
            out_ref[rows, :] = jnp.concatenate(
                [coupling_ref[block, g * per + q] for q in range(per)], axis=1
            )
    last = blocks * groups * width
    out_ref[last : last + 8, :] = jnp.zeros((8, 128), jnp.float32)
    out_ref[last : last + blocks, 0:slots] = source_ref[...].astype(jnp.float32)
    out_ref[last + blocks : last + 2 * blocks, 0:slots] = expansion_ref[...].astype(jnp.float32)


def laplacian(tile, low, high, rim, geometry, rows):
    layers, halves, ny, depth, _ = geometry
    lanes = lane_index(rows)
    place = lanes % depth
    first_row, last_row = lanes < depth, lanes >= 128 - depth
    result = []
    for x in range(layers):
        result.append([])
        for h in range(halves):
            c = tile[x][h]
            before = tile[x - 1][h] if x else low[h]
            after = tile[x + 1][h] if x + 1 < layers else high[h]
            up = jnp.where(first_row, 0.0, turn(c, depth))
            down = jnp.where(last_row, 0.0, turn(c, -depth))
            edge = turn(tile[x][h - 1], 1 - depth) if h else turn(rim, -x)
            left = jnp.where(place == 0, edge, turn(c, 1))
            if h + 1 < halves:
                edge = turn(tile[x][h + 1], depth - 1)
            else:
                edge = turn(rim, depth - 1 - depth // 2 - x)
            right = jnp.where(place == depth - 1, edge, turn(c, -1))
            result[-1].append(((before + after) + (up + down)) + ((left + right) - 6.0 * c))
    return result


def halves_of(value):
    upper = value.astype(jnp.bfloat16)
    lower = (value - upper.astype(jnp.float32)).astype(jnp.bfloat16)
    return upper, lower


def columns(tile, tiles):
    base = (tile // CHUNK) * 2 * CHUNK * 128 + (tile % CHUNK) * 128
    return base, base + CHUNK * 128


def prepare_kernel(geometry, width, local_u, local_a, e, *rest):
    layers, halves, ny, depth, chips = geometry
    body_refs, low_refs, high_refs = rest[0:2], rest[2:4], rest[4:6]
    sources, fields = rest[-2:]
    tiles = layers * halves
    rim_at = 2 * tiles * 128
    me = lax.axis_index("modes")

    for side in range(2):
        body, low, high = body_refs[side], low_refs[side], high_refs[side]
        device = me ^ (2 * e) ^ side

        def load(start, rows, body=body, low=low, high=high):
            part = pl.ds(start, rows)
            tile = [[body[x * halves + h, part, :] for h in range(halves)] for x in range(layers)]
            below = [low[h, part, :] for h in range(halves)]
            above = [high[h, part, :] for h in range(halves)]
            return tile, below, above, body[tiles, part, :]

        def prepare_u(g, carry, load=load, device=device):
            start = pl.multiple_of(g * 16, 16)
            tile, below, above, rim = load(start, 16)
            lap = laplacian(tile, below, above, rim, geometry, 16)
            block = device * (local_u // width) + (g * 16) // width
            row = pl.multiple_of((g * 16) % width, 16)

            def put(value, at):
                upper, lower = halves_of(value)
                where = pl.ds(at, 128)
                sources[block, pl.ds(row, 16), where] = upper
                sources[block, pl.ds(width + row, 16), where] = lower
                sources[block, pl.ds(2 * width + row, 16), where] = upper

            for t in range(tiles):
                x, h = t // halves, t % halves
                put(tile[x][h], columns(t, tiles)[0])
                put(lap[x][h], columns(t, tiles)[1])
            for h in range(halves):
                put(below[h], rim_at + h * 128)
                put(above[h], rim_at + (halves + h) * 128)
            put(rim, rim_at + 2 * halves * 128)
            return carry

        lax.fori_loop(0, local_u // 16, prepare_u, 0)
        tile, below, above, rim = load(local_u, local_a)
        lap = laplacian(tile, below, above, rim, geometry, local_a)
        rows = pl.ds(pl.multiple_of(device * local_a, local_a), local_a)
        for t in range(tiles):
            x, h = t // halves, t % halves
            fields[rows, pl.ds(columns(t, tiles)[0], 128)] = tile[x][h]
            fields[rows, pl.ds(columns(t, tiles)[1], 128)] = lap[x][h]
        for h in range(halves):
            fields[rows, pl.ds(rim_at + h * 128, 128)] = below[h]
            fields[rows, pl.ds(rim_at + (halves + h) * 128, 128)] = above[h]
        fields[rows, pl.ds(rim_at + 2 * halves * 128, 128)] = rim


def apply_kernel(geometry, blocks, slots, width, pack, sources, fields, out_ref, mix, numbers, table, product, cross, sem):
    layers, halves, ny, depth, chips = geometry
    tiles = layers * halves
    chunks = tiles // CHUNK
    span = CHUNK * 128
    rim_at = 2 * tiles * 128
    rims = (2 * halves + 1) * 128
    per = 128 // width
    rows = blocks * slots // per * width

    numbers[...] = pack[rows : rows + 8, :].astype(jnp.int32)
    copy = pltpu.make_async_copy(numbers, table, sem)
    copy.start()
    value = pack[0:rows, :]
    upper, lower = halves_of(value)
    take = lax.broadcasted_iota(jnp.int32, (256, per * 128), 0)
    give = lax.broadcasted_iota(jnp.int32, (256, per * 128), 1)
    lane = give % 128
    wanted = (give // 128) * width + lane % width + jnp.where(lane >= 2 * width, 128, 0)
    chosen = jnp.where((take == wanted) & (lane < 3 * width), 1.0, 0.0).astype(jnp.bfloat16)
    mix[...] = jnp.dot(
        jnp.concatenate([upper, lower], axis=1), chosen, preferred_element_type=jnp.float32
    ).astype(jnp.bfloat16)
    copy.wait()

    def one_block(n, carry):
        def operands(s, first, count):
            j, k = table[n, s], table[blocks + n, s]
            group = pl.multiple_of((n * (slots // per) + s // per) * width, width)
            lanes = (s % per) * 128
            mixed = jnp.dot(
                mix[pl.ds(group, width), lanes : lanes + 3 * width],
                sources[j, :, first : first + count],
                preferred_element_type=jnp.float32,
            )
            return mixed, k

        for chunk in range(chunks):
            base = chunk * 2 * span
            total = jnp.zeros((width, span), jnp.float32)
            rest_total = jnp.zeros((width, span), jnp.float32)
            for s in range(slots):
                mixed, k = operands(s, base, 2 * span)
                field = fields[pl.ds(k, 1), base : base + span]
                bent = fields[pl.ds(k, 1), base + span : base + 2 * span]
                value, curve = mixed[:, :span], mixed[:, span:]
                total = total + field * value
                rest_total = rest_total + (bent * value - field * curve)
            for i in range(CHUNK):
                product[chunk * CHUNK + i] = total[:, i * 128 : (i + 1) * 128]
                cross[chunk * CHUNK + i] = rest_total[:, i * 128 : (i + 1) * 128]

        total = jnp.zeros((width, rims), jnp.float32)
        for s in range(slots):
            mixed, k = operands(s, rim_at, rims)
            total = total + fields[pl.ds(k, 1), rim_at : rim_at + rims] * mixed
        for i in range(2 * halves + 1):
            product[tiles + i] = total[:, i * 128 : (i + 1) * 128]

        for r in range(0, width, 8):
            part = slice(r, r + 8)
            tile = [[product[x * halves + h, part, :] for h in range(halves)] for x in range(layers)]
            low = [product[tiles + h, part, :] for h in range(halves)]
            high = [product[tiles + halves + h, part, :] for h in range(halves)]
            rim = product[tiles + 2 * halves, part, :]
            lap = laplacian(tile, low, high, rim, geometry, 8)
            for t in range(tiles):
                row = pl.multiple_of(n * width + r, 8)
                out_ref[t, pl.ds(row, 8), :] = 0.5 * (
                    cross[t, part, :] - lap[t // halves][t % halves]
                )
        return carry

    lax.fori_loop(0, blocks, one_block, 0)


def unpack_kernel(geometry, *rest):
    layers, halves, ny, depth, chips = geometry
    parts, out_ref, stage = rest[:chips], rest[chips], rest[chips + 1]
    me = lax.axis_index("modes") // 2
    for e in range(chips):
        stage[e ^ me] = parts[e][...]
    lanes = lane_index(8)
    modes = out_ref.shape[0] // (layers * ny)

    def group(g, carry):
        source = pl.multiple_of(g * 8, 8)
        for x in range(layers):
            tiles = [
                stage[d // halves, x * halves + d % halves, pl.ds(source, 8), :] for d in range(ny)
            ]
            tiles = swap_lanes(tiles, depth, lanes)
            for y in range(ny):
                out_ref[pl.ds(g * 8 * layers * ny + x * ny + y, 8, stride=layers * ny), :] = tiles[y]
        return carry

    lax.fori_loop(0, modes // 8, group, 0)


def vmem(count):
    return [pl.BlockSpec(memory_space=pltpu.VMEM)] * count


def on_device(solution_modes, coefficient_modes, coupling, source_block, expansion_index):
    local_u, layers, ny, nz = solution_modes.shape
    local_a = coefficient_modes.shape[0]
    blocks, slots, width = coupling.shape[:3]
    count = lax.axis_size("modes")
    chips = count // 2
    depth = 128 // ny
    halves = (nz // depth) // chips
    geometry = (layers, halves, ny, depth, chips)
    tiles = layers * halves
    modes = local_u + local_a
    f32 = jnp.float32

    def call(kernel, shapes, inputs, scratch, limit, name, **more):
        return pl.pallas_call(
            kernel,
            out_shape=shapes,
            in_specs=vmem(inputs),
            out_specs=jax.tree.map(lambda _: pl.BlockSpec(memory_space=pltpu.VMEM), shapes),
            scratch_shapes=scratch,
            compiler_params=pltpu.CompilerParams(vmem_limit_bytes=limit * 1024 * 1024),
            name=name,
            **more,
        )

    sends = call(
        functools.partial(pack_fields, geometry),
        [jax.ShapeDtypeStruct((tiles + 1, modes, 128), f32)] * chips,
        2,
        [pltpu.VMEM((chips, tiles + 1, modes, 128), f32)],
        PACK_LIMIT,
        "pack_fields",
    )(solution_modes.reshape(-1, nz), coefficient_modes.reshape(-1, nz))
    rows = blocks * slots * width // (128 // width)
    pack = call(
        pack_coupling, jax.ShapeDtypeStruct((rows + 8, 128), f32), 3, [], PACK_LIMIT, "pack_coupling"
    )(coupling, source_block, expansion_index)

    def trade(value, e):
        return lax.ppermute(value, "modes", [(i, i ^ (2 * e)) for i in range(count)])

    def sibling(value):
        return lax.ppermute(value, "modes", [(i, i ^ 1) for i in range(count)])

    bodies = [sends[0]] + [trade(sends[e], e) for e in range(1, chips)]
    pack_later = lax.optimization_barrier((pack, bodies[1]))[0] if chips > 1 else pack
    packs = [pack] + [trade(pack_later, e) for e in range(1, chips)]
    n_tiles = lax.axis_size("tiles")
    up = [(i, i + 1) for i in range(n_tiles - 1)]
    down = [(i + 1, i) for i in range(n_tiles - 1)]
    low, high, other_low, other_high = [], [], [], []
    for group in (range(0, chips - 1), range(chips - 1, chips)):
        if not len(group):
            continue
        top = jnp.concatenate([bodies[e][tiles - halves : tiles] for e in group])
        bottom = jnp.concatenate([bodies[e][:halves] for e in group])
        part = jnp.concatenate([lax.ppermute(top, "tiles", up), lax.ppermute(bottom, "tiles", down)])
        other = sibling(part)
        size = len(group) * halves
        for i in range(len(group)):
            here = slice(i * halves, (i + 1) * halves)
            there = slice(size + i * halves, size + (i + 1) * halves)
            low.append(part[here])
            high.append(part[there])
            other_low.append(other[here])
            other_high.append(other[there])
    others = [sibling(body) for body in bodies]

    ncol = 2 * tiles * 128 + (2 * halves + 1) * 128
    n_blocks = count * (local_u // width)
    prepared = ()
    for e in range(chips):
        prepared = call(
            functools.partial(prepare_kernel, geometry, width, local_u, local_a, e),
            (
                jax.ShapeDtypeStruct((n_blocks, 3 * width, ncol), jnp.bfloat16),
                jax.ShapeDtypeStruct((count * local_a, ncol), f32),
            ),
            6 + len(prepared),
            [],
            PREPARE_LIMIT,
            "prepare",
            input_output_aliases={6: 0, 7: 1} if prepared else {},
        )(bodies[e], others[e], low[e], other_low[e], high[e], other_high[e], *prepared)
    sources, fields = prepared

    parts = [None] * chips
    for e in list(range(chips - 1, -1, -1)):
        result = call(
            functools.partial(apply_kernel, geometry, blocks, slots, width),
            jax.ShapeDtypeStruct((tiles, local_u, 128), f32),
            3,
            [
                pltpu.VMEM((rows, 128 // width * 128), jnp.bfloat16),
                pltpu.VMEM((8, 128), jnp.int32),
                pltpu.SMEM((8, 128), jnp.int32),
                pltpu.VMEM((tiles + 2 * halves + 1, width, 128), f32),
                pltpu.VMEM((tiles, width, 128), f32),
                pltpu.SemaphoreType.DMA,
            ],
            APPLY_LIMIT,
            "apply",
        )(packs[e], sources, fields)
        parts[e] = trade(result, e) if e else result
    out = call(
        functools.partial(unpack_kernel, geometry),
        jax.ShapeDtypeStruct((local_u * layers * ny, nz), f32),
        chips,
        [pltpu.VMEM((chips, tiles, local_u, 128), f32)],
        PACK_LIMIT,
        "unpack",
    )(*parts)
    return out.reshape(solution_modes.shape)


def solution(mesh):
    placed = (
        P("modes", "tiles", None, None),
        P("modes", "tiles", None, None),
        P("modes", None, None, None),
        P("modes", None),
        P("modes", None),
    )
    return jax.shard_map(
        on_device,
        mesh=mesh,
        in_specs=placed,
        out_specs=P("modes", "tiles", None, None),
        check_vma=False,
    )
```

time: 150 us -> 90.2 us (0.60)
  Pallas kernels: 76.4 us -> 38.4 us
  waiting for transfers between devices: 41.4 us -> 22.5 us
  local copies, waits for them, and re-layouts: 9.33 us -> 4.88 us
  starting transfers between devices: 20 us -> 23.7 us
  other arithmetic: 2.29 us -> 0.09 us
    pallas_call x3 -> x11, Pallas kernels: 76.4 us -> 38.4 us  [the longest x4 24.4 us: on_device(): call(functools.partial(apply_kernel, geometry, blocks, slots, width), jax...]
    ppermute x9, waiting for transfers between devices: 34.1 us -> 17.5 us  [trade(): return lax.ppermute(value, 'modes', [(i, i ^ 2 * e) for i in range(count)])]
    ppermute x1 -> x2, starting transfers between devices: 3.49 us -> 8.04 us  [on_device(): lax.ppermute(top, 'tiles', up)]
    ppermute x9, starting transfers between devices: 14.5 us -> 11.7 us  [trade(): return lax.ppermute(value, 'modes', [(i, i ^ 2 * e) for i in range(count)])]
    another operation x3 -> x0, other arithmetic: 2.28 us -> none  [the longest x1 0.86 us: on_device(): top = jnp.stack([body[tiles - halves:tiles] for body in bodies])]
    another operation x6 -> x0, local copies, waits for them, and re-layouts: 2.25 us -> none  [the longest x4 0.98 us: on_device(): bottom = jnp.stack([body[:halves] for body in bodies])]
    squeeze x1 -> x0, local copies, waits for them, and re-layouts: 1.99 us -> none  [on_device(): parts = [result[0]] + [trade(result[e], e) for e in range(1, chips)]]
    unnamed x35 -> x10, local copies, waits for them, and re-layouts: 2.85 us -> 4.75 us
  transfers between devices with their start and end apart: 17 -> 19, of which waited for: 7 -> 5; matrix products, arithmetic and copies ran while one was open for 4% -> 0% of each run, Pallas kernels for 0% -> 35%
where the time goes in v2:
time: 90.2 us; the launch traced here: 89.9 us
  Pallas kernels  38.4 us (43%)
  starting transfers between devices  23.7 us (26%)
  waiting for transfers between devices  22.5 us (25%)
  local copies, waits for them, and re-layouts  4.88 us (5%)
    pallas_call x4, Pallas kernels, on_device(): call(functools.partial(apply_kernel, geometry, blocks, slots, width), jax...  24.4 us
    ppermute x9, waiting for transfers between devices, trade(): return lax.ppermute(value, 'modes', [(i, i ^ 2 * e) for i in range(count)])  17.5 us
    ppermute x9, starting transfers between devices, trade(): return lax.ppermute(value, 'modes', [(i, i ^ 2 * e) for i in range(count)])  11.7 us
    ppermute x2, starting transfers between devices, on_device(): lax.ppermute(top, 'tiles', up)  8.04 us
    pallas_call x4, Pallas kernels, on_device(): call(functools.partial(prepare_kernel, geometry, width, local_u, local_a,...  7.14 us
    unnamed x10, local copies, waits for them, and re-layouts  4.75 us
    ppermute x2, waiting for transfers between devices, on_device(): lax.ppermute(bottom, 'tiles', down)  4.3 us
    pallas_call x1, Pallas kernels, on_device(): call(functools.partial(pack_fields, geometry), [jax.ShapeDtypeStruct((til...  3.4 us
  transfers between devices with their start and end apart: 19, of which 5 were waited for; matrix products, arithmetic and copies ran while one was open for 0% of the time, Pallas kernels for 35%

profile of v2, /device:TPU:0, one launch (start us, length us, event | category | flops | bytes accessed | tf_op | source)
XLA Modules:
  0.0 89.9 jit_solution(6677931779242899543)
XLA Ops:
  0.0 1.2 %copy-done = f32[64,4,8,128]{3,2,1,0:T(8,128)S(1)} copy-done((f32[64,4,8,128]{3,2,1,0:T(8,128)S(1)}, f32[64,4,8,128]{3,2,1,0:T(8,128)}, u32[]{:S(2)}) %copy-start) | copy-done | bytes 1048600
  1.2 0.9 %copy-done.2 = f32[16,4,8,128]{3,2,1,0:T(8,128)S(1)} copy-done((f32[16,4,8,128]{3,2,1,0:T(8,128)S(1)}, f32[16,4,8,128]{3,2,1,0:T(8,128)}, u32[]{:S(2)}) %copy-start.2) | copy-done | bytes 262168
  2.2 3.4 %pack_fields.1 = (f32[9,80,128]{2,1,0:T(8,128)S(1)}, f32[9,80,128]{2,1,0:T(8,128)S(1)}, f32[9,80,128]{2,1,0:T(8,128)S(1)}, f32[9,80,128]{2,1,0:T(8,128)S(1)}) custom-call(f32[2048,128]{1,0:T(8,128)S(1)} %bitcast.3, f32[512,128]{1,0:T(8,128)S(1)} %bitcast.4), custom_call_target="tpu_custom_call" | custom-call | tf_op jit(solution)/shard_map/pack_fields/pallas_call | solution.py:320
  5.6 3.0 %collective-permute-start.7 = (f32[9,80,128]{2,1,0:T(8,128)S(1)}, f32[9,80,128]{2,1,0:T(8,128)S(1)}, u32[]{:S(2)}, u32[]{:S(2)}) collective-permute-start(f32[9,80,128]{2,1,0:T(8,128)S(1)} %get-tuple-element.21), channel_id=1, source_target_pairs={{0,8},{4,12},{8,0},{12,4},{16,24},{20,28},{24,16},{28,20},{1,9},{5... | collective-permute-start | bytes 1105928 | tf_op jit(solution)/shard_map/ppermute | solution.py:334
  8.6 1.5 %collective-permute-start.5 = (f32[9,80,128]{2,1,0:T(8,128)S(1)}, f32[9,80,128]{2,1,0:T(8,128)S(1)}, u32[]{:S(2)}, u32[]{:S(2)}) collective-permute-start(f32[9,80,128]{2,1,0:T(8,128)S(1)} %get-tuple-element.19), channel_id=1, source_target_pairs={{0,16},{4,20},{8,24},{12,28},{16,0},{20,4},{24,8},{28,12},{1,17},{... | collective-permute-start | bytes 1105928 | tf_op jit(solution)/shard_map/ppermute | solution.py:334
  10.1 7.9 %collective-permute-done.7.rest_0_ = f32[9,80,128]{2,1,0:T(8,128)S(1)} collective-permute-done((f32[9,80,128]{2,1,0:T(8,128)S(1)}, f32[9,80,128]{2,1,0:T(8,128)S(1)}, u32[]{:S(2)}, u32[]{:S(2)}) %collective-permute-start.7) | collective-permute-done | bytes 368672 | tf_op jit(solution)/shard_map/ppermute | solution.py:334
  18.0 8.5 %collective-permute-done.5.rest_0_ = f32[9,80,128]{2,1,0:T(8,128)S(1)} collective-permute-done((f32[9,80,128]{2,1,0:T(8,128)S(1)}, f32[9,80,128]{2,1,0:T(8,128)S(1)}, u32[]{:S(2)}, u32[]{:S(2)}) %collective-permute-start.5) | collective-permute-done | bytes 368672 | tf_op jit(solution)/shard_map/ppermute | solution.py:334
  26.6 1.3 %collective-permute-start.9 = (f32[6,80,128]{2,1,0:T(8,128)S(1)}, f32[6,80,128]{2,1,0:T(8,128)S(1)}, u32[]{:S(2)}, u32[]{:S(2)}) collective-permute-start(f32[6,80,128]{2,1,0:T(8,128)S(1)} %pad_maximum_fusion.2), channel_id=1, source_target_pairs={{1,0},{2,1},{3,2},{5,4},{6,5},{7,6},{9,8},{10,9},{11,10},{13,12},{... | collective-permute-start | bytes 737288 | tf_op jit(solution)/shard_map/ppermute | solution.py:351
  27.9 4.6 %collective-permute-start.8 = (f32[6,80,128]{2,1,0:T(8,128)S(1)}, f32[6,80,128]{2,1,0:T(8,128)S(1)}, u32[]{:S(2)}, u32[]{:S(2)}) collective-permute-start(f32[6,80,128]{2,1,0:T(8,128)S(1)} %pad_maximum_fusion.1), channel_id=1, source_target_pairs={{0,1},{1,2},{2,3},{4,5},{5,6},{6,7},{8,9},{9,10},{10,11},{12,13},{... | collective-permute-start | bytes 737288 | tf_op jit(solution)/shard_map/ppermute | solution.py:351
  32.5 3.5 %collective-permute-start.2 = (f32[2,80,128]{2,1,0:T(8,128)S(1)}, f32[2,80,128]{2,1,0:T(8,128)S(1)}, u32[]{:S(2)}, u32[]{:S(2)}) collective-permute-start(f32[2,80,128]{2,1,0:T(8,128)S(1)} %get-tuple-element.44), channel_id=1, source_target_pairs={{0,1},{1,2},{2,3},{4,5},{5,6},{6,7},{8,9},{9,10},{10,11},{12,13},{... | collective-permute-start | bytes 245768 | tf_op jit(solution)/shard_map/ppermute | solution.py:351
  36.0 1.3 %collective-permute-start.3 = (f32[2,80,128]{2,1,0:T(8,128)S(1)}, f32[2,80,128]{2,1,0:T(8,128)S(1)}, u32[]{:S(2)}, u32[]{:S(2)}) collective-permute-start(f32[2,80,128]{2,1,0:T(8,128)S(1)} %get-tuple-element.43), channel_id=1, source_target_pairs={{1,0},{2,1},{3,2},{5,4},{6,5},{7,6},{9,8},{10,9},{11,10},{13,12},{... | collective-permute-start | bytes 245768 | tf_op jit(solution)/shard_map/ppermute | solution.py:351
  37.3 0.7 collective-permute-done.2.rest_2_
  38.0 4.3 %collective-permute-done.3.rest_4_ = f32[2,80,128]{2,1,0:T(8,128)S(1)} collective-permute-done((f32[2,80,128]{2,1,0:T(8,128)S(1)}, f32[2,80,128]{2,1,0:T(8,128)S(1)}, u32[]{:S(2)}, u32[]{:S(2)}) %collective-permute-start.3) | collective-permute-done | bytes 81952 | tf_op jit(solution)/shard_map/ppermute | solution.py:351
  42.5 0.5 collective-permute-start.10
  43.1 1.2 %copy-done.1 = f32[2,32,32,32]{3,2,1,0:T(8,128)S(1)} copy-done((f32[2,32,32,32]{3,2,1,0:T(8,128)S(1)}, f32[2,32,32,32]{3,2,1,0:T(8,128)}, u32[]{:S(2)}) %copy-start.1) | copy-done | bytes 262168
  44.3 0.7 copy-done.3
  45.0 0.7 copy-done.4
  46.0 1.6 %collective-permute-start.17 = (f32[520,128]{1,0:T(8,128)S(1)}, f32[520,128]{1,0:T(8,128)S(1)}, u32[]{:S(2)}, u32[]{:S(2)}) collective-permute-start(f32[520,128]{1,0:T(8,128)S(1)} %pack_coupling.1.pack), channel_id=1, source_target_pairs={{0,24},{4,28},{8,16},{12,20},{16,8},{20,12},{24,0},{28,4},{1,25},{... | collective-permute-start | bytes 798728 | tf_op jit(solution)/shard_map/ppermute | solution.py:334
  47.8 1.8 %collective-permute-start.13 = (f32[520,128]{1,0:T(8,128)S(1)}, f32[520,128]{1,0:T(8,128)S(1)}, u32[]{:S(2)}, u32[]{:S(2)}) collective-permute-start(f32[520,128]{1,0:T(8,128)S(1)} %pack_coupling.1.pack), channel_id=1, source_target_pairs={{0,8},{4,12},{8,0},{12,4},{16,24},{20,28},{24,16},{28,20},{1,9},{5... | collective-permute-start | bytes 798728 | tf_op jit(solution)/shard_map/ppermute | solution.py:334
  50.2 1.8 %prepare.4 = (bf16[16,96,2688]{2,1,0:T(8,128)(2,1)S(1)}, f32[128,2688]{1,0:T(8,128)S(1)}) custom-call(f32[9,80,128]{2,1,0:T(8,128)S(1)} %get-tuple-element.20.rest_0_, f32[9,80,128]{2,1,0:T(8,128)S(1)} %collective-permute-done.12.rest_1_, f32[2,80,128]{2,1,0:T(8,128)S(1)} %get-tuple-element.48.rest_2_, f32[2,80,128]{2,1,0:T(8,128)S(1)} %get-tuple-element.32.rest_3_, ...), custom_call_target="tpu_custom_call" | custom-call | tf_op jit(solution)/shard_map/prepare/pallas_call | solution.py:367
  52.0 1.8 %prepare.5 = (bf16[16,96,2688]{2,1,0:T(8,128)(2,1)S(1)}, f32[128,2688]{1,0:T(8,128)S(1)}) custom-call(f32[9,80,128]{2,1,0:T(8,128)S(1)} %collective-permute-done.7.rest_0_, f32[9,80,128]{2,1,0:T(8,128)S(1)} %collective-permute-done.11.rest_1_, f32[2,80,128]{2,1,0:T(8,128)S(1)} %get-tuple-element.49.rest_2_, ...), custom_call_target="tpu_custom_call", output_to_operand_aliasing={{0}: (6, {}), {1}: (7, {})} | custom-call | tf_op jit(solution)/shard_map/prepare/pallas_call | solution.py:367
  53.8 1.8 %prepare.6 = (bf16[16,96,2688]{2,1,0:T(8,128)(2,1)S(1)}, f32[128,2688]{1,0:T(8,128)S(1)}) custom-call(f32[9,80,128]{2,1,0:T(8,128)S(1)} %collective-permute-done.5.rest_0_, f32[9,80,128]{2,1,0:T(8,128)S(1)} %collective-permute-done.6.rest_1_, f32[2,80,128]{2,1,0:T(8,128)S(1)} %get-tuple-element.50.rest_2_, ...), custom_call_target="tpu_custom_call", output_to_operand_aliasing={{0}: (6, {}), {1}: (7, {})} | custom-call | tf_op jit(solution)/shard_map/prepare/pallas_call | solution.py:367
  55.6 1.8 %prepare.7 = (bf16[16,96,2688]{2,1,0:T(8,128)(2,1)S(1)}, f32[128,2688]{1,0:T(8,128)S(1)}) custom-call(f32[9,80,128]{2,1,0:T(8,128)S(1)} %collective-permute-done.rest_0_, f32[9,80,128]{2,1,0:T(8,128)S(1)} %collective-permute-done.1.rest_1_, f32[2,80,128]{2,1,0:T(8,128)S(1)} %collective-permute-done.2.rest_2_, ...), custom_call_target="tpu_custom_call", output_to_operand_aliasing={{0}: (6, {}), {1}: (7, {})} | custom-call | tf_op jit(solution)/shard_map/prepare/pallas_call | solution.py:367
  57.4 6.1 %apply.7 = f32[8,64,128]{2,1,0:T(8,128)S(1)} custom-call(f32[520,128]{1,0:T(8,128)S(1)} %collective-permute-done.17.pack, bf16[16,96,2688]{2,1,0:T(8,128)(2,1)S(1)} %get-tuple-element.28.sources, f32[128,2688]{1,0:T(8,128)S(1)} %get-tuple-element.29.fields), custom_call_target="tpu_custom_call" | custom-call | tf_op jit(solution)/shard_map/apply/pallas_call | solution.py:383
  63.5 2.6 %collective-permute-start.18 = (f32[8,64,128]{2,1,0:T(8,128)S(1)}, f32[8,64,128]{2,1,0:T(8,128)S(1)}, u32[]{:S(2)}, u32[]{:S(2)}) collective-permute-start(f32[8,64,128]{2,1,0:T(8,128)S(1)} %apply.7), channel_id=1, source_target_pairs={{0,24},{4,28},{8,16},{12,20},{16,8},{20,12},{24,0},{28,4},{1,25},{... | collective-permute-start | bytes 786440 | tf_op jit(solution)/shard_map/ppermute | solution.py:334
  66.1 6.0 %apply.6 = f32[8,64,128]{2,1,0:T(8,128)S(1)} custom-call(f32[520,128]{1,0:T(8,128)S(1)} %collective-permute-done.15.pack, bf16[16,96,2688]{2,1,0:T(8,128)(2,1)S(1)} %get-tuple-element.28.sources, f32[128,2688]{1,0:T(8,128)S(1)} %get-tuple-element.29.fields), custom_call_target="tpu_custom_call" | custom-call | tf_op jit(solution)/shard_map/apply/pallas_call | solution.py:383
  72.1 0.6 collective-permute-start.16
  72.7 6.1 %apply.5 = f32[8,64,128]{2,1,0:T(8,128)S(1)} custom-call(f32[520,128]{1,0:T(8,128)S(1)} %collective-permute-done.13.pack, bf16[16,96,2688]{2,1,0:T(8,128)(2,1)S(1)} %get-tuple-element.28.sources, f32[128,2688]{1,0:T(8,128)S(1)} %get-tuple-element.29.fields), custom_call_target="tpu_custom_call" | custom-call | tf_op jit(solution)/shard_map/apply/pallas_call | solution.py:383
  78.8 0.5 collective-permute-start.14
  79.3 6.2 %apply.4.rest_0_ = f32[8,64,128]{2,1,0:T(8,128)S(1)} custom-call(f32[520,128]{1,0:T(8,128)S(1)} %pack_coupling.1.pack, bf16[16,96,2688]{2,1,0:T(8,128)(2,1)S(1)} %get-tuple-element.28.sources, f32[128,2688]{1,0:T(8,128)S(1)} %get-tuple-element.29.fields), custom_call_target="tpu_custom_call" | custom-call | tf_op jit(solution)/shard_map/apply/pallas_call | solution.py:383
  85.6 1.1 %collective-permute-done.14.rest_1_ = f32[8,64,128]{2,1,0:T(8,128)S(1)} collective-permute-done((f32[8,64,128]{2,1,0:T(8,128)S(1)}, f32[8,64,128]{2,1,0:T(8,128)S(1)}, u32[]{:S(2)}, u32[]{:S(2)}) %collective-permute-start.14) | collective-permute-done | bytes 262176 | tf_op jit(solution)/shard_map/ppermute | solution.py:334
  86.6 3.3 %unpack.1 = f32[2048,128]{1,0:T(8,128)} custom-call(f32[8,64,128]{2,1,0:T(8,128)S(1)} %apply.4.rest_0_, f32[8,64,128]{2,1,0:T(8,128)S(1)} %collective-permute-done.14.rest_1_, f32[8,64,128]{2,1,0:T(8,128)S(1)} %collective-permute-done.16.rest_2_, f32[8,64,128]{2,1,0:T(8,128)S(1)} %collective-permute-done.18.rest_3_), custom_call_target="tpu_custom_call" | custom-call | tf_op jit(solution)/shard_map/unpack/pallas_call | solution.py:399
  (39 shorter events, 1.5 us)
Async XLA Ops:
  0.0 1.2 %copy-start = (f32[64,4,8,128]{3,2,1,0:T(8,128)S(1)}, f32[64,4,8,128]{3,2,1,0:T(8,128)}, u32[]{:S(2)}) copy-start(f32[64,4,8,128]{3,2,1,0:T(8,128)} %param.5) | copy-start | bytes 3145732
  1.2 0.9 %copy-start.2 = (f32[16,4,8,128]{3,2,1,0:T(8,128)S(1)}, f32[16,4,8,128]{3,2,1,0:T(8,128)}, u32[]{:S(2)}) copy-start(f32[16,4,8,128]{3,2,1,0:T(8,128)} %param.6) | copy-start | bytes 786436
  5.6 12.4 %collective-permute-start.7 = (f32[9,80,128]{2,1,0:T(8,128)S(1)}, f32[9,80,128]{2,1,0:T(8,128)S(1)}, u32[]{:S(2)}, u32[]{:S(2)}) collective-permute-start(f32[9,80,128]{2,1,0:T(8,128)S(1)} %get-tuple-element.21), channel_id=1, source_target_pairs={{0,8},{4,12},{8,0},{12,4},{16,24},{20,28},{24,16},{28,20},{1,9},{5... | collective-permute-start | bytes 1105928 | tf_op jit(solution)/shard_map/ppermute | solution.py:334
  8.6 17.9 %collective-permute-start.5 = (f32[9,80,128]{2,1,0:T(8,128)S(1)}, f32[9,80,128]{2,1,0:T(8,128)S(1)}, u32[]{:S(2)}, u32[]{:S(2)}) collective-permute-start(f32[9,80,128]{2,1,0:T(8,128)S(1)} %get-tuple-element.19), channel_id=1, source_target_pairs={{0,16},{4,20},{8,24},{12,28},{16,0},{20,4},{24,8},{28,12},{1,17},{... | collective-permute-start | bytes 1105928 | tf_op jit(solution)/shard_map/ppermute | solution.py:334
  10.1 22.4 %collective-permute-start = (f32[9,80,128]{2,1,0:T(8,128)S(1)}, f32[9,80,128]{2,1,0:T(8,128)S(1)}, u32[]{:S(2)}, u32[]{:S(2)}) collective-permute-start(f32[9,80,128]{2,1,0:T(8,128)S(1)} %get-tuple-element.18), channel_id=1, source_target_pairs={{0,24},{4,28},{8,16},{12,20},{16,8},{20,12},{24,0},{28,4},{1,25},{... | collective-permute-start | bytes 1105928 | tf_op jit(solution)/shard_map/ppermute | solution.py:334
  26.6 15.8 %collective-permute-start.9 = (f32[6,80,128]{2,1,0:T(8,128)S(1)}, f32[6,80,128]{2,1,0:T(8,128)S(1)}, u32[]{:S(2)}, u32[]{:S(2)}) collective-permute-start(f32[6,80,128]{2,1,0:T(8,128)S(1)} %pad_maximum_fusion.2), channel_id=1, source_target_pairs={{1,0},{2,1},{3,2},{5,4},{6,5},{7,6},{9,8},{10,9},{11,10},{13,12},{... | collective-permute-start | bytes 737288 | tf_op jit(solution)/shard_map/ppermute | solution.py:351
  27.9 14.5 %collective-permute-start.8 = (f32[6,80,128]{2,1,0:T(8,128)S(1)}, f32[6,80,128]{2,1,0:T(8,128)S(1)}, u32[]{:S(2)}, u32[]{:S(2)}) collective-permute-start(f32[6,80,128]{2,1,0:T(8,128)S(1)} %pad_maximum_fusion.1), channel_id=1, source_target_pairs={{0,1},{1,2},{2,3},{4,5},{5,6},{6,7},{8,9},{9,10},{10,11},{12,13},{... | collective-permute-start | bytes 737288 | tf_op jit(solution)/shard_map/ppermute | solution.py:351
  32.5 5.5 %collective-permute-start.2 = (f32[2,80,128]{2,1,0:T(8,128)S(1)}, f32[2,80,128]{2,1,0:T(8,128)S(1)}, u32[]{:S(2)}, u32[]{:S(2)}) collective-permute-start(f32[2,80,128]{2,1,0:T(8,128)S(1)} %get-tuple-element.44), channel_id=1, source_target_pairs={{0,1},{1,2},{2,3},{4,5},{5,6},{6,7},{8,9},{9,10},{10,11},{12,13},{... | collective-permute-start | bytes 245768 | tf_op jit(solution)/shard_map/ppermute | solution.py:351
  36.0 6.3 %collective-permute-start.3 = (f32[2,80,128]{2,1,0:T(8,128)S(1)}, f32[2,80,128]{2,1,0:T(8,128)S(1)}, u32[]{:S(2)}, u32[]{:S(2)}) collective-permute-start(f32[2,80,128]{2,1,0:T(8,128)S(1)} %get-tuple-element.43), channel_id=1, source_target_pairs={{1,0},{2,1},{3,2},{5,4},{6,5},{7,6},{9,8},{10,9},{11,10},{13,12},{... | collective-permute-start | bytes 245768 | tf_op jit(solution)/shard_map/ppermute | solution.py:351
  42.3 5.3 %collective-permute-start.4 = (f32[4,80,128]{2,1,0:T(8,128)S(1)}, f32[4,80,128]{2,1,0:T(8,128)S(1)}, u32[]{:S(2)}, u32[]{:S(2)}) collective-permute-start(f32[4,80,128]{2,1,0:T(8,128)S(1)} %pad_maximum_fusion.3), channel_id=1, source_target_pairs={{0,4},{4,0},{8,12},{12,8},{16,20},{20,16},{24,28},{28,24},{1,5},{5... | collective-permute-start | bytes 491528 | tf_op jit(solution)/shard_map/ppermute | solution.py:337
  42.5 7.4 %collective-permute-start.10 = (f32[12,80,128]{2,1,0:T(8,128)S(1)}, f32[12,80,128]{2,1,0:T(8,128)S(1)}, u32[]{:S(2)}, u32[]{:S(2)}) collective-permute-start(f32[12,80,128]{2,1,0:T(8,128)S(1)} %pad_maximum_fusion), channel_id=1, source_target_pairs={{0,4},{4,0},{8,12},{12,8},{16,20},{20,16},{24,28},{28,24},{1,5},{5... | collective-permute-start | bytes 1474568 | tf_op jit(solution)/shard_map/ppermute | solution.py:337
  43.0 4.8 %collective-permute-start.12 = (f32[9,80,128]{2,1,0:T(8,128)S(1)}, f32[9,80,128]{2,1,0:T(8,128)S(1)}, u32[]{:S(2)}, u32[]{:S(2)}) collective-permute-start(f32[9,80,128]{2,1,0:T(8,128)S(1)} %get-tuple-element.20.rest_0_), channel_id=1, source_target_pairs={{0,4},{4,0},{8,12},{12,8},{16,20},{20,16},{24,28},{28,24},{1,5},{5... | collective-permute-start | bytes 1105928 | tf_op jit(solution)/shard_map/ppermute | solution.py:337
  43.1 1.2 %copy-start.1 = (f32[2,32,32,32]{3,2,1,0:T(8,128)S(1)}, f32[2,32,32,32]{3,2,1,0:T(8,128)}, u32[]{:S(2)}) copy-start(f32[2,32,32,32]{3,2,1,0:T(8,128)} %coupling_ref.1) | copy-start | bytes 786436
  44.3 0.7 copy-start.3
  45.0 0.7 copy-start.4
  46.0 11.5 %collective-permute-start.17 = (f32[520,128]{1,0:T(8,128)S(1)}, f32[520,128]{1,0:T(8,128)S(1)}, u32[]{:S(2)}, u32[]{:S(2)}) collective-permute-start(f32[520,128]{1,0:T(8,128)S(1)} %pack_coupling.1.pack), channel_id=1, source_target_pairs={{0,24},{4,28},{8,16},{12,20},{16,8},{20,12},{24,0},{28,4},{1,25},{... | collective-permute-start | bytes 798728 | tf_op jit(solution)/shard_map/ppermute | solution.py:334
  47.5 18.5 %collective-permute-start.15 = (f32[520,128]{1,0:T(8,128)S(1)}, f32[520,128]{1,0:T(8,128)S(1)}, u32[]{:S(2)}, u32[]{:S(2)}) collective-permute-start(f32[520,128]{1,0:T(8,128)S(1)} %pack_coupling.1.pack), channel_id=1, source_target_pairs={{0,16},{4,20},{8,24},{12,28},{16,0},{20,4},{24,8},{28,12},{1,17},{... | collective-permute-start | bytes 798728 | tf_op jit(solution)/shard_map/ppermute | solution.py:334
  47.6 2.0 %collective-permute-start.11 = (f32[9,80,128]{2,1,0:T(8,128)S(1)}, f32[9,80,128]{2,1,0:T(8,128)S(1)}, u32[]{:S(2)}, u32[]{:S(2)}) collective-permute-start(f32[9,80,128]{2,1,0:T(8,128)S(1)} %collective-permute-done.7.rest_0_), channel_id=1, source_target_pairs={{0,4},{4,0},{8,12},{12,8},{16,20},{20,16},{24,28},{28,24},{1,5},{5... | collective-permute-start | bytes 1105928 | tf_op jit(solution)/shard_map/ppermute | solution.py:337
  47.8 24.8 %collective-permute-start.13 = (f32[520,128]{1,0:T(8,128)S(1)}, f32[520,128]{1,0:T(8,128)S(1)}, u32[]{:S(2)}, u32[]{:S(2)}) collective-permute-start(f32[520,128]{1,0:T(8,128)S(1)} %pack_coupling.1.pack), channel_id=1, source_target_pairs={{0,8},{4,12},{8,0},{12,4},{16,24},{20,28},{24,16},{28,20},{1,9},{5... | collective-permute-start | bytes 798728 | tf_op jit(solution)/shard_map/ppermute | solution.py:334
  49.6 4.2 %collective-permute-start.6 = (f32[9,80,128]{2,1,0:T(8,128)S(1)}, f32[9,80,128]{2,1,0:T(8,128)S(1)}, u32[]{:S(2)}, u32[]{:S(2)}) collective-permute-start(f32[9,80,128]{2,1,0:T(8,128)S(1)} %collective-permute-done.5.rest_0_), channel_id=1, source_target_pairs={{0,4},{4,0},{8,12},{12,8},{16,20},{20,16},{24,28},{28,24},{1,5},{5... | collective-permute-start | bytes 1105928 | tf_op jit(solution)/shard_map/ppermute | solution.py:337
  49.9 5.7 %collective-permute-start.1 = (f32[9,80,128]{2,1,0:T(8,128)S(1)}, f32[9,80,128]{2,1,0:T(8,128)S(1)}, u32[]{:S(2)}, u32[]{:S(2)}) collective-permute-start(f32[9,80,128]{2,1,0:T(8,128)S(1)} %collective-permute-done.rest_0_), channel_id=1, source_target_pairs={{0,4},{4,0},{8,12},{12,8},{16,20},{20,16},{24,28},{28,24},{1,5},{5... | collective-permute-start | bytes 1105928 | tf_op jit(solution)/shard_map/ppermute | solution.py:337
  63.5 22.0 %collective-permute-start.18 = (f32[8,64,128]{2,1,0:T(8,128)S(1)}, f32[8,64,128]{2,1,0:T(8,128)S(1)}, u32[]{:S(2)}, u32[]{:S(2)}) collective-permute-start(f32[8,64,128]{2,1,0:T(8,128)S(1)} %apply.7), channel_id=1, source_target_pairs={{0,24},{4,28},{8,16},{12,20},{16,8},{20,12},{24,0},{28,4},{1,25},{... | collective-permute-start | bytes 786440 | tf_op jit(solution)/shard_map/ppermute | solution.py:334
  72.1 13.4 %collective-permute-start.16 = (f32[8,64,128]{2,1,0:T(8,128)S(1)}, f32[8,64,128]{2,1,0:T(8,128)S(1)}, u32[]{:S(2)}, u32[]{:S(2)}) collective-permute-start(f32[8,64,128]{2,1,0:T(8,128)S(1)} %apply.6), channel_id=1, source_target_pairs={{0,16},{4,20},{8,24},{12,28},{16,0},{20,4},{24,8},{28,12},{1,17},{... | collective-permute-start | bytes 786440 | tf_op jit(solution)/shard_map/ppermute | solution.py:334
  78.8 7.9 %collective-permute-start.14 = (f32[8,64,128]{2,1,0:T(8,128)S(1)}, f32[8,64,128]{2,1,0:T(8,128)S(1)}, u32[]{:S(2)}, u32[]{:S(2)}) collective-permute-start(f32[8,64,128]{2,1,0:T(8,128)S(1)} %apply.5), channel_id=1, source_target_pairs={{0,8},{4,12},{8,0},{12,4},{16,24},{20,28},{24,16},{28,20},{1,9},{5... | collective-permute-start | bytes 786440 | tf_op jit(solution)/shard_map/ppermute | solution.py:334

commit v3 on v2

--- a/solution.py
+++ b/solution.py
@@ -7,10 +7,12 @@
 from jax.experimental.pallas import tpu as pltpu
 from jax.sharding import PartitionSpec as P
 
-PACK_LIMIT = 16
+PACK_LIMIT = 60
 PREPARE_LIMIT = 24
+UNPACK_LIMIT = 16
 APPLY_LIMIT = 24
 CHUNK = 4
+PIECES = 4
 
 
 def lane_index(rows):
@@ -40,28 +42,32 @@
     return value if shift == 0 else pltpu.roll(value, shift, 1)
 
 
-def pack_fields(geometry, u_ref, a_ref, *rest):
+def pack_kernel(geometry, u_hbm, a_hbm, coupling_hbm, source_hbm, expansion_hbm, *rest):
     layers, halves, ny, depth, chips = geometry
-    sends, stage = rest[:chips], rest[chips]
+    sends, pack = rest[:chips], rest[chips]
+    stage, u_ref, a_ref, coupling_ref, source_ref, expansion_ref, sems = rest[chips + 1 :]
     me = lax.axis_index("modes") // 2
+    rows_u = u_ref.shape[0] // PIECES
+    pairs = [(a_hbm, a_ref)]
+    pairs += [(u_hbm.at[pl.ds(i * rows_u, rows_u)], u_ref.at[pl.ds(i * rows_u, rows_u)]) for i in range(PIECES)]
+    pairs += [(coupling_hbm, coupling_ref), (source_hbm, source_ref), (expansion_hbm, expansion_ref)]
+    copies = [pltpu.make_async_copy(one, two, sems.at[i]) for i, (one, two) in enumerate(pairs)]
+    for copy in copies:
+        copy.start()
     lanes = lane_index(8)
     place = lanes % depth
-    row = 0
-    for ref in (u_ref, a_ref):
-        modes = ref.shape[0] // (layers * ny)
-
-        def group(g, carry, ref=ref, row=row):
-            target = pl.multiple_of(row + g * 8, 8)
+    cells = layers * ny
+
+    def regroup(ref, first, count, target):
+        def group(g, carry):
+            to = pl.multiple_of(target + g * 8, 8)
             by_layer = []
             for x in range(layers):
-                tiles = [
-                    ref[pl.ds(g * 8 * layers * ny + x * ny + y, 8, stride=layers * ny), :]
-                    for y in range(ny)
-                ]
+                tiles = [ref[pl.ds((first + g * 8) * cells + x * ny + y, 8, stride=cells), :] for y in range(ny)]
                 tiles = swap_lanes(tiles, depth, lanes)
                 by_layer.append(tiles)
                 for d in range(ny):
-                    stage[d // halves, x * halves + d % halves, pl.ds(target, 8), :] = tiles[d]
+                    stage[d // halves, x * halves + d % halves, pl.ds(to, 8), :] = tiles[d]
             for chip in range(chips):
                 rim = jnp.zeros((8, 128), jnp.float32)
                 left, right = chip * halves - 1, (chip + 1) * halves
@@ -71,29 +77,42 @@
                     if right < ny:
                         at = depth // 2 + x
                         rim = jnp.where(place == at, turn(by_layer[x][right], at), rim)
-                stage[chip, layers * halves, pl.ds(target, 8), :] = rim
+                stage[chip, layers * halves, pl.ds(to, 8), :] = rim
             return carry
 
-        lax.fori_loop(0, modes // 8, group, 0)
-        row += modes
-    for e in range(chips):
-        sends[e][...] = stage[e ^ me]
-
-
-def pack_coupling(coupling_ref, source_ref, expansion_ref, out_ref):
+        lax.fori_loop(0, count // 8, group, 0, unroll=True)
+        for e in range(chips):
+            rows = pl.ds(target, count)
+            copy = pltpu.make_async_copy(
+                stage.at[e ^ me, :, rows], sends[e].at[:, rows], sems.at[len(copies) + len(sent)]
+            )
+            copy.start()
+            sent.append(copy)
+
+    sent = []
+    local_a, local_u = a_ref.shape[0] // cells, u_ref.shape[0] // cells
+    copies[0].wait()
+    regroup(a_ref, 0, local_a, local_u)
+    for i in range(PIECES):
+        copies[1 + i].wait()
+        regroup(u_ref, i * (local_u // PIECES), local_u // PIECES, i * (local_u // PIECES))
+    for copy in copies[1 + PIECES :]:
+        copy.wait()
     blocks, slots, width, _ = coupling_ref.shape
     per = 128 // width
     groups = slots // per
     for block in range(blocks):
         for g in range(groups):
             rows = slice((block * groups + g) * width, (block * groups + g + 1) * width)
-            out_ref[rows, :] = jnp.concatenate(
+            pack[rows, :] = jnp.concatenate(
                 [coupling_ref[block, g * per + q] for q in range(per)], axis=1
             )
     last = blocks * groups * width
-    out_ref[last : last + 8, :] = jnp.zeros((8, 128), jnp.float32)
-    out_ref[last : last + blocks, 0:slots] = source_ref[...].astype(jnp.float32)
-    out_ref[last + blocks : last + 2 * blocks, 0:slots] = expansion_ref[...].astype(jnp.float32)
+    pack[last : last + 8, :] = jnp.zeros((8, 128), jnp.float32)
+    pack[last : last + blocks, 0:slots] = source_ref[...].astype(jnp.float32)
+    pack[last + blocks : last + 2 * blocks, 0:slots] = expansion_ref[...].astype(jnp.float32)
+    for copy in sent:
+        copy.wait()
 
 
 def laplacian(tile, low, high, rim, geometry, rows):
@@ -132,17 +151,23 @@
     return base, base + CHUNK * 128
 
 
-def prepare_kernel(geometry, width, local_u, local_a, e, *rest):
+def prepare_kernel(geometry, width, local_u, local_a, group, *rest):
     layers, halves, ny, depth, chips = geometry
-    body_refs, low_refs, high_refs = rest[0:2], rest[2:4], rest[4:6]
+    many = len(group)
+    bodies, low_ref, high_ref, other = rest[:many], rest[many], rest[many + 1], rest[many + 2]
     sources, fields = rest[-2:]
     tiles = layers * halves
     rim_at = 2 * tiles * 128
     me = lax.axis_index("modes")
 
-    for side in range(2):
-        body, low, high = body_refs[side], low_refs[side], high_refs[side]
-        device = me ^ (2 * e) ^ side
+    for i, side in [(i, side) for i in range(many) for side in range(2)]:
+        first = i * (tiles + 1)
+        body = other.at[pl.ds(first, tiles + 1)] if side else bodies[i]
+        first = many * (tiles + 1) + i * halves
+        low = other.at[pl.ds(first, halves)] if side else low_ref.at[pl.ds(i * halves, halves)]
+        first += many * halves
+        high = other.at[pl.ds(first, halves)] if side else high_ref.at[pl.ds(i * halves, halves)]
+        device = me ^ (2 * group[i]) ^ side
 
         def load(start, rows, body=body, low=low, high=high):
             part = pl.ds(start, rows)
@@ -175,7 +200,7 @@
             put(rim, rim_at + 2 * halves * 128)
             return carry
 
-        lax.fori_loop(0, local_u // 16, prepare_u, 0)
+        lax.fori_loop(0, local_u // 16, prepare_u, 0, unroll=4)
         tile, below, above, rim = load(local_u, local_a)
         lap = laplacian(tile, below, above, rim, geometry, local_a)
         rows = pl.ds(pl.multiple_of(device * local_a, local_a), local_a)
@@ -267,25 +292,33 @@
 
 def unpack_kernel(geometry, *rest):
     layers, halves, ny, depth, chips = geometry
-    parts, out_ref, stage = rest[:chips], rest[chips], rest[chips + 1]
+    parts, out_hbm = rest[:chips], rest[chips]
+    stage, out_ref, sems = rest[chips + 1 :]
     me = lax.axis_index("modes") // 2
     for e in range(chips):
         stage[e ^ me] = parts[e][...]
     lanes = lane_index(8)
-    modes = out_ref.shape[0] // (layers * ny)
+    cells = layers * ny
+    modes = out_ref.shape[0] // cells
+    size = modes // PIECES
 
     def group(g, carry):
         source = pl.multiple_of(g * 8, 8)
         for x in range(layers):
-            tiles = [
-                stage[d // halves, x * halves + d % halves, pl.ds(source, 8), :] for d in range(ny)
-            ]
+            tiles = [stage[d // halves, x * halves + d % halves, pl.ds(source, 8), :] for d in range(ny)]
             tiles = swap_lanes(tiles, depth, lanes)
             for y in range(ny):
-                out_ref[pl.ds(g * 8 * layers * ny + x * ny + y, 8, stride=layers * ny), :] = tiles[y]
+                out_ref[pl.ds(g * 8 * cells + x * ny + y, 8, stride=cells), :] = tiles[y]
         return carry
 
-    lax.fori_loop(0, modes // 8, group, 0)
+    copies = []
+    for i in range(PIECES):
+        lax.fori_loop(i * size // 8, (i + 1) * size // 8, group, 0)
+        rows = pl.ds(i * size * cells, size * cells)
+        copies.append(pltpu.make_async_copy(out_ref.at[rows], out_hbm.at[rows], sems.at[i]))
+        copies[-1].start()
+    for copy in copies:
+        copy.wait()
 
 
 def vmem(count):
@@ -317,18 +350,31 @@
             **more,
         )
 
-    sends = call(
-        functools.partial(pack_fields, geometry),
-        [jax.ShapeDtypeStruct((tiles + 1, modes, 128), f32)] * chips,
-        2,
-        [pltpu.VMEM((chips, tiles + 1, modes, 128), f32)],
-        PACK_LIMIT,
-        "pack_fields",
-    )(solution_modes.reshape(-1, nz), coefficient_modes.reshape(-1, nz))
     rows = blocks * slots * width // (128 // width)
-    pack = call(
-        pack_coupling, jax.ShapeDtypeStruct((rows + 8, 128), f32), 3, [], PACK_LIMIT, "pack_coupling"
-    )(coupling, source_block, expansion_index)
+    *sends, pack = pl.pallas_call(
+        functools.partial(pack_kernel, geometry),
+        out_shape=[jax.ShapeDtypeStruct((tiles + 1, modes, 128), f32)] * chips
+        + [jax.ShapeDtypeStruct((rows + 8, 128), f32)],
+        in_specs=[pl.BlockSpec(memory_space=pltpu.HBM)] * 5,
+        out_specs=[pl.BlockSpec(memory_space=pltpu.HBM)] * chips + vmem(1),
+        scratch_shapes=[
+            pltpu.VMEM((chips, tiles + 1, modes, 128), f32),
+            pltpu.VMEM((local_u * layers * ny, nz), f32),
+            pltpu.VMEM((local_a * layers * ny, nz), f32),
+            pltpu.VMEM(coupling.shape, f32),
+            pltpu.VMEM(source_block.shape, jnp.int32),
+            pltpu.VMEM(expansion_index.shape, jnp.int32),
+            pltpu.SemaphoreType.DMA((PIECES + 4 + chips * (PIECES + 1),)),
+        ],
+        compiler_params=pltpu.CompilerParams(vmem_limit_bytes=PACK_LIMIT * 1024 * 1024),
+        name="pack",
+    )(
+        solution_modes.reshape(-1, nz),
+        coefficient_modes.reshape(-1, nz),
+        coupling,
+        source_block,
+        expansion_index,
+    )
 
     def trade(value, e):
         return lax.ppermute(value, "modes", [(i, i ^ (2 * e)) for i in range(count)])
@@ -337,45 +383,35 @@
         return lax.ppermute(value, "modes", [(i, i ^ 1) for i in range(count)])
 
     bodies = [sends[0]] + [trade(sends[e], e) for e in range(1, chips)]
-    pack_later = lax.optimization_barrier((pack, bodies[1]))[0] if chips > 1 else pack
-    packs = [pack] + [trade(pack_later, e) for e in range(1, chips)]
+    late = lax.optimization_barrier((pack, bodies[-1]))[0]
+    packs = [pack] + [trade(late, e) for e in range(1, chips)]
     n_tiles = lax.axis_size("tiles")
     up = [(i, i + 1) for i in range(n_tiles - 1)]
     down = [(i + 1, i) for i in range(n_tiles - 1)]
-    low, high, other_low, other_high = [], [], [], []
-    for group in (range(0, chips - 1), range(chips - 1, chips)):
-        if not len(group):
-            continue
+    gathered = []
+    for group in (range(0, chips // 2), range(chips // 2, chips)):
         top = jnp.concatenate([bodies[e][tiles - halves : tiles] for e in group])
         bottom = jnp.concatenate([bodies[e][:halves] for e in group])
-        part = jnp.concatenate([lax.ppermute(top, "tiles", up), lax.ppermute(bottom, "tiles", down)])
-        other = sibling(part)
-        size = len(group) * halves
-        for i in range(len(group)):
-            here = slice(i * halves, (i + 1) * halves)
-            there = slice(size + i * halves, size + (i + 1) * halves)
-            low.append(part[here])
-            high.append(part[there])
-            other_low.append(other[here])
-            other_high.append(other[there])
-    others = [sibling(body) for body in bodies]
+        low, high = lax.ppermute(top, "tiles", up), lax.ppermute(bottom, "tiles", down)
+        mine = [bodies[e] for e in group] + [low, high]
+        gathered.append((group, mine + [sibling(jnp.concatenate(mine))]))
 
     ncol = 2 * tiles * 128 + (2 * halves + 1) * 128
     n_blocks = count * (local_u // width)
     prepared = ()
-    for e in range(chips):
+    for group, inputs in gathered:
         prepared = call(
-            functools.partial(prepare_kernel, geometry, width, local_u, local_a, e),
+            functools.partial(prepare_kernel, geometry, width, local_u, local_a, group),
             (
                 jax.ShapeDtypeStruct((n_blocks, 3 * width, ncol), jnp.bfloat16),
                 jax.ShapeDtypeStruct((count * local_a, ncol), f32),
             ),
-            6 + len(prepared),
+            len(inputs) + len(prepared),
             [],
             PREPARE_LIMIT,
             "prepare",
-            input_output_aliases={6: 0, 7: 1} if prepared else {},
-        )(bodies[e], others[e], low[e], other_low[e], high[e], other_high[e], *prepared)
+            input_output_aliases={len(inputs): 0, len(inputs) + 1: 1} if prepared else {},
+        )(*inputs, *prepared)
     sources, fields = prepared
 
     parts = [None] * chips
@@ -396,13 +432,18 @@
             "apply",
         )(packs[e], sources, fields)
         parts[e] = trade(result, e) if e else result
-    out = call(
+    out = pl.pallas_call(
         functools.partial(unpack_kernel, geometry),
-        jax.ShapeDtypeStruct((local_u * layers * ny, nz), f32),
-        chips,
-        [pltpu.VMEM((chips, tiles, local_u, 128), f32)],
-        PACK_LIMIT,
-        "unpack",
+        out_shape=jax.ShapeDtypeStruct((local_u * layers * ny, nz), f32),
+        in_specs=vmem(chips),
+        out_specs=pl.BlockSpec(memory_space=pl.ANY),
+        scratch_shapes=[
+            pltpu.VMEM((chips, tiles, local_u, 128), f32),
+            pltpu.VMEM((local_u * layers * ny, nz), f32),
+            pltpu.SemaphoreType.DMA((PIECES,)),
+        ],
+        compiler_params=pltpu.CompilerParams(vmem_limit_bytes=UNPACK_LIMIT * 1024 * 1024),
+        name="unpack",
     )(*parts)
     return out.reshape(solution_modes.shape)
 

time: 90.2 us -> 78.2 us (0.87)
  waiting for transfers between devices: 22.5 us -> 17.6 us
  local copies, waits for them, and re-layouts: 4.88 us -> 0.98 us
  Pallas kernels: 38.4 us -> 36.5 us
  starting transfers between devices: 23.7 us -> 22.2 us
    ppermute x9, waiting for transfers between devices: 17.5 us -> 11.9 us  [trade(): return lax.ppermute(value, 'modes', [(i, i ^ 2 * e) for i in range(count)])]
    unnamed x10 -> x4, local copies, waits for them, and re-layouts: 4.75 us -> 0.01 us
    pallas_call x4 -> x2, Pallas kernels: 7.14 us -> 4.1 us  [on_device(): call(functools.partial(prepare_kernel, geometry, width, local_u, local_a,...]
    ppermute x6 -> x2, starting transfers between devices: 1.37 us -> 0.14 us  [sibling(): return lax.ppermute(value, 'modes', [(i, i ^ 1) for i in range(count)])]
    pallas_call x3 -> x2, Pallas kernels: 6.92 us -> 8.03 us  [the longest x1 5.02 us: on_device(): pl.pallas_call(functools.partial(pack_kernel, geometry), out_shape=[jax.S...]
    slice x4, local copies, waits for them, and re-layouts: 0.05 us -> 0.97 us  [on_device(): bottom = jnp.concatenate([bodies[e][:halves] for e in group])]
  transfers between devices with their start and end apart: 19 -> 15, of which waited for: 5 -> 7; matrix products, arithmetic and copies ran while one was open for 0% -> 2% of each run, Pallas kernels for 35% -> 37%
where the time goes in v3:
time: 78.2 us; the launch traced here: 77.9 us
  Pallas kernels  36.5 us (47%)
  starting transfers between devices  22.2 us (28%)
  waiting for transfers between devices  17.6 us (23%)
  local copies, waits for them, and re-layouts  0.98 us (1%)
    pallas_call x4, Pallas kernels, on_device(): call(functools.partial(apply_kernel, geometry, blocks, slots, width), jax...  24.4 us
    ppermute x9, waiting for transfers between devices, trade(): return lax.ppermute(value, 'modes', [(i, i ^ 2 * e) for i in range(count)])  11.9 us
    ppermute x9, starting transfers between devices, trade(): return lax.ppermute(value, 'modes', [(i, i ^ 2 * e) for i in range(count)])  11.8 us
    ppermute x2, starting transfers between devices, on_device(): lax.ppermute(top, 'tiles', up)  7.68 us
    pallas_call x1, Pallas kernels, on_device(): pl.pallas_call(functools.partial(pack_kernel, geometry), out_shape=[jax.S...  5.02 us
    ppermute x2, waiting for transfers between devices, on_device(): lax.ppermute(bottom, 'tiles', down)  4.43 us
    pallas_call x2, Pallas kernels, on_device(): call(functools.partial(prepare_kernel, geometry, width, local_u, local_a,...  4.1 us
    pallas_call x1, Pallas kernels, on_device(): pl.pallas_call(functools.partial(unpack_kernel, geometry), out_shape=jax....  3.01 us
  transfers between devices with their start and end apart: 15, of which 7 were waited for; matrix products, arithmetic and copies ran while one was open for 2% of the time, Pallas kernels for 37%

profile of v3, /device:TPU:0, one launch (start us, length us, event | category | flops | bytes accessed | tf_op | source)
XLA Modules:
  0.0 77.9 jit_solution(13651691108967035498)
XLA Ops:
  0.0 5.0 %pack.1 = (f32[9,80,128]{2,1,0:T(8,128)}, f32[9,80,128]{2,1,0:T(8,128)}, f32[9,80,128]{2,1,0:T(8,128)}, f32[9,80,128]{2,1,0:T(8,128)}, f32[520,128]{1,0:T(8,128)}) custom-call(f32[2048,128]{1,0:T(8,128)} %bitcast.3, f32[512,128]{1,0:T(8,128)} %bitcast.4, f32[2,32,32,32]{3,2,1,0:T(8,128)} %coupling_hbm.1, s32[2,32]{1,0:T(2,128)} %source_hbm.1, ...), custom_call_target="tpu_custom_call" | custom-call | tf_op jit(solution)/shard_map/pack/pallas_call | solution.py:354
  5.0 3.0 %collective-permute-start.5 = (f32[9,80,128]{2,1,0:T(8,128)}, f32[9,80,128]{2,1,0:T(8,128)S(1)}, u32[]{:S(2)}, u32[]{:S(2)}) collective-permute-start(f32[9,80,128]{2,1,0:T(8,128)} %get-tuple-element.19), channel_id=1, source_target_pairs={{0,8},{4,12},{8,0},{12,4},{16,24},{20,28},{24,16},{28,20},{1,9},{5... | collective-permute-start | bytes 1105928 | tf_op jit(solution)/shard_map/ppermute | solution.py:380
  8.0 1.5 %collective-permute-start = (f32[9,80,128]{2,1,0:T(8,128)}, f32[9,80,128]{2,1,0:T(8,128)S(1)}, u32[]{:S(2)}, u32[]{:S(2)}) collective-permute-start(f32[9,80,128]{2,1,0:T(8,128)} %get-tuple-element.16), channel_id=1, source_target_pairs={{0,16},{4,20},{8,24},{12,28},{16,0},{20,4},{24,8},{28,12},{1,17},{... | collective-permute-start | bytes 1105928 | tf_op jit(solution)/shard_map/ppermute | solution.py:380
  9.6 0.9 %fusion = (f32[2,80,128]{2,1,0:T(8,128)S(1)}, f32[2,80,128]{2,1,0:T(8,128)S(1)}) fusion(f32[9,80,128]{2,1,0:T(8,128)} %get-tuple-element.18.rest_0_), kind=kLoop, calls=%fused_computation.6 | loop fusion | bytes 327680 | tf_op jit(solution)/shard_map/slice | solution.py:394
  10.5 7.1 %collective-permute-done.5.rest_1_ = f32[9,80,128]{2,1,0:T(8,128)S(1)} collective-permute-done((f32[9,80,128]{2,1,0:T(8,128)}, f32[9,80,128]{2,1,0:T(8,128)S(1)}, u32[]{:S(2)}, u32[]{:S(2)}) %collective-permute-start.5) | collective-permute-done | bytes 368672 | tf_op jit(solution)/shard_map/ppermute | solution.py:380
  17.7 4.2 %collective-permute-start.6 = (f32[4,80,128]{2,1,0:T(8,128)S(1)}, f32[4,80,128]{2,1,0:T(8,128)S(1)}, u32[]{:S(2)}, u32[]{:S(2)}) collective-permute-start(f32[4,80,128]{2,1,0:T(8,128)S(1)} %pad_maximum_fusion.4), channel_id=1, source_target_pairs={{0,1},{1,2},{2,3},{4,5},{5,6},{6,7},{8,9},{9,10},{10,11},{12,13},{... | collective-permute-start | bytes 491528 | tf_op jit(solution)/shard_map/ppermute | solution.py:395
  21.9 1.3 %collective-permute-start.7 = (f32[4,80,128]{2,1,0:T(8,128)S(1)}, f32[4,80,128]{2,1,0:T(8,128)S(1)}, u32[]{:S(2)}, u32[]{:S(2)}) collective-permute-start(f32[4,80,128]{2,1,0:T(8,128)S(1)} %pad_maximum_fusion.5), channel_id=1, source_target_pairs={{1,0},{2,1},{3,2},{5,4},{6,5},{7,6},{9,8},{10,9},{11,10},{13,12},{... | collective-permute-start | bytes 491528 | tf_op jit(solution)/shard_map/ppermute | solution.py:395
  23.2 2.8 %collective-permute-done.1.rest_1_ = f32[9,80,128]{2,1,0:T(8,128)S(1)} collective-permute-done((f32[9,80,128]{2,1,0:T(8,128)}, f32[9,80,128]{2,1,0:T(8,128)S(1)}, u32[]{:S(2)}, u32[]{:S(2)}) %collective-permute-start.1) | collective-permute-done | bytes 368672 | tf_op jit(solution)/shard_map/ppermute | solution.py:380
  26.1 0.1 collective-permute-done.rest_0_
  26.2 3.5 %collective-permute-start.2 = (f32[4,80,128]{2,1,0:T(8,128)S(1)}, f32[4,80,128]{2,1,0:T(8,128)S(1)}, u32[]{:S(2)}, u32[]{:S(2)}) collective-permute-start(f32[4,80,128]{2,1,0:T(8,128)S(1)} %pad_maximum_fusion.2), channel_id=1, source_target_pairs={{0,1},{1,2},{2,3},{4,5},{5,6},{6,7},{8,9},{9,10},{10,11},{12,13},{... | collective-permute-start | bytes 491528 | tf_op jit(solution)/shard_map/ppermute | solution.py:395
  29.7 1.3 %collective-permute-start.3 = (f32[4,80,128]{2,1,0:T(8,128)S(1)}, f32[4,80,128]{2,1,0:T(8,128)S(1)}, u32[]{:S(2)}, u32[]{:S(2)}) collective-permute-start(f32[4,80,128]{2,1,0:T(8,128)S(1)} %pad_maximum_fusion.3), channel_id=1, source_target_pairs={{1,0},{2,1},{3,2},{5,4},{6,5},{7,6},{9,8},{10,9},{11,10},{13,12},{... | collective-permute-start | bytes 491528 | tf_op jit(solution)/shard_map/ppermute | solution.py:395
  31.1 0.1 pad_maximum_fusion.1
  31.2 0.1 collective-permute-start.8
  31.2 1.3 %collective-permute-done.2.rest_2_ = f32[4,80,128]{2,1,0:T(8,128)S(1)} collective-permute-done((f32[4,80,128]{2,1,0:T(8,128)S(1)}, f32[4,80,128]{2,1,0:T(8,128)S(1)}, u32[]{:S(2)}, u32[]{:S(2)}) %collective-permute-start.2) | collective-permute-done | bytes 163872 | tf_op jit(solution)/shard_map/ppermute | solution.py:395
  32.5 4.4 %collective-permute-done.3.rest_3_ = f32[4,80,128]{2,1,0:T(8,128)S(1)} collective-permute-done((f32[4,80,128]{2,1,0:T(8,128)S(1)}, f32[4,80,128]{2,1,0:T(8,128)S(1)}, u32[]{:S(2)}, u32[]{:S(2)}) %collective-permute-start.3) | collective-permute-done | bytes 163872 | tf_op jit(solution)/shard_map/ppermute | solution.py:395
  37.0 0.1 pad_maximum_fusion
  37.0 0.1 collective-permute-start.4
  37.1 1.3 %collective-permute-start.9 = (f32[520,128]{1,0:T(8,128)S(1)}, f32[520,128]{1,0:T(8,128)S(1)}, u32[]{:S(2)}, u32[]{:S(2)}) collective-permute-start(f32[520,128]{1,0:T(8,128)S(1)} %copy-done.1), channel_id=1, source_target_pairs={{0,8},{4,12},{8,0},{12,4},{16,24},{20,28},{24,16},{28,20},{1,9},{5... | collective-permute-start | bytes 798728 | tf_op jit(solution)/shard_map/ppermute | solution.py:380
  38.5 0.8 %collective-permute-start.11 = (f32[520,128]{1,0:T(8,128)S(1)}, f32[520,128]{1,0:T(8,128)S(1)}, u32[]{:S(2)}, u32[]{:S(2)}) collective-permute-start(f32[520,128]{1,0:T(8,128)S(1)} %copy-done.1), channel_id=1, source_target_pairs={{0,16},{4,20},{8,24},{12,28},{16,0},{20,4},{24,8},{28,12},{1,17},{... | collective-permute-start | bytes 798728 | tf_op jit(solution)/shard_map/ppermute | solution.py:380
  39.2 1.4 %collective-permute-start.13 = (f32[520,128]{1,0:T(8,128)S(1)}, f32[520,128]{1,0:T(8,128)S(1)}, u32[]{:S(2)}, u32[]{:S(2)}) collective-permute-start(f32[520,128]{1,0:T(8,128)S(1)} %copy-done.1), channel_id=1, source_target_pairs={{0,24},{4,28},{8,16},{12,20},{16,8},{20,12},{24,0},{28,4},{1,25},{... | collective-permute-start | bytes 798728 | tf_op jit(solution)/shard_map/ppermute | solution.py:380
  40.7 2.0 %prepare.2 = (bf16[16,96,2688]{2,1,0:T(8,128)(2,1)S(1)}, f32[128,2688]{1,0:T(8,128)S(1)}) custom-call(f32[9,80,128]{2,1,0:T(8,128)S(1)} %copy-done, f32[9,80,128]{2,1,0:T(8,128)S(1)} %collective-permute-done.5.rest_1_, f32[4,80,128]{2,1,0:T(8,128)S(1)} %collective-permute-done.6.rest_2_, f32[4,80,128]{2,1,0:T(8,128)S(1)} %collective-permute-done.7.rest_3_, ...), custom_call_target="tpu_custom_call" | custom-call | tf_op jit(solution)/shard_map/prepare/pallas_call | solution.py:403
  42.7 2.1 %prepare.3 = (bf16[16,96,2688]{2,1,0:T(8,128)(2,1)S(1)}, f32[128,2688]{1,0:T(8,128)S(1)}) custom-call(f32[9,80,128]{2,1,0:T(8,128)S(1)} %collective-permute-done.rest_0_, f32[9,80,128]{2,1,0:T(8,128)S(1)} %collective-permute-done.1.rest_1_, f32[4,80,128]{2,1,0:T(8,128)S(1)} %collective-permute-done.2.rest_2_, ...), custom_call_target="tpu_custom_call", output_to_operand_aliasing={{0}: (5, {}), {1}: (6, {})} | custom-call | tf_op jit(solution)/shard_map/prepare/pallas_call | solution.py:403
  44.8 1.6 %collective-permute-done.9.pack = f32[520,128]{1,0:T(8,128)S(1)} collective-permute-done((f32[520,128]{1,0:T(8,128)S(1)}, f32[520,128]{1,0:T(8,128)S(1)}, u32[]{:S(2)}, u32[]{:S(2)}) %collective-permute-start.9) | collective-permute-done | bytes 266272 | tf_op jit(solution)/shard_map/ppermute | solution.py:380
  46.4 6.2 %apply.5 = f32[8,64,128]{2,1,0:T(8,128)S(1)} custom-call(f32[520,128]{1,0:T(8,128)S(1)} %collective-permute-done.9.pack, bf16[16,96,2688]{2,1,0:T(8,128)(2,1)S(1)} %get-tuple-element.22.sources, f32[128,2688]{1,0:T(8,128)S(1)} %get-tuple-element.23.fields), custom_call_target="tpu_custom_call" | custom-call | tf_op jit(solution)/shard_map/apply/pallas_call | solution.py:419
  52.6 1.3 %collective-permute-start.10 = (f32[8,64,128]{2,1,0:T(8,128)S(1)}, f32[8,64,128]{2,1,0:T(8,128)S(1)}, u32[]{:S(2)}, u32[]{:S(2)}) collective-permute-start(f32[8,64,128]{2,1,0:T(8,128)S(1)} %apply.5), channel_id=1, source_target_pairs={{0,8},{4,12},{8,0},{12,4},{16,24},{20,28},{24,16},{28,20},{1,9},{5... | collective-permute-start | bytes 786440 | tf_op jit(solution)/shard_map/ppermute | solution.py:380
  54.0 6.0 %apply.6 = f32[8,64,128]{2,1,0:T(8,128)S(1)} custom-call(f32[520,128]{1,0:T(8,128)S(1)} %collective-permute-done.11.pack, bf16[16,96,2688]{2,1,0:T(8,128)(2,1)S(1)} %get-tuple-element.22.sources, f32[128,2688]{1,0:T(8,128)S(1)} %get-tuple-element.23.fields), custom_call_target="tpu_custom_call" | custom-call | tf_op jit(solution)/shard_map/apply/pallas_call | solution.py:419
  60.0 0.9 %collective-permute-start.12 = (f32[8,64,128]{2,1,0:T(8,128)S(1)}, f32[8,64,128]{2,1,0:T(8,128)S(1)}, u32[]{:S(2)}, u32[]{:S(2)}) collective-permute-start(f32[8,64,128]{2,1,0:T(8,128)S(1)} %apply.6), channel_id=1, source_target_pairs={{0,16},{4,20},{8,24},{12,28},{16,0},{20,4},{24,8},{28,12},{1,17},{... | collective-permute-start | bytes 786440 | tf_op jit(solution)/shard_map/ppermute | solution.py:380
  60.9 6.1 %apply.7 = f32[8,64,128]{2,1,0:T(8,128)S(1)} custom-call(f32[520,128]{1,0:T(8,128)S(1)} %collective-permute-done.13.pack, bf16[16,96,2688]{2,1,0:T(8,128)(2,1)S(1)} %get-tuple-element.22.sources, f32[128,2688]{1,0:T(8,128)S(1)} %get-tuple-element.23.fields), custom_call_target="tpu_custom_call" | custom-call | tf_op jit(solution)/shard_map/apply/pallas_call | solution.py:419
  66.9 1.5 %collective-permute-start.14 = (f32[8,64,128]{2,1,0:T(8,128)S(1)}, f32[8,64,128]{2,1,0:T(8,128)S(1)}, u32[]{:S(2)}, u32[]{:S(2)}) collective-permute-start(f32[8,64,128]{2,1,0:T(8,128)S(1)} %apply.7), channel_id=1, source_target_pairs={{0,24},{4,28},{8,16},{12,20},{16,8},{20,12},{24,0},{28,4},{1,25},{... | collective-permute-start | bytes 786440 | tf_op jit(solution)/shard_map/ppermute | solution.py:380
  68.4 6.1 %apply.4.rest_0_ = f32[8,64,128]{2,1,0:T(8,128)S(1)} custom-call(f32[520,128]{1,0:T(8,128)S(1)} %copy-done.1, bf16[16,96,2688]{2,1,0:T(8,128)(2,1)S(1)} %get-tuple-element.22.sources, f32[128,2688]{1,0:T(8,128)S(1)} %get-tuple-element.23.fields), custom_call_target="tpu_custom_call" | custom-call | tf_op jit(solution)/shard_map/apply/pallas_call | solution.py:419
  74.5 0.2 collective-permute-done.14.rest_3_
  74.7 3.0 %unpack.1 = f32[2048,128]{1,0:T(8,128)} custom-call(f32[8,64,128]{2,1,0:T(8,128)S(1)} %apply.4.rest_0_, f32[8,64,128]{2,1,0:T(8,128)S(1)} %collective-permute-done.10.rest_1_, f32[8,64,128]{2,1,0:T(8,128)S(1)} %collective-permute-done.12.rest_2_, f32[8,64,128]{2,1,0:T(8,128)S(1)} %collective-permute-done.14.rest_3_), custom_call_target="tpu_custom_call" | custom-call | tf_op jit(solution)/shard_map/unpack/pallas_call | solution.py:435
  (20 shorter events, 0.1 us)
Async XLA Ops:
  5.0 12.6 %collective-permute-start.5 = (f32[9,80,128]{2,1,0:T(8,128)}, f32[9,80,128]{2,1,0:T(8,128)S(1)}, u32[]{:S(2)}, u32[]{:S(2)}) collective-permute-start(f32[9,80,128]{2,1,0:T(8,128)} %get-tuple-element.19), channel_id=1, source_target_pairs={{0,8},{4,12},{8,0},{12,4},{16,24},{20,28},{24,16},{28,20},{1,9},{5... | collective-permute-start | bytes 1105928 | tf_op jit(solution)/shard_map/ppermute | solution.py:380
  8.0 18.2 %collective-permute-start = (f32[9,80,128]{2,1,0:T(8,128)}, f32[9,80,128]{2,1,0:T(8,128)S(1)}, u32[]{:S(2)}, u32[]{:S(2)}) collective-permute-start(f32[9,80,128]{2,1,0:T(8,128)} %get-tuple-element.16), channel_id=1, source_target_pairs={{0,16},{4,20},{8,24},{12,28},{16,0},{20,4},{24,8},{28,12},{1,17},{... | collective-permute-start | bytes 1105928 | tf_op jit(solution)/shard_map/ppermute | solution.py:380
  9.6 16.5 %collective-permute-start.1 = (f32[9,80,128]{2,1,0:T(8,128)}, f32[9,80,128]{2,1,0:T(8,128)S(1)}, u32[]{:S(2)}, u32[]{:S(2)}) collective-permute-start(f32[9,80,128]{2,1,0:T(8,128)} %get-tuple-element.17), channel_id=1, source_target_pairs={{0,24},{4,28},{8,16},{12,20},{16,8},{20,12},{24,0},{28,4},{1,25},{... | collective-permute-start | bytes 1105928 | tf_op jit(solution)/shard_map/ppermute | solution.py:380
  17.7 13.4 %copy-start = (f32[9,80,128]{2,1,0:T(8,128)S(1)}, f32[9,80,128]{2,1,0:T(8,128)}, u32[]{:S(2)}) copy-start(f32[9,80,128]{2,1,0:T(8,128)} %get-tuple-element.18.rest_0_) | copy-start | bytes 1105924
  17.7 13.3 %collective-permute-start.6 = (f32[4,80,128]{2,1,0:T(8,128)S(1)}, f32[4,80,128]{2,1,0:T(8,128)S(1)}, u32[]{:S(2)}, u32[]{:S(2)}) collective-permute-start(f32[4,80,128]{2,1,0:T(8,128)S(1)} %pad_maximum_fusion.4), channel_id=1, source_target_pairs={{0,1},{1,2},{2,3},{4,5},{5,6},{6,7},{8,9},{9,10},{10,11},{12,13},{... | collective-permute-start | bytes 491528 | tf_op jit(solution)/shard_map/ppermute | solution.py:395
  21.9 9.1 %collective-permute-start.7 = (f32[4,80,128]{2,1,0:T(8,128)S(1)}, f32[4,80,128]{2,1,0:T(8,128)S(1)}, u32[]{:S(2)}, u32[]{:S(2)}) collective-permute-start(f32[4,80,128]{2,1,0:T(8,128)S(1)} %pad_maximum_fusion.5), channel_id=1, source_target_pairs={{1,0},{2,1},{3,2},{5,4},{6,5},{7,6},{9,8},{10,9},{11,10},{13,12},{... | collective-permute-start | bytes 491528 | tf_op jit(solution)/shard_map/ppermute | solution.py:395
  26.2 6.3 %collective-permute-start.2 = (f32[4,80,128]{2,1,0:T(8,128)S(1)}, f32[4,80,128]{2,1,0:T(8,128)S(1)}, u32[]{:S(2)}, u32[]{:S(2)}) collective-permute-start(f32[4,80,128]{2,1,0:T(8,128)S(1)} %pad_maximum_fusion.2), channel_id=1, source_target_pairs={{0,1},{1,2},{2,3},{4,5},{5,6},{6,7},{8,9},{9,10},{10,11},{12,13},{... | collective-permute-start | bytes 491528 | tf_op jit(solution)/shard_map/ppermute | solution.py:395
  29.7 7.2 %collective-permute-start.3 = (f32[4,80,128]{2,1,0:T(8,128)S(1)}, f32[4,80,128]{2,1,0:T(8,128)S(1)}, u32[]{:S(2)}, u32[]{:S(2)}) collective-permute-start(f32[4,80,128]{2,1,0:T(8,128)S(1)} %pad_maximum_fusion.3), channel_id=1, source_target_pairs={{1,0},{2,1},{3,2},{5,4},{6,5},{7,6},{9,8},{10,9},{11,10},{13,12},{... | collective-permute-start | bytes 491528 | tf_op jit(solution)/shard_map/ppermute | solution.py:395
  31.2 6.0 %copy-start.1 = (f32[520,128]{1,0:T(8,128)S(1)}, f32[520,128]{1,0:T(8,128)}, u32[]{:S(2)}) copy-start(f32[520,128]{1,0:T(8,128)} %get-tuple-element.24.pack) | copy-start | bytes 798724
  31.2 9.5 %collective-permute-start.8 = (f32[26,80,128]{2,1,0:T(8,128)S(1)}, f32[26,80,128]{2,1,0:T(8,128)S(1)}, u32[]{:S(2)}, u32[]{:S(2)}) collective-permute-start(f32[26,80,128]{2,1,0:T(8,128)S(1)} %pad_maximum_fusion.1), channel_id=1, source_target_pairs={{0,4},{4,0},{8,12},{12,8},{16,20},{20,16},{24,28},{28,24},{1,5},{5... | collective-permute-start | bytes 3194888 | tf_op jit(solution)/shard_map/ppermute | solution.py:383
  37.0 5.7 %collective-permute-start.4 = (f32[26,80,128]{2,1,0:T(8,128)S(1)}, f32[26,80,128]{2,1,0:T(8,128)S(1)}, u32[]{:S(2)}, u32[]{:S(2)}) collective-permute-start(f32[26,80,128]{2,1,0:T(8,128)S(1)} %pad_maximum_fusion), channel_id=1, source_target_pairs={{0,4},{4,0},{8,12},{12,8},{16,20},{20,16},{24,28},{28,24},{1,5},{5... | collective-permute-start | bytes 3194888 | tf_op jit(solution)/shard_map/ppermute | solution.py:383
  37.1 9.3 %collective-permute-start.9 = (f32[520,128]{1,0:T(8,128)S(1)}, f32[520,128]{1,0:T(8,128)S(1)}, u32[]{:S(2)}, u32[]{:S(2)}) collective-permute-start(f32[520,128]{1,0:T(8,128)S(1)} %copy-done.1), channel_id=1, source_target_pairs={{0,8},{4,12},{8,0},{12,4},{16,24},{20,28},{24,16},{28,20},{1,9},{5... | collective-permute-start | bytes 798728 | tf_op jit(solution)/shard_map/ppermute | solution.py:380
  38.5 15.5 %collective-permute-start.11 = (f32[520,128]{1,0:T(8,128)S(1)}, f32[520,128]{1,0:T(8,128)S(1)}, u32[]{:S(2)}, u32[]{:S(2)}) collective-permute-start(f32[520,128]{1,0:T(8,128)S(1)} %copy-done.1), channel_id=1, source_target_pairs={{0,16},{4,20},{8,24},{12,28},{16,0},{20,4},{24,8},{28,12},{1,17},{... | collective-permute-start | bytes 798728 | tf_op jit(solution)/shard_map/ppermute | solution.py:380
  39.2 21.6 %collective-permute-start.13 = (f32[520,128]{1,0:T(8,128)S(1)}, f32[520,128]{1,0:T(8,128)S(1)}, u32[]{:S(2)}, u32[]{:S(2)}) collective-permute-start(f32[520,128]{1,0:T(8,128)S(1)} %copy-done.1), channel_id=1, source_target_pairs={{0,24},{4,28},{8,16},{12,20},{16,8},{20,12},{24,0},{28,4},{1,25},{... | collective-permute-start | bytes 798728 | tf_op jit(solution)/shard_map/ppermute | solution.py:380
  52.6 21.9 %collective-permute-start.10 = (f32[8,64,128]{2,1,0:T(8,128)S(1)}, f32[8,64,128]{2,1,0:T(8,128)S(1)}, u32[]{:S(2)}, u32[]{:S(2)}) collective-permute-start(f32[8,64,128]{2,1,0:T(8,128)S(1)} %apply.5), channel_id=1, source_target_pairs={{0,8},{4,12},{8,0},{12,4},{16,24},{20,28},{24,16},{28,20},{1,9},{5... | collective-permute-start | bytes 786440 | tf_op jit(solution)/shard_map/ppermute | solution.py:380
  60.0 14.5 %collective-permute-start.12 = (f32[8,64,128]{2,1,0:T(8,128)S(1)}, f32[8,64,128]{2,1,0:T(8,128)S(1)}, u32[]{:S(2)}, u32[]{:S(2)}) collective-permute-start(f32[8,64,128]{2,1,0:T(8,128)S(1)} %apply.6), channel_id=1, source_target_pairs={{0,16},{4,20},{8,24},{12,28},{16,0},{20,4},{24,8},{28,12},{1,17},{... | collective-permute-start | bytes 786440 | tf_op jit(solution)/shard_map/ppermute | solution.py:380
  66.9 7.8 %collective-permute-start.14 = (f32[8,64,128]{2,1,0:T(8,128)S(1)}, f32[8,64,128]{2,1,0:T(8,128)S(1)}, u32[]{:S(2)}, u32[]{:S(2)}) collective-permute-start(f32[8,64,128]{2,1,0:T(8,128)S(1)} %apply.7), channel_id=1, source_target_pairs={{0,24},{4,28},{8,16},{12,20},{16,8},{20,12},{24,0},{28,4},{1,25},{... | collective-permute-start | bytes 786440 | tf_op jit(solution)/shard_map/ppermute | solution.py:380

commit v4 on v3

--- a/solution.py
+++ b/solution.py
@@ -42,15 +42,13 @@
     return value if shift == 0 else pltpu.roll(value, shift, 1)
 
 
-def pack_kernel(geometry, u_hbm, a_hbm, coupling_hbm, source_hbm, expansion_hbm, *rest):
+def pack_kernel(geometry, u_hbm, a_hbm, *rest):
     layers, halves, ny, depth, chips = geometry
-    sends, pack = rest[:chips], rest[chips]
-    stage, u_ref, a_ref, coupling_ref, source_ref, expansion_ref, sems = rest[chips + 1 :]
+    sends, (stage, u_ref, a_ref, sems) = rest[:chips], rest[chips:]
     me = lax.axis_index("modes") // 2
     rows_u = u_ref.shape[0] // PIECES
     pairs = [(a_hbm, a_ref)]
     pairs += [(u_hbm.at[pl.ds(i * rows_u, rows_u)], u_ref.at[pl.ds(i * rows_u, rows_u)]) for i in range(PIECES)]
-    pairs += [(coupling_hbm, coupling_ref), (source_hbm, source_ref), (expansion_hbm, expansion_ref)]
     copies = [pltpu.make_async_copy(one, two, sems.at[i]) for i, (one, two) in enumerate(pairs)]
     for copy in copies:
         copy.start()
@@ -96,8 +94,11 @@
     for i in range(PIECES):
         copies[1 + i].wait()
         regroup(u_ref, i * (local_u // PIECES), local_u // PIECES, i * (local_u // PIECES))
-    for copy in copies[1 + PIECES :]:
+    for copy in sent:
         copy.wait()
+
+
+def pack_coupling(coupling_ref, source_ref, expansion_ref, pack):
     blocks, slots, width, _ = coupling_ref.shape
     per = 128 // width
     groups = slots // per
@@ -111,8 +112,6 @@
     pack[last : last + 8, :] = jnp.zeros((8, 128), jnp.float32)
     pack[last : last + blocks, 0:slots] = source_ref[...].astype(jnp.float32)
     pack[last + blocks : last + 2 * blocks, 0:slots] = expansion_ref[...].astype(jnp.float32)
-    for copy in sent:
-        copy.wait()
 
 
 def laplacian(tile, low, high, rim, geometry, rows):
@@ -351,30 +350,31 @@
         )
 
     rows = blocks * slots * width // (128 // width)
-    *sends, pack = pl.pallas_call(
+    sends = pl.pallas_call(
         functools.partial(pack_kernel, geometry),
-        out_shape=[jax.ShapeDtypeStruct((tiles + 1, modes, 128), f32)] * chips
-        + [jax.ShapeDtypeStruct((rows + 8, 128), f32)],
-        in_specs=[pl.BlockSpec(memory_space=pltpu.HBM)] * 5,
-        out_specs=[pl.BlockSpec(memory_space=pltpu.HBM)] * chips + vmem(1),
+        out_shape=[jax.ShapeDtypeStruct((tiles + 1, modes, 128), f32)] * chips,
+        in_specs=[pl.BlockSpec(memory_space=pltpu.HBM)] * 2,
+        out_specs=[pl.BlockSpec(memory_space=pltpu.HBM)] * chips,
         scratch_shapes=[
             pltpu.VMEM((chips, tiles + 1, modes, 128), f32),
             pltpu.VMEM((local_u * layers * ny, nz), f32),
             pltpu.VMEM((local_a * layers * ny, nz), f32),
-            pltpu.VMEM(coupling.shape, f32),
-            pltpu.VMEM(source_block.shape, jnp.int32),
-            pltpu.VMEM(expansion_index.shape, jnp.int32),
-            pltpu.SemaphoreType.DMA((PIECES + 4 + chips * (PIECES + 1),)),
+            pltpu.SemaphoreType.DMA((PIECES + 1 + chips * (PIECES + 1),)),
         ],
         compiler_params=pltpu.CompilerParams(vmem_limit_bytes=PACK_LIMIT * 1024 * 1024),
         name="pack",
     )(
         solution_modes.reshape(-1, nz),
         coefficient_modes.reshape(-1, nz),
-        coupling,
-        source_block,
-        expansion_index,
     )
+    pack = call(
+        pack_coupling,
+        jax.ShapeDtypeStruct((rows + 8, 128), f32),
+        3,
+        [],
+        UNPACK_LIMIT,
+        "pack_coupling",
+    )(coupling, source_block, expansion_index)
 
     def trade(value, e):
         return lax.ppermute(value, "modes", [(i, i ^ (2 * e)) for i in range(count)])
@@ -389,7 +389,7 @@
     up = [(i, i + 1) for i in range(n_tiles - 1)]
     down = [(i + 1, i) for i in range(n_tiles - 1)]
     gathered = []
-    for group in (range(0, chips // 2), range(chips // 2, chips)):
+    for group in ([0, chips - 1], list(range(1, chips - 1))):
         top = jnp.concatenate([bodies[e][tiles - halves : tiles] for e in group])
         bottom = jnp.concatenate([bodies[e][:halves] for e in group])
         low, high = lax.ppermute(top, "tiles", up), lax.ppermute(bottom, "tiles", down)

time: 78.2 us -> 76.9 us (0.983)
  waiting for transfers between devices: 17.6 us -> 15.7 us
  starting transfers between devices: 22.2 us -> 23.3 us
    ppermute x2, waiting for transfers between devices: 4.43 us -> 1.62 us  [on_device(): lax.ppermute(bottom, 'tiles', down)]
    ppermute x2, starting transfers between devices: 7.68 us -> 8.69 us  [on_device(): lax.ppermute(top, 'tiles', up)]
    ppermute x9, waiting for transfers between devices: 11.9 us -> 12.9 us  [trade(): return lax.ppermute(value, 'modes', [(i, i ^ 2 * e) for i in range(count)])]
  transfers between devices with their start and end apart: 15 -> 15, of which waited for: 7 -> 6; matrix products, arithmetic and copies ran while one was open for 2% -> 2% of each run, Pallas kernels for 37% -> 37%
where the time goes in v4:
time: 76.9 us; the launch traced here: 76.6 us
  Pallas kernels  36 us (47%)
  starting transfers between devices  23.3 us (30%)
  waiting for transfers between devices  15.7 us (20%)
  local copies, waits for them, and re-layouts  1 us (1%)
    pallas_call x4, Pallas kernels, on_device(): call(functools.partial(apply_kernel, geometry, blocks, slots, width), jax...  24.4 us
    ppermute x9, waiting for transfers between devices, trade(): return lax.ppermute(value, 'modes', [(i, i ^ 2 * e) for i in range(count)])  12.9 us
    ppermute x9, starting transfers between devices, trade(): return lax.ppermute(value, 'modes', [(i, i ^ 2 * e) for i in range(count)])  11.8 us
    ppermute x2, starting transfers between devices, on_device(): lax.ppermute(top, 'tiles', up)  8.69 us
    pallas_call x1, Pallas kernels, on_device(): pl.pallas_call(functools.partial(pack_kernel, geometry), out_shape=[jax.S...  4.27 us
    pallas_call x2, Pallas kernels, on_device(): call(functools.partial(prepare_kernel, geometry, width, local_u, local_a,...  4.09 us
    pallas_call x1, Pallas kernels, on_device(): pl.pallas_call(functools.partial(unpack_kernel, geometry), out_shape=jax....  3.01 us
    ppermute x2, starting transfers between devices, on_device(): lax.ppermute(bottom, 'tiles', down)  2.58 us
  transfers between devices with their start and end apart: 15, of which 6 were waited for; matrix products, arithmetic and copies ran while one was open for 2% of the time, Pallas kernels for 37%

profile of v4, /device:TPU:0, one launch (start us, length us, event | category | flops | bytes accessed | tf_op | source)
XLA Modules:
  0.0 76.6 jit_solution(12904289181796987399)
XLA Ops:
  0.0 4.3 %pack.1 = (f32[9,80,128]{2,1,0:T(8,128)}, f32[9,80,128]{2,1,0:T(8,128)}, f32[9,80,128]{2,1,0:T(8,128)}, f32[9,80,128]{2,1,0:T(8,128)}) custom-call(f32[2048,128]{1,0:T(8,128)} %bitcast.3, f32[512,128]{1,0:T(8,128)} %bitcast.4), custom_call_target="tpu_custom_call" | custom-call | tf_op jit(solution)/shard_map/pack/pallas_call | solution.py:353
  4.3 4.0 %collective-permute-start.5 = (f32[9,80,128]{2,1,0:T(8,128)}, f32[9,80,128]{2,1,0:T(8,128)S(1)}, u32[]{:S(2)}, u32[]{:S(2)}) collective-permute-start(f32[9,80,128]{2,1,0:T(8,128)} %get-tuple-element.17), channel_id=1, source_target_pairs={{0,24},{4,28},{8,16},{12,20},{16,8},{20,12},{24,0},{28,4},{1,25},{... | collective-permute-start | bytes 1105928 | tf_op jit(solution)/shard_map/ppermute | solution.py:380
  8.2 0.5 collective-permute-start
  8.8 0.1 collective-permute-start.1
  8.9 0.9 %fusion = (f32[2,80,128]{2,1,0:T(8,128)S(1)}, f32[2,80,128]{2,1,0:T(8,128)S(1)}) fusion(f32[9,80,128]{2,1,0:T(8,128)} %get-tuple-element.16.rest_0_), kind=kLoop, calls=%fused_computation.6 | loop fusion | bytes 327680 | tf_op jit(solution)/shard_map/slice | solution.py:394
  9.8 8.1 %collective-permute-done.5.rest_1_ = f32[9,80,128]{2,1,0:T(8,128)S(1)} collective-permute-done((f32[9,80,128]{2,1,0:T(8,128)}, f32[9,80,128]{2,1,0:T(8,128)S(1)}, u32[]{:S(2)}, u32[]{:S(2)}) %collective-permute-start.5) | collective-permute-done | bytes 368672 | tf_op jit(solution)/shard_map/ppermute | solution.py:380
  18.0 4.1 %collective-permute-start.6 = (f32[4,80,128]{2,1,0:T(8,128)S(1)}, f32[4,80,128]{2,1,0:T(8,128)S(1)}, u32[]{:S(2)}, u32[]{:S(2)}) collective-permute-start(f32[4,80,128]{2,1,0:T(8,128)S(1)} %pad_maximum_fusion.4), channel_id=1, source_target_pairs={{0,1},{1,2},{2,3},{4,5},{5,6},{6,7},{8,9},{9,10},{10,11},{12,13},{... | collective-permute-start | bytes 491528 | tf_op jit(solution)/shard_map/ppermute | solution.py:395
  22.1 1.3 %collective-permute-start.7 = (f32[4,80,128]{2,1,0:T(8,128)S(1)}, f32[4,80,128]{2,1,0:T(8,128)S(1)}, u32[]{:S(2)}, u32[]{:S(2)}) collective-permute-start(f32[4,80,128]{2,1,0:T(8,128)S(1)} %pad_maximum_fusion.5), channel_id=1, source_target_pairs={{1,0},{2,1},{3,2},{5,4},{6,5},{7,6},{9,8},{10,9},{11,10},{13,12},{... | collective-permute-start | bytes 491528 | tf_op jit(solution)/shard_map/ppermute | solution.py:395
  23.4 1.8 %collective-permute-done.rest_0_ = f32[9,80,128]{2,1,0:T(8,128)S(1)} collective-permute-done((f32[9,80,128]{2,1,0:T(8,128)}, f32[9,80,128]{2,1,0:T(8,128)S(1)}, u32[]{:S(2)}, u32[]{:S(2)}) %collective-permute-start) | collective-permute-done | bytes 368672 | tf_op jit(solution)/shard_map/ppermute | solution.py:380
  25.3 1.3 %collective-permute-start.3 = (f32[4,80,128]{2,1,0:T(8,128)S(1)}, f32[4,80,128]{2,1,0:T(8,128)S(1)}, u32[]{:S(2)}, u32[]{:S(2)}) collective-permute-start(f32[4,80,128]{2,1,0:T(8,128)S(1)} %pad_maximum_fusion.3), channel_id=1, source_target_pairs={{1,0},{2,1},{3,2},{5,4},{6,5},{7,6},{9,8},{10,9},{11,10},{13,12},{... | collective-permute-start | bytes 491528 | tf_op jit(solution)/shard_map/ppermute | solution.py:395
  26.6 4.6 %collective-permute-start.2 = (f32[4,80,128]{2,1,0:T(8,128)S(1)}, f32[4,80,128]{2,1,0:T(8,128)S(1)}, u32[]{:S(2)}, u32[]{:S(2)}) collective-permute-start(f32[4,80,128]{2,1,0:T(8,128)S(1)} %pad_maximum_fusion.2), channel_id=1, source_target_pairs={{0,1},{1,2},{2,3},{4,5},{5,6},{6,7},{8,9},{9,10},{10,11},{12,13},{... | collective-permute-start | bytes 491528 | tf_op jit(solution)/shard_map/ppermute | solution.py:395
  31.2 0.1 pad_maximum_fusion.1
  31.3 0.1 collective-permute-start.8
  31.4 1.6 %collective-permute-done.3.rest_3_ = f32[4,80,128]{2,1,0:T(8,128)S(1)} collective-permute-done((f32[4,80,128]{2,1,0:T(8,128)S(1)}, f32[4,80,128]{2,1,0:T(8,128)S(1)}, u32[]{:S(2)}, u32[]{:S(2)}) %collective-permute-start.3) | collective-permute-done | bytes 163872 | tf_op jit(solution)/shard_map/ppermute | solution.py:395
  33.0 1.2 %collective-permute-done.2.rest_2_ = f32[4,80,128]{2,1,0:T(8,128)S(1)} collective-permute-done((f32[4,80,128]{2,1,0:T(8,128)S(1)}, f32[4,80,128]{2,1,0:T(8,128)S(1)}, u32[]{:S(2)}, u32[]{:S(2)}) %collective-permute-start.2) | collective-permute-done | bytes 163872 | tf_op jit(solution)/shard_map/ppermute | solution.py:395
  34.2 0.1 pad_maximum_fusion
  34.4 0.3 pack_coupling.1.pack
  34.7 2.7 %collective-permute-start.13 = (f32[520,128]{1,0:T(8,128)S(1)}, f32[520,128]{1,0:T(8,128)S(1)}, u32[]{:S(2)}, u32[]{:S(2)}) collective-permute-start(f32[520,128]{1,0:T(8,128)S(1)} %pack_coupling.1.pack), channel_id=1, source_target_pairs={{0,24},{4,28},{8,16},{12,20},{16,8},{20,12},{24,0},{28,4},{1,25},{... | collective-permute-start | bytes 798728 | tf_op jit(solution)/shard_map/ppermute | solution.py:380
  37.4 0.5 collective-permute-start.11
  37.9 0.4 collective-permute-start.9
  38.2 2.0 %prepare.2 = (bf16[16,96,2688]{2,1,0:T(8,128)(2,1)S(1)}, f32[128,2688]{1,0:T(8,128)S(1)}) custom-call(f32[9,80,128]{2,1,0:T(8,128)S(1)} %copy-done, f32[9,80,128]{2,1,0:T(8,128)S(1)} %collective-permute-done.5.rest_1_, f32[4,80,128]{2,1,0:T(8,128)S(1)} %collective-permute-done.6.rest_2_, f32[4,80,128]{2,1,0:T(8,128)S(1)} %collective-permute-done.7.rest_3_, ...), custom_call_target="tpu_custom_call" | custom-call | tf_op jit(solution)/shard_map/prepare/pallas_call | solution.py:403
  40.3 2.0 %prepare.3 = (bf16[16,96,2688]{2,1,0:T(8,128)(2,1)S(1)}, f32[128,2688]{1,0:T(8,128)S(1)}) custom-call(f32[9,80,128]{2,1,0:T(8,128)S(1)} %collective-permute-done.rest_0_, f32[9,80,128]{2,1,0:T(8,128)S(1)} %collective-permute-done.1.rest_1_, f32[4,80,128]{2,1,0:T(8,128)S(1)} %collective-permute-done.2.rest_2_, ...), custom_call_target="tpu_custom_call", output_to_operand_aliasing={{0}: (5, {}), {1}: (6, {})} | custom-call | tf_op jit(solution)/shard_map/prepare/pallas_call | solution.py:403
  42.4 2.5 %collective-permute-done.13.pack = f32[520,128]{1,0:T(8,128)S(1)} collective-permute-done((f32[520,128]{1,0:T(8,128)S(1)}, f32[520,128]{1,0:T(8,128)S(1)}, u32[]{:S(2)}, u32[]{:S(2)}) %collective-permute-start.13) | collective-permute-done | bytes 266272 | tf_op jit(solution)/shard_map/ppermute | solution.py:380
  44.9 6.2 %apply.7 = f32[8,64,128]{2,1,0:T(8,128)S(1)} custom-call(f32[520,128]{1,0:T(8,128)S(1)} %collective-permute-done.13.pack, bf16[16,96,2688]{2,1,0:T(8,128)(2,1)S(1)} %get-tuple-element.20.sources, f32[128,2688]{1,0:T(8,128)S(1)} %get-tuple-element.21.fields), custom_call_target="tpu_custom_call" | custom-call | tf_op jit(solution)/shard_map/apply/pallas_call | solution.py:419
  51.1 2.6 %collective-permute-start.14 = (f32[8,64,128]{2,1,0:T(8,128)S(1)}, f32[8,64,128]{2,1,0:T(8,128)S(1)}, u32[]{:S(2)}, u32[]{:S(2)}) collective-permute-start(f32[8,64,128]{2,1,0:T(8,128)S(1)} %apply.7), channel_id=1, source_target_pairs={{0,24},{4,28},{8,16},{12,20},{16,8},{20,12},{24,0},{28,4},{1,25},{... | collective-permute-start | bytes 786440 | tf_op jit(solution)/shard_map/ppermute | solution.py:380
  53.8 6.0 %apply.6 = f32[8,64,128]{2,1,0:T(8,128)S(1)} custom-call(f32[520,128]{1,0:T(8,128)S(1)} %collective-permute-done.11.pack, bf16[16,96,2688]{2,1,0:T(8,128)(2,1)S(1)} %get-tuple-element.20.sources, f32[128,2688]{1,0:T(8,128)S(1)} %get-tuple-element.21.fields), custom_call_target="tpu_custom_call" | custom-call | tf_op jit(solution)/shard_map/apply/pallas_call | solution.py:419
  59.8 0.6 collective-permute-start.12
  60.4 6.1 %apply.5 = f32[8,64,128]{2,1,0:T(8,128)S(1)} custom-call(f32[520,128]{1,0:T(8,128)S(1)} %collective-permute-done.9.pack, bf16[16,96,2688]{2,1,0:T(8,128)(2,1)S(1)} %get-tuple-element.20.sources, f32[128,2688]{1,0:T(8,128)S(1)} %get-tuple-element.21.fields), custom_call_target="tpu_custom_call" | custom-call | tf_op jit(solution)/shard_map/apply/pallas_call | solution.py:419
  66.5 0.5 collective-permute-start.10
  66.9 6.0 %apply.4.rest_0_ = f32[8,64,128]{2,1,0:T(8,128)S(1)} custom-call(f32[520,128]{1,0:T(8,128)S(1)} %pack_coupling.1.pack, bf16[16,96,2688]{2,1,0:T(8,128)(2,1)S(1)} %get-tuple-element.20.sources, f32[128,2688]{1,0:T(8,128)S(1)} %get-tuple-element.21.fields), custom_call_target="tpu_custom_call" | custom-call | tf_op jit(solution)/shard_map/apply/pallas_call | solution.py:419
  73.0 0.5 collective-permute-done.10.rest_1_
  73.5 3.0 %unpack.1 = f32[2048,128]{1,0:T(8,128)} custom-call(f32[8,64,128]{2,1,0:T(8,128)S(1)} %apply.4.rest_0_, f32[8,64,128]{2,1,0:T(8,128)S(1)} %collective-permute-done.10.rest_1_, f32[8,64,128]{2,1,0:T(8,128)S(1)} %collective-permute-done.12.rest_2_, f32[8,64,128]{2,1,0:T(8,128)S(1)} %collective-permute-done.14.rest_3_), custom_call_target="tpu_custom_call" | custom-call | tf_op jit(solution)/shard_map/unpack/pallas_call | solution.py:435
  (25 shorter events, 0.2 us)
Async XLA Ops:
  4.3 13.6 %collective-permute-start.5 = (f32[9,80,128]{2,1,0:T(8,128)}, f32[9,80,128]{2,1,0:T(8,128)S(1)}, u32[]{:S(2)}, u32[]{:S(2)}) collective-permute-start(f32[9,80,128]{2,1,0:T(8,128)} %get-tuple-element.17), channel_id=1, source_target_pairs={{0,24},{4,28},{8,16},{12,20},{16,8},{20,12},{24,0},{28,4},{1,25},{... | collective-permute-start | bytes 1105928 | tf_op jit(solution)/shard_map/ppermute | solution.py:380
  8.2 17.0 %collective-permute-start = (f32[9,80,128]{2,1,0:T(8,128)}, f32[9,80,128]{2,1,0:T(8,128)S(1)}, u32[]{:S(2)}, u32[]{:S(2)}) collective-permute-start(f32[9,80,128]{2,1,0:T(8,128)} %get-tuple-element.14), channel_id=1, source_target_pairs={{0,8},{4,12},{8,0},{12,4},{16,24},{20,28},{24,16},{28,20},{1,9},{5... | collective-permute-start | bytes 1105928 | tf_op jit(solution)/shard_map/ppermute | solution.py:380
  8.8 16.5 %collective-permute-start.1 = (f32[9,80,128]{2,1,0:T(8,128)}, f32[9,80,128]{2,1,0:T(8,128)S(1)}, u32[]{:S(2)}, u32[]{:S(2)}) collective-permute-start(f32[9,80,128]{2,1,0:T(8,128)} %get-tuple-element.15), channel_id=1, source_target_pairs={{0,16},{4,20},{8,24},{12,28},{16,0},{20,4},{24,8},{28,12},{1,17},{... | collective-permute-start | bytes 1105928 | tf_op jit(solution)/shard_map/ppermute | solution.py:380
  17.9 13.3 %copy-start = (f32[9,80,128]{2,1,0:T(8,128)S(1)}, f32[9,80,128]{2,1,0:T(8,128)}, u32[]{:S(2)}) copy-start(f32[9,80,128]{2,1,0:T(8,128)} %get-tuple-element.16.rest_0_) | copy-start | bytes 1105924
  18.0 13.2 %collective-permute-start.6 = (f32[4,80,128]{2,1,0:T(8,128)S(1)}, f32[4,80,128]{2,1,0:T(8,128)S(1)}, u32[]{:S(2)}, u32[]{:S(2)}) collective-permute-start(f32[4,80,128]{2,1,0:T(8,128)S(1)} %pad_maximum_fusion.4), channel_id=1, source_target_pairs={{0,1},{1,2},{2,3},{4,5},{5,6},{6,7},{8,9},{9,10},{10,11},{12,13},{... | collective-permute-start | bytes 491528 | tf_op jit(solution)/shard_map/ppermute | solution.py:395
  22.1 9.1 %collective-permute-start.7 = (f32[4,80,128]{2,1,0:T(8,128)S(1)}, f32[4,80,128]{2,1,0:T(8,128)S(1)}, u32[]{:S(2)}, u32[]{:S(2)}) collective-permute-start(f32[4,80,128]{2,1,0:T(8,128)S(1)} %pad_maximum_fusion.5), channel_id=1, source_target_pairs={{1,0},{2,1},{3,2},{5,4},{6,5},{7,6},{9,8},{10,9},{11,10},{13,12},{... | collective-permute-start | bytes 491528 | tf_op jit(solution)/shard_map/ppermute | solution.py:395
  25.3 7.7 %collective-permute-start.3 = (f32[4,80,128]{2,1,0:T(8,128)S(1)}, f32[4,80,128]{2,1,0:T(8,128)S(1)}, u32[]{:S(2)}, u32[]{:S(2)}) collective-permute-start(f32[4,80,128]{2,1,0:T(8,128)S(1)} %pad_maximum_fusion.3), channel_id=1, source_target_pairs={{1,0},{2,1},{3,2},{5,4},{6,5},{7,6},{9,8},{10,9},{11,10},{13,12},{... | collective-permute-start | bytes 491528 | tf_op jit(solution)/shard_map/ppermute | solution.py:395
  26.6 7.6 %collective-permute-start.2 = (f32[4,80,128]{2,1,0:T(8,128)S(1)}, f32[4,80,128]{2,1,0:T(8,128)S(1)}, u32[]{:S(2)}, u32[]{:S(2)}) collective-permute-start(f32[4,80,128]{2,1,0:T(8,128)S(1)} %pad_maximum_fusion.2), channel_id=1, source_target_pairs={{0,1},{1,2},{2,3},{4,5},{5,6},{6,7},{8,9},{9,10},{10,11},{12,13},{... | collective-permute-start | bytes 491528 | tf_op jit(solution)/shard_map/ppermute | solution.py:395
  31.3 3.1 %copy-start.1 = (f32[2,32,32,32]{3,2,1,0:T(8,128)S(1)}, f32[2,32,32,32]{3,2,1,0:T(8,128)}, u32[]{:S(2)}) copy-start(f32[2,32,32,32]{3,2,1,0:T(8,128)} %coupling_ref.1) | copy-start | bytes 786436
  31.3 3.1 %copy-start.2 = (s32[2,32]{1,0:T(2,128)S(1)}, s32[2,32]{1,0:T(2,128)}, u32[]{:S(2)}) copy-start(s32[2,32]{1,0:T(2,128)} %source_ref.1) | copy-start | bytes 772
  31.3 3.1 %copy-start.3 = (s32[2,32]{1,0:T(2,128)S(1)}, s32[2,32]{1,0:T(2,128)}, u32[]{:S(2)}) copy-start(s32[2,32]{1,0:T(2,128)} %expansion_ref.1) | copy-start | bytes 772
  31.3 6.9 %collective-permute-start.8 = (f32[26,80,128]{2,1,0:T(8,128)S(1)}, f32[26,80,128]{2,1,0:T(8,128)S(1)}, u32[]{:S(2)}, u32[]{:S(2)}) collective-permute-start(f32[26,80,128]{2,1,0:T(8,128)S(1)} %pad_maximum_fusion.1), channel_id=1, source_target_pairs={{0,4},{4,0},{8,12},{12,8},{16,20},{20,16},{24,28},{28,24},{1,5},{5... | collective-permute-start | bytes 3194888 | tf_op jit(solution)/shard_map/ppermute | solution.py:383
  34.3 6.0 %collective-permute-start.4 = (f32[26,80,128]{2,1,0:T(8,128)S(1)}, f32[26,80,128]{2,1,0:T(8,128)S(1)}, u32[]{:S(2)}, u32[]{:S(2)}) collective-permute-start(f32[26,80,128]{2,1,0:T(8,128)S(1)} %pad_maximum_fusion), channel_id=1, source_target_pairs={{0,4},{4,0},{8,12},{12,8},{16,20},{20,16},{24,28},{28,24},{1,5},{5... | collective-permute-start | bytes 3194888 | tf_op jit(solution)/shard_map/ppermute | solution.py:383
  34.7 10.2 %collective-permute-start.13 = (f32[520,128]{1,0:T(8,128)S(1)}, f32[520,128]{1,0:T(8,128)S(1)}, u32[]{:S(2)}, u32[]{:S(2)}) collective-permute-start(f32[520,128]{1,0:T(8,128)S(1)} %pack_coupling.1.pack), channel_id=1, source_target_pairs={{0,24},{4,28},{8,16},{12,20},{16,8},{20,12},{24,0},{28,4},{1,25},{... | collective-permute-start | bytes 798728 | tf_op jit(solution)/shard_map/ppermute | solution.py:380
  37.4 16.4 %collective-permute-start.11 = (f32[520,128]{1,0:T(8,128)S(1)}, f32[520,128]{1,0:T(8,128)S(1)}, u32[]{:S(2)}, u32[]{:S(2)}) collective-permute-start(f32[520,128]{1,0:T(8,128)S(1)} %pack_coupling.1.pack), channel_id=1, source_target_pairs={{0,16},{4,20},{8,24},{12,28},{16,0},{20,4},{24,8},{28,12},{1,17},{... | collective-permute-start | bytes 798728 | tf_op jit(solution)/shard_map/ppermute | solution.py:380
  37.9 22.5 %collective-permute-start.9 = (f32[520,128]{1,0:T(8,128)S(1)}, f32[520,128]{1,0:T(8,128)S(1)}, u32[]{:S(2)}, u32[]{:S(2)}) collective-permute-start(f32[520,128]{1,0:T(8,128)S(1)} %pack_coupling.1.pack), channel_id=1, source_target_pairs={{0,8},{4,12},{8,0},{12,4},{16,24},{20,28},{24,16},{28,20},{1,9},{5... | collective-permute-start | bytes 798728 | tf_op jit(solution)/shard_map/ppermute | solution.py:380
  51.1 21.8 %collective-permute-start.14 = (f32[8,64,128]{2,1,0:T(8,128)S(1)}, f32[8,64,128]{2,1,0:T(8,128)S(1)}, u32[]{:S(2)}, u32[]{:S(2)}) collective-permute-start(f32[8,64,128]{2,1,0:T(8,128)S(1)} %apply.7), channel_id=1, source_target_pairs={{0,24},{4,28},{8,16},{12,20},{16,8},{20,12},{24,0},{28,4},{1,25},{... | collective-permute-start | bytes 786440 | tf_op jit(solution)/shard_map/ppermute | solution.py:380
  59.8 13.2 %collective-permute-start.12 = (f32[8,64,128]{2,1,0:T(8,128)S(1)}, f32[8,64,128]{2,1,0:T(8,128)S(1)}, u32[]{:S(2)}, u32[]{:S(2)}) collective-permute-start(f32[8,64,128]{2,1,0:T(8,128)S(1)} %apply.6), channel_id=1, source_target_pairs={{0,16},{4,20},{8,24},{12,28},{16,0},{20,4},{24,8},{28,12},{1,17},{... | collective-permute-start | bytes 786440 | tf_op jit(solution)/shard_map/ppermute | solution.py:380
  66.5 7.0 %collective-permute-start.10 = (f32[8,64,128]{2,1,0:T(8,128)S(1)}, f32[8,64,128]{2,1,0:T(8,128)S(1)}, u32[]{:S(2)}, u32[]{:S(2)}) collective-permute-start(f32[8,64,128]{2,1,0:T(8,128)S(1)} %apply.5), channel_id=1, source_target_pairs={{0,8},{4,12},{8,0},{12,4},{16,24},{20,28},{24,16},{28,20},{1,9},{5... | collective-permute-start | bytes 786440 | tf_op jit(solution)/shard_map/ppermute | solution.py:380

commit v5 on v4

--- a/solution.py
+++ b/solution.py
@@ -102,16 +102,17 @@
     blocks, slots, width, _ = coupling_ref.shape
     per = 128 // width
     groups = slots // per
-    for block in range(blocks):
-        for g in range(groups):
-            rows = slice((block * groups + g) * width, (block * groups + g + 1) * width)
-            pack[rows, :] = jnp.concatenate(
-                [coupling_ref[block, g * per + q] for q in range(per)], axis=1
-            )
-    last = blocks * groups * width
-    pack[last : last + 8, :] = jnp.zeros((8, 128), jnp.float32)
-    pack[last : last + blocks, 0:slots] = source_ref[...].astype(jnp.float32)
-    pack[last + blocks : last + 2 * blocks, 0:slots] = expansion_ref[...].astype(jnp.float32)
+    half = blocks * groups // 2
+    for n in range(blocks * groups):
+        rows = slice(n % half * width, (n % half + 1) * width)
+        block, g = n // groups, n % groups
+        pack[n // half, rows, :] = jnp.concatenate(
+            [coupling_ref[block, g * per + q] for q in range(per)], axis=1
+        )
+    last = half * width
+    pack[:, last : last + 8, :] = jnp.zeros((2, 8, 128), jnp.float32)
+    pack[0, last : last + blocks, 0:slots] = source_ref[...].astype(jnp.float32)
+    pack[0, last + blocks : last + 2 * blocks, 0:slots] = expansion_ref[...].astype(jnp.float32)
 
 
 def laplacian(tile, low, high, rim, geometry, rows):
@@ -213,7 +214,8 @@
         fields[rows, pl.ds(rim_at + 2 * halves * 128, 128)] = rim
 
 
-def apply_kernel(geometry, blocks, slots, width, pack, sources, fields, out_ref, mix, numbers, table, product, cross, sem):
+def apply_kernel(geometry, blocks, slots, width, e, *rest):
+    packs, (sources, fields, out_ref, mix, numbers, table, product, cross, sem) = rest[:-9], rest[-9:]
     layers, halves, ny, depth, chips = geometry
     tiles = layers * halves
     chunks = tiles // CHUNK
@@ -221,12 +223,21 @@
     rim_at = 2 * tiles * 128
     rims = (2 * halves + 1) * 128
     per = 128 // width
-    rows = blocks * slots // per * width
-
-    numbers[...] = pack[rows : rows + 8, :].astype(jnp.int32)
+    rows = blocks * slots // per * width // 2
+    if e:
+        core = lax.axis_index("modes") % 2
+        bits = chips.bit_length() - 1
+        reverse = sum(((e >> i) & 1) << (bits - 1 - i) for i in range(bits))
+        mine = packs[0][jnp.where(core == 0, e, reverse)]
+        other = packs[1][jnp.where(core == 0, reverse, e)]
+        first = jnp.where(core == 0, mine, other)
+        second = jnp.where(core == 0, other, mine)
+    else:
+        first, second = packs[0][0], packs[0][1]
+    numbers[...] = first[rows : rows + 8].astype(jnp.int32)
     copy = pltpu.make_async_copy(numbers, table, sem)
     copy.start()
-    value = pack[0:rows, :]
+    value = jnp.concatenate([first[:rows], second[:rows]], axis=0)
     upper, lower = halves_of(value)
     take = lax.broadcasted_iota(jnp.int32, (256, per * 128), 0)
     give = lax.broadcasted_iota(jnp.int32, (256, per * 128), 1)
@@ -286,7 +297,7 @@
                 )
         return carry
 
-    lax.fori_loop(0, blocks, one_block, 0)
+    lax.fori_loop(0, blocks, one_block, 0, unroll=True)
 
 
 def unpack_kernel(geometry, *rest):
@@ -369,7 +380,7 @@
     )
     pack = call(
         pack_coupling,
-        jax.ShapeDtypeStruct((rows + 8, 128), f32),
+        jax.ShapeDtypeStruct((2, rows // 2 + 8, 128), f32),
         3,
         [],
         UNPACK_LIMIT,
@@ -383,8 +394,6 @@
         return lax.ppermute(value, "modes", [(i, i ^ 1) for i in range(count)])
 
     bodies = [sends[0]] + [trade(sends[e], e) for e in range(1, chips)]
-    late = lax.optimization_barrier((pack, bodies[-1]))[0]
-    packs = [pack] + [trade(late, e) for e in range(1, chips)]
     n_tiles = lax.axis_size("tiles")
     up = [(i, i + 1) for i in range(n_tiles - 1)]
     down = [(i + 1, i) for i in range(n_tiles - 1)]
@@ -395,6 +404,18 @@
         low, high = lax.ppermute(top, "tiles", up), lax.ppermute(bottom, "tiles", down)
         mine = [bodies[e] for e in group] + [low, high]
         gathered.append((group, mine + [sibling(jnp.concatenate(mine))]))
+
+    bits = chips.bit_length() - 1
+    core = lax.axis_index("modes") % 2
+    keep = lax.dynamic_index_in_dim(pack, core, 0)
+    give = lax.dynamic_index_in_dim(pack, 1 - core, 0)
+    held = jnp.concatenate([keep, sibling(give)])[None]
+    for i in range(bits):
+        if i == bits - 1:
+            held = lax.optimization_barrier((held, gathered[0][1][-2]))[0]
+        pairs = [(m, m ^ (2 << (i if m % 2 == 0 else bits - 1 - i))) for m in range(count)]
+        held = jnp.concatenate([held, lax.ppermute(held, "modes", pairs)])
+    packs = [held[:, 0], sibling(held[:, 1])]
 
     ncol = 2 * tiles * 128 + (2 * halves + 1) * 128
     n_blocks = count * (local_u // width)
@@ -417,9 +438,9 @@
     parts = [None] * chips
     for e in list(range(chips - 1, -1, -1)):
         result = call(
-            functools.partial(apply_kernel, geometry, blocks, slots, width),
+            functools.partial(apply_kernel, geometry, blocks, slots, width, e),
             jax.ShapeDtypeStruct((tiles, local_u, 128), f32),
-            3,
+            4 if e else 3,
             [
                 pltpu.VMEM((rows, 128 // width * 128), jnp.bfloat16),
                 pltpu.VMEM((8, 128), jnp.int32),
@@ -430,7 +451,7 @@
             ],
             APPLY_LIMIT,
             "apply",
-        )(packs[e], sources, fields)
+        )(*(packs if e else [pack]), sources, fields)
         parts[e] = trade(result, e) if e else result
     out = pl.pallas_call(
         functools.partial(unpack_kernel, geometry),

time: 76.9 us -> 74.7 us (0.971)
  starting transfers between devices: 23.3 us -> 22.5 us
    ppermute x9 -> x6, waiting for transfers between devices: 12.9 us -> 8.38 us  [trade(): return lax.ppermute(value, 'modes', [(i, i ^ 2 * e) for i in range(count)])]
    ppermute x9 -> x6, starting transfers between devices: 11.8 us -> 8.31 us  [trade(): return lax.ppermute(value, 'modes', [(i, i ^ 2 * e) for i in range(count)])]
    ppermute x0 -> x2, waiting for transfers between devices: none -> 2.35 us  [on_device(): held = jnp.concatenate([held, lax.ppermute(held, 'modes', pairs)])]
    ppermute x0 -> x2, starting transfers between devices: none -> 2.33 us  [on_device(): held = jnp.concatenate([held, lax.ppermute(held, 'modes', pairs)])]
    ppermute x2, waiting for transfers between devices: 1.2 us -> 3.43 us  [on_device(): lax.ppermute(top, 'tiles', up)]
    ppermute x2, waiting for transfers between devices: 1.62 us -> 0.01 us  [on_device(): lax.ppermute(bottom, 'tiles', down)]
    ppermute x2 -> x4, waiting for transfers between devices: 0.01 us -> 1.32 us  [sibling(): return lax.ppermute(value, 'modes', [(i, i ^ 1) for i in range(count)])]
    slice x4, local copies, waits for them, and re-layouts: 0.97 us -> 0.05 us  [on_device(): bottom = jnp.concatenate([bodies[e][:halves] for e in group])]
  transfers between devices with their start and end apart: 15 -> 16, of which waited for: 6 -> 7; matrix products, arithmetic and copies ran while one was open for 2% -> 1% of each run, Pallas kernels for 37% -> 30%
where the time goes in v5:
time: 74.7 us; the launch traced here: 74.5 us
  Pallas kernels  35.5 us (48%)
  starting transfers between devices  22.5 us (30%)
  waiting for transfers between devices  15.5 us (21%)
    pallas_call x4, Pallas kernels, on_device(): call(functools.partial(apply_kernel, geometry, blocks, slots, width, e),...  23.7 us
    ppermute x2, starting transfers between devices, on_device(): lax.ppermute(top, 'tiles', up)  9.02 us
    ppermute x6, waiting for transfers between devices, trade(): return lax.ppermute(value, 'modes', [(i, i ^ 2 * e) for i in range(count)])  8.38 us
    ppermute x6, starting transfers between devices, trade(): return lax.ppermute(value, 'modes', [(i, i ^ 2 * e) for i in range(count)])  8.31 us
    pallas_call x1, Pallas kernels, on_device(): pl.pallas_call(functools.partial(pack_kernel, geometry), out_shape=[jax.S...  4.36 us
    pallas_call x2, Pallas kernels, on_device(): call(functools.partial(prepare_kernel, geometry, width, local_u, local_a,...  4.1 us
    ppermute x2, waiting for transfers between devices, on_device(): lax.ppermute(top, 'tiles', up)  3.43 us
    pallas_call x1, Pallas kernels, on_device(): pl.pallas_call(functools.partial(unpack_kernel, geometry), out_shape=jax....  3.01 us
  transfers between devices with their start and end apart: 16, of which 7 were waited for; matrix products, arithmetic and copies ran while one was open for 1% of the time, Pallas kernels for 30%

profile of v5, /device:TPU:0, one launch (start us, length us, event | category | flops | bytes accessed | tf_op | source)
XLA Modules:
  0.0 74.5 jit_solution(7611032853446928669)
XLA Ops:
  0.0 4.4 %pack.1 = (f32[9,80,128]{2,1,0:T(8,128)}, f32[9,80,128]{2,1,0:T(8,128)}, f32[9,80,128]{2,1,0:T(8,128)}, f32[9,80,128]{2,1,0:T(8,128)}) custom-call(f32[2048,128]{1,0:T(8,128)} %bitcast.9, f32[512,128]{1,0:T(8,128)} %bitcast.10), custom_call_target="tpu_custom_call" | custom-call | tf_op jit(solution)/shard_map/pack/pallas_call | solution.py:364
  4.4 4.0 %collective-permute-start.5 = (f32[9,80,128]{2,1,0:T(8,128)}, f32[9,80,128]{2,1,0:T(8,128)S(1)}, u32[]{:S(2)}, u32[]{:S(2)}) collective-permute-start(f32[9,80,128]{2,1,0:T(8,128)} %get-tuple-element.17), channel_id=1, source_target_pairs={{0,24},{4,28},{8,16},{12,20},{16,8},{20,12},{24,0},{28,4},{1,25},{... | collective-permute-start | bytes 1105928 | tf_op jit(solution)/shard_map/ppermute | solution.py:391
  8.4 0.5 collective-permute-start
  8.9 0.1 collective-permute-start.1
  9.0 0.3 pack_coupling.1.rest_0_
  9.4 1.3 %collective-permute-done.9 = f32[1,264,128]{2,1,0:T(8,128)S(1)} collective-permute-done((f32[1,264,128]{2,1,0:T(8,128)S(1)}, f32[1,264,128]{2,1,0:T(8,128)S(1)}, u32[]{:S(2)}, u32[]{:S(2)}) %collective-permute-start.9) | collective-permute-done | bytes 135200 | tf_op jit(solution)/shard_map/ppermute | solution.py:394
  10.8 2.0 %collective-permute-start.10 = (f32[1,2,264,128]{3,2,0,1:T(8,128)S(1)}, f32[1,2,264,128]{3,2,0,1:T(8,128)S(1)}, u32[]{:S(2)}, u32[]{:S(2)}) collective-permute-start(f32[1,2,264,128]{3,2,0,1:T(8,128)S(1)} %maximum_bitcast_fusion), channel_id=1, source_target_pairs={{0,8},{4,20},{8,0},{12,28},{16,24},{20,4},{24,16},{28,12},{1,9},{5... | collective-permute-start | bytes 811016 | tf_op jit(solution)/shard_map/ppermute | solution.py:417
  12.7 5.3 %collective-permute-done.5.rest_1_ = f32[9,80,128]{2,1,0:T(8,128)S(1)} collective-permute-done((f32[9,80,128]{2,1,0:T(8,128)}, f32[9,80,128]{2,1,0:T(8,128)S(1)}, u32[]{:S(2)}, u32[]{:S(2)}) %collective-permute-start.5) | collective-permute-done | bytes 368672 | tf_op jit(solution)/shard_map/ppermute | solution.py:391
  18.1 1.3 %collective-permute-start.7 = (f32[4,80,128]{2,1,0:T(8,128)S(1)}, f32[4,80,128]{2,1,0:T(8,128)S(1)}, u32[]{:S(2)}, u32[]{:S(2)}) collective-permute-start(f32[4,80,128]{2,1,0:T(8,128)S(1)} %pad_maximum_fusion.6), channel_id=1, source_target_pairs={{1,0},{2,1},{3,2},{5,4},{6,5},{7,6},{9,8},{10,9},{11,10},{13,12},{... | collective-permute-start | bytes 491528 | tf_op jit(solution)/shard_map/ppermute | solution.py:404
  19.4 4.6 %collective-permute-start.6 = (f32[4,80,128]{2,1,0:T(8,128)S(1)}, f32[4,80,128]{2,1,0:T(8,128)S(1)}, u32[]{:S(2)}, u32[]{:S(2)}) collective-permute-start(f32[4,80,128]{2,1,0:T(8,128)S(1)} %pad_maximum_fusion.5), channel_id=1, source_target_pairs={{0,1},{1,2},{2,3},{4,5},{5,6},{6,7},{8,9},{9,10},{10,11},{12,13},{... | collective-permute-start | bytes 491528 | tf_op jit(solution)/shard_map/ppermute | solution.py:404
  24.0 1.3 %collective-permute-done.rest_0_ = f32[9,80,128]{2,1,0:T(8,128)S(1)} collective-permute-done((f32[9,80,128]{2,1,0:T(8,128)}, f32[9,80,128]{2,1,0:T(8,128)S(1)}, u32[]{:S(2)}, u32[]{:S(2)}) %collective-permute-start) | collective-permute-done | bytes 368672 | tf_op jit(solution)/shard_map/ppermute | solution.py:391
  25.4 1.3 %collective-permute-start.3 = (f32[4,80,128]{2,1,0:T(8,128)S(1)}, f32[4,80,128]{2,1,0:T(8,128)S(1)}, u32[]{:S(2)}, u32[]{:S(2)}) collective-permute-start(f32[4,80,128]{2,1,0:T(8,128)S(1)} %pad_maximum_fusion.4), channel_id=1, source_target_pairs={{1,0},{2,1},{3,2},{5,4},{6,5},{7,6},{9,8},{10,9},{11,10},{13,12},{... | collective-permute-start | bytes 491528 | tf_op jit(solution)/shard_map/ppermute | solution.py:404
  26.7 1.5 %collective-permute-done.10 = f32[1,2,264,128]{3,2,0,1:T(8,128)S(1)} collective-permute-done((f32[1,2,264,128]{3,2,0,1:T(8,128)S(1)}, f32[1,2,264,128]{3,2,0,1:T(8,128)S(1)}, u32[]{:S(2)}, u32[]{:S(2)}) %collective-permute-start.10) | collective-permute-done | bytes 270368 | tf_op jit(solution)/shard_map/ppermute | solution.py:417
  28.3 0.4 collective-permute-start.11
  28.7 4.4 %collective-permute-start.2 = (f32[4,80,128]{2,1,0:T(8,128)S(1)}, f32[4,80,128]{2,1,0:T(8,128)S(1)}, u32[]{:S(2)}, u32[]{:S(2)}) collective-permute-start(f32[4,80,128]{2,1,0:T(8,128)S(1)} %pad_maximum_fusion.3), channel_id=1, source_target_pairs={{0,1},{1,2},{2,3},{4,5},{5,6},{6,7},{8,9},{9,10},{10,11},{12,13},{... | collective-permute-start | bytes 491528 | tf_op jit(solution)/shard_map/ppermute | solution.py:404
  33.1 0.1 pad_maximum_fusion.1
  33.2 0.1 collective-permute-start.8
  33.3 3.4 %collective-permute-done.2.rest_2_ = f32[4,80,128]{2,1,0:T(8,128)S(1)} collective-permute-done((f32[4,80,128]{2,1,0:T(8,128)S(1)}, f32[4,80,128]{2,1,0:T(8,128)S(1)}, u32[]{:S(2)}, u32[]{:S(2)}) %collective-permute-start.2) | collective-permute-done | bytes 163872 | tf_op jit(solution)/shard_map/ppermute | solution.py:404
  36.7 0.1 pad_maximum_fusion
  36.9 0.8 %collective-permute-done.11 = f32[2,2,264,128]{3,2,0,1:T(8,128)S(1)} collective-permute-done((f32[2,2,264,128]{3,2,0,1:T(8,128)S(1)}, f32[2,2,264,128]{3,2,0,1:T(8,128)S(1)}, u32[]{:S(2)}, u32[]{:S(2)}) %collective-permute-start.11) | collective-permute-done | bytes 540704 | tf_op jit(solution)/shard_map/ppermute | solution.py:417
  37.8 0.1 slice_bitcast_fusion
  37.9 2.0 %prepare.2 = (bf16[16,96,2688]{2,1,0:T(8,128)(2,1)S(1)}, f32[128,2688]{1,0:T(8,128)S(1)}) custom-call(f32[9,80,128]{2,1,0:T(8,128)S(1)} %copy-done, f32[9,80,128]{2,1,0:T(8,128)S(1)} %collective-permute-done.5.rest_1_, f32[4,80,128]{2,1,0:T(8,128)S(1)} %collective-permute-done.6.rest_2_, f32[4,80,128]{2,1,0:T(8,128)S(1)} %collective-permute-done.7.rest_3_, ...), custom_call_target="tpu_custom_call" | custom-call | tf_op jit(solution)/shard_map/prepare/pallas_call | solution.py:424
  40.0 2.0 %prepare.3 = (bf16[16,96,2688]{2,1,0:T(8,128)(2,1)S(1)}, f32[128,2688]{1,0:T(8,128)S(1)}) custom-call(f32[9,80,128]{2,1,0:T(8,128)S(1)} %collective-permute-done.rest_0_, f32[9,80,128]{2,1,0:T(8,128)S(1)} %collective-permute-done.1.rest_1_, f32[4,80,128]{2,1,0:T(8,128)S(1)} %collective-permute-done.2.rest_2_, ...), custom_call_target="tpu_custom_call", output_to_operand_aliasing={{0}: (5, {}), {1}: (6, {})} | custom-call | tf_op jit(solution)/shard_map/prepare/pallas_call | solution.py:424
  42.1 5.9 %apply.7 = f32[8,64,128]{2,1,0:T(8,128)S(1)} custom-call(f32[4,264,128]{2,1,0:T(8,128)S(1)} %get-tuple-element.24.rest_0_, f32[4,264,128]{2,1,0:T(8,128)S(1)} %collective-permute-done.12.rest_1_, bf16[16,96,2688]{2,1,0:T(8,128)(2,1)S(1)} %get-tuple-element.20.rest_1_.rest_2_, f32[128,2688]{1,0:T(8,128)S(1)} %get-tuple-element.21.rest_2_.rest_3_), custom_call_target="tpu_custom_call" | custom-call | tf_op jit(solution)/shard_map/apply/pallas_call | solution.py:440
  48.0 1.5 %collective-permute-start.15 = (f32[8,64,128]{2,1,0:T(8,128)S(1)}, f32[8,64,128]{2,1,0:T(8,128)S(1)}, u32[]{:S(2)}, u32[]{:S(2)}) collective-permute-start(f32[8,64,128]{2,1,0:T(8,128)S(1)} %apply.7), channel_id=1, source_target_pairs={{0,24},{4,28},{8,16},{12,20},{16,8},{20,12},{24,0},{28,4},{1,25},{... | collective-permute-start | bytes 786440 | tf_op jit(solution)/shard_map/ppermute | solution.py:391
  49.4 6.1 %apply.6 = f32[8,64,128]{2,1,0:T(8,128)S(1)} custom-call(f32[4,264,128]{2,1,0:T(8,128)S(1)} %get-tuple-element.24.rest_0_, f32[4,264,128]{2,1,0:T(8,128)S(1)} %collective-permute-done.12.rest_1_, bf16[16,96,2688]{2,1,0:T(8,128)(2,1)S(1)} %get-tuple-element.20.rest_1_.rest_2_, f32[128,2688]{1,0:T(8,128)S(1)} %get-tuple-element.21.rest_2_.rest_3_), custom_call_target="tpu_custom_call" | custom-call | tf_op jit(solution)/shard_map/apply/pallas_call | solution.py:440
  55.5 1.6 %collective-permute-start.14 = (f32[8,64,128]{2,1,0:T(8,128)S(1)}, f32[8,64,128]{2,1,0:T(8,128)S(1)}, u32[]{:S(2)}, u32[]{:S(2)}) collective-permute-start(f32[8,64,128]{2,1,0:T(8,128)S(1)} %apply.6), channel_id=1, source_target_pairs={{0,16},{4,20},{8,24},{12,28},{16,0},{20,4},{24,8},{28,12},{1,17},{... | collective-permute-start | bytes 786440 | tf_op jit(solution)/shard_map/ppermute | solution.py:391
  57.1 5.9 %apply.5 = f32[8,64,128]{2,1,0:T(8,128)S(1)} custom-call(f32[4,264,128]{2,1,0:T(8,128)S(1)} %get-tuple-element.24.rest_0_, f32[4,264,128]{2,1,0:T(8,128)S(1)} %collective-permute-done.12.rest_1_, bf16[16,96,2688]{2,1,0:T(8,128)(2,1)S(1)} %get-tuple-element.20.rest_1_.rest_2_, f32[128,2688]{1,0:T(8,128)S(1)} %get-tuple-element.21.rest_2_.rest_3_), custom_call_target="tpu_custom_call" | custom-call | tf_op jit(solution)/shard_map/apply/pallas_call | solution.py:440
  63.0 0.6 collective-permute-start.13
  63.6 5.9 %apply.4.rest_0_ = f32[8,64,128]{2,1,0:T(8,128)S(1)} custom-call(f32[2,264,128]{2,1,0:T(8,128)S(1)} %pack_coupling.1.rest_0_, bf16[16,96,2688]{2,1,0:T(8,128)(2,1)S(1)} %get-tuple-element.20.rest_1_.rest_2_, f32[128,2688]{1,0:T(8,128)S(1)} %get-tuple-element.21.rest_2_.rest_3_), custom_call_target="tpu_custom_call" | custom-call | tf_op jit(solution)/shard_map/apply/pallas_call | solution.py:440
  69.5 1.7 %collective-permute-done.13.rest_1_ = f32[8,64,128]{2,1,0:T(8,128)S(1)} collective-permute-done((f32[8,64,128]{2,1,0:T(8,128)S(1)}, f32[8,64,128]{2,1,0:T(8,128)S(1)}, u32[]{:S(2)}, u32[]{:S(2)}) %collective-permute-start.13) | collective-permute-done | bytes 262176 | tf_op jit(solution)/shard_map/ppermute | solution.py:391
  71.3 3.0 %unpack.1 = f32[2048,128]{1,0:T(8,128)} custom-call(f32[8,64,128]{2,1,0:T(8,128)S(1)} %apply.4.rest_0_, f32[8,64,128]{2,1,0:T(8,128)S(1)} %collective-permute-done.13.rest_1_, f32[8,64,128]{2,1,0:T(8,128)S(1)} %collective-permute-done.14.rest_2_, f32[8,64,128]{2,1,0:T(8,128)S(1)} %collective-permute-done.15.rest_3_), custom_call_target="tpu_custom_call" | custom-call | tf_op jit(solution)/shard_map/unpack/pallas_call | solution.py:456
  (33 shorter events, 0.5 us)
Async XLA Ops:
  0.0 9.0 %copy-start.1 = (f32[2,32,32,32]{3,2,1,0:T(8,128)S(1)}, f32[2,32,32,32]{3,2,1,0:T(8,128)}, u32[]{:S(2)}) copy-start(f32[2,32,32,32]{3,2,1,0:T(8,128)} %coupling_ref.1) | copy-start | bytes 786436
  0.0 9.0 %copy-start.2 = (s32[2,32]{1,0:T(2,128)S(1)}, s32[2,32]{1,0:T(2,128)}, u32[]{:S(2)}) copy-start(s32[2,32]{1,0:T(2,128)} %source_ref.1) | copy-start | bytes 772
  0.0 9.0 %copy-start.3 = (s32[2,32]{1,0:T(2,128)S(1)}, s32[2,32]{1,0:T(2,128)}, u32[]{:S(2)}) copy-start(s32[2,32]{1,0:T(2,128)} %expansion_ref.1) | copy-start | bytes 772
  4.4 5.0 %copy-start = (f32[9,80,128]{2,1,0:T(8,128)S(1)}, f32[9,80,128]{2,1,0:T(8,128)}, u32[]{:S(2)}) copy-start(f32[9,80,128]{2,1,0:T(8,128)} %get-tuple-element.16.rest_0_) | copy-start | bytes 1105924
  4.4 13.6 %collective-permute-start.5 = (f32[9,80,128]{2,1,0:T(8,128)}, f32[9,80,128]{2,1,0:T(8,128)S(1)}, u32[]{:S(2)}, u32[]{:S(2)}) collective-permute-start(f32[9,80,128]{2,1,0:T(8,128)} %get-tuple-element.17), channel_id=1, source_target_pairs={{0,24},{4,28},{8,16},{12,20},{16,8},{20,12},{24,0},{28,4},{1,25},{... | collective-permute-start | bytes 1105928 | tf_op jit(solution)/shard_map/ppermute | solution.py:391
  8.4 17.0 %collective-permute-start = (f32[9,80,128]{2,1,0:T(8,128)}, f32[9,80,128]{2,1,0:T(8,128)S(1)}, u32[]{:S(2)}, u32[]{:S(2)}) collective-permute-start(f32[9,80,128]{2,1,0:T(8,128)} %get-tuple-element.14), channel_id=1, source_target_pairs={{0,8},{4,12},{8,0},{12,4},{16,24},{20,28},{24,16},{28,20},{1,9},{5... | collective-permute-start | bytes 1105928 | tf_op jit(solution)/shard_map/ppermute | solution.py:391
  8.9 16.5 %collective-permute-start.1 = (f32[9,80,128]{2,1,0:T(8,128)}, f32[9,80,128]{2,1,0:T(8,128)S(1)}, u32[]{:S(2)}, u32[]{:S(2)}) collective-permute-start(f32[9,80,128]{2,1,0:T(8,128)} %get-tuple-element.15), channel_id=1, source_target_pairs={{0,16},{4,20},{8,24},{12,28},{16,0},{20,4},{24,8},{28,12},{1,17},{... | collective-permute-start | bytes 1105928 | tf_op jit(solution)/shard_map/ppermute | solution.py:391
  9.3 1.4 %collective-permute-start.9 = (f32[1,264,128]{2,1,0:T(8,128)S(1)}, f32[1,264,128]{2,1,0:T(8,128)S(1)}, u32[]{:S(2)}, u32[]{:S(2)}) collective-permute-start(f32[1,264,128]{2,1,0:T(8,128)S(1)} %get-tuple-element.34), channel_id=1, source_target_pairs={{0,4},{4,0},{8,12},{12,8},{16,20},{20,16},{24,28},{28,24},{1,5},{5... | collective-permute-start | bytes 405512 | tf_op jit(solution)/shard_map/ppermute | solution.py:394
  10.8 17.5 %collective-permute-start.10 = (f32[1,2,264,128]{3,2,0,1:T(8,128)S(1)}, f32[1,2,264,128]{3,2,0,1:T(8,128)S(1)}, u32[]{:S(2)}, u32[]{:S(2)}) collective-permute-start(f32[1,2,264,128]{3,2,0,1:T(8,128)S(1)} %maximum_bitcast_fusion), channel_id=1, source_target_pairs={{0,8},{4,20},{8,0},{12,28},{16,24},{20,4},{24,16},{28,12},{1,9},{5... | collective-permute-start | bytes 811016 | tf_op jit(solution)/shard_map/ppermute | solution.py:417
  18.1 10.2 %collective-permute-start.7 = (f32[4,80,128]{2,1,0:T(8,128)S(1)}, f32[4,80,128]{2,1,0:T(8,128)S(1)}, u32[]{:S(2)}, u32[]{:S(2)}) collective-permute-start(f32[4,80,128]{2,1,0:T(8,128)S(1)} %pad_maximum_fusion.6), channel_id=1, source_target_pairs={{1,0},{2,1},{3,2},{5,4},{6,5},{7,6},{9,8},{10,9},{11,10},{13,12},{... | collective-permute-start | bytes 491528 | tf_op jit(solution)/shard_map/ppermute | solution.py:404
  19.4 13.7 %collective-permute-start.6 = (f32[4,80,128]{2,1,0:T(8,128)S(1)}, f32[4,80,128]{2,1,0:T(8,128)S(1)}, u32[]{:S(2)}, u32[]{:S(2)}) collective-permute-start(f32[4,80,128]{2,1,0:T(8,128)S(1)} %pad_maximum_fusion.5), channel_id=1, source_target_pairs={{0,1},{1,2},{2,3},{4,5},{5,6},{6,7},{8,9},{9,10},{10,11},{12,13},{... | collective-permute-start | bytes 491528 | tf_op jit(solution)/shard_map/ppermute | solution.py:404
  25.4 7.8 %collective-permute-start.3 = (f32[4,80,128]{2,1,0:T(8,128)S(1)}, f32[4,80,128]{2,1,0:T(8,128)S(1)}, u32[]{:S(2)}, u32[]{:S(2)}) collective-permute-start(f32[4,80,128]{2,1,0:T(8,128)S(1)} %pad_maximum_fusion.4), channel_id=1, source_target_pairs={{1,0},{2,1},{3,2},{5,4},{6,5},{7,6},{9,8},{10,9},{11,10},{13,12},{... | collective-permute-start | bytes 491528 | tf_op jit(solution)/shard_map/ppermute | solution.py:404
  28.3 9.4 %collective-permute-start.11 = (f32[2,2,264,128]{3,2,0,1:T(8,128)S(1)}, f32[2,2,264,128]{3,2,0,1:T(8,128)S(1)}, u32[]{:S(2)}, u32[]{:S(2)}) collective-permute-start(f32[2,2,264,128]{3,2,0,1:T(8,128)S(1)} %pad_maximum_fusion.2), channel_id=1, source_target_pairs={{0,16},{4,12},{8,24},{12,4},{16,0},{20,28},{24,8},{28,20},{1,17},{... | collective-permute-start | bytes 1622024 | tf_op jit(solution)/shard_map/ppermute | solution.py:417
  28.7 8.0 %collective-permute-start.2 = (f32[4,80,128]{2,1,0:T(8,128)S(1)}, f32[4,80,128]{2,1,0:T(8,128)S(1)}, u32[]{:S(2)}, u32[]{:S(2)}) collective-permute-start(f32[4,80,128]{2,1,0:T(8,128)S(1)} %pad_maximum_fusion.3), channel_id=1, source_target_pairs={{0,1},{1,2},{2,3},{4,5},{5,6},{6,7},{8,9},{9,10},{10,11},{12,13},{... | collective-permute-start | bytes 491528 | tf_op jit(solution)/shard_map/ppermute | solution.py:404
  33.2 4.7 %collective-permute-start.8 = (f32[26,80,128]{2,1,0:T(8,128)S(1)}, f32[26,80,128]{2,1,0:T(8,128)S(1)}, u32[]{:S(2)}, u32[]{:S(2)}) collective-permute-start(f32[26,80,128]{2,1,0:T(8,128)S(1)} %pad_maximum_fusion.1), channel_id=1, source_target_pairs={{0,4},{4,0},{8,12},{12,8},{16,20},{20,16},{24,28},{28,24},{1,5},{5... | collective-permute-start | bytes 3194888 | tf_op jit(solution)/shard_map/ppermute | solution.py:394
  36.8 3.2 %collective-permute-start.4 = (f32[26,80,128]{2,1,0:T(8,128)S(1)}, f32[26,80,128]{2,1,0:T(8,128)S(1)}, u32[]{:S(2)}, u32[]{:S(2)}) collective-permute-start(f32[26,80,128]{2,1,0:T(8,128)S(1)} %pad_maximum_fusion), channel_id=1, source_target_pairs={{0,4},{4,0},{8,12},{12,8},{16,20},{20,16},{24,28},{28,24},{1,5},{5... | collective-permute-start | bytes 3194888 | tf_op jit(solution)/shard_map/ppermute | solution.py:394
  37.8 4.2 %collective-permute-start.12 = (f32[4,264,128]{2,1,0:T(8,128)S(1)}, f32[4,264,128]{2,1,0:T(8,128)S(1)}, u32[]{:S(2)}, u32[]{:S(2)}) collective-permute-start(f32[4,264,128]{2,1,0:T(8,128)S(1)} %get-tuple-element.23), channel_id=1, source_target_pairs={{0,4},{4,0},{8,12},{12,8},{16,20},{20,16},{24,28},{28,24},{1,5},{5... | collective-permute-start | bytes 1622024 | tf_op jit(solution)/shard_map/ppermute | solution.py:394
  48.0 21.6 %collective-permute-start.15 = (f32[8,64,128]{2,1,0:T(8,128)S(1)}, f32[8,64,128]{2,1,0:T(8,128)S(1)}, u32[]{:S(2)}, u32[]{:S(2)}) collective-permute-start(f32[8,64,128]{2,1,0:T(8,128)S(1)} %apply.7), channel_id=1, source_target_pairs={{0,24},{4,28},{8,16},{12,20},{16,8},{20,12},{24,0},{28,4},{1,25},{... | collective-permute-start | bytes 786440 | tf_op jit(solution)/shard_map/ppermute | solution.py:391
  55.5 14.0 %collective-permute-start.14 = (f32[8,64,128]{2,1,0:T(8,128)S(1)}, f32[8,64,128]{2,1,0:T(8,128)S(1)}, u32[]{:S(2)}, u32[]{:S(2)}) collective-permute-start(f32[8,64,128]{2,1,0:T(8,128)S(1)} %apply.6), channel_id=1, source_target_pairs={{0,16},{4,20},{8,24},{12,28},{16,0},{20,4},{24,8},{28,12},{1,17},{... | collective-permute-start | bytes 786440 | tf_op jit(solution)/shard_map/ppermute | solution.py:391
  63.0 8.3 %collective-permute-start.13 = (f32[8,64,128]{2,1,0:T(8,128)S(1)}, f32[8,64,128]{2,1,0:T(8,128)S(1)}, u32[]{:S(2)}, u32[]{:S(2)}) collective-permute-start(f32[8,64,128]{2,1,0:T(8,128)S(1)} %apply.5), channel_id=1, source_target_pairs={{0,8},{4,12},{8,0},{12,4},{16,24},{20,28},{24,16},{28,20},{1,9},{5... | collective-permute-start | bytes 786440 | tf_op jit(solution)/shard_map/ppermute | solution.py:391

commit v6 on v5

--- a/solution.py
+++ b/solution.py
@@ -98,7 +98,7 @@
         copy.wait()
 
 
-def pack_coupling(coupling_ref, source_ref, expansion_ref, pack):
+def pack_coupling(coupling_ref, source_ref, expansion_ref, pack, select):
     blocks, slots, width, _ = coupling_ref.shape
     per = 128 // width
     groups = slots // per
@@ -113,6 +113,11 @@
     pack[:, last : last + 8, :] = jnp.zeros((2, 8, 128), jnp.float32)
     pack[0, last : last + blocks, 0:slots] = source_ref[...].astype(jnp.float32)
     pack[0, last + blocks : last + 2 * blocks, 0:slots] = expansion_ref[...].astype(jnp.float32)
+    take = lax.broadcasted_iota(jnp.int32, (256, per * 128), 0)
+    give = lax.broadcasted_iota(jnp.int32, (256, per * 128), 1)
+    lane = give % 128
+    wanted = (give // 128) * width + lane % width + jnp.where(lane >= 2 * width, 128, 0)
+    select[...] = jnp.where((take == wanted) & (lane < 3 * width), 1.0, 0.0).astype(jnp.bfloat16)
 
 
 def laplacian(tile, low, high, rim, geometry, rows):
@@ -215,7 +220,7 @@
 
 
 def apply_kernel(geometry, blocks, slots, width, e, *rest):
-    packs, (sources, fields, out_ref, mix, numbers, table, product, cross, sem) = rest[:-9], rest[-9:]
+    packs, (chosen, sources, fields, out_ref, mix, numbers, table, product, cross, sem) = rest[:-10], rest[-10:]
     layers, halves, ny, depth, chips = geometry
     tiles = layers * halves
     chunks = tiles // CHUNK
@@ -239,13 +244,8 @@
     copy.start()
     value = jnp.concatenate([first[:rows], second[:rows]], axis=0)
     upper, lower = halves_of(value)
-    take = lax.broadcasted_iota(jnp.int32, (256, per * 128), 0)
-    give = lax.broadcasted_iota(jnp.int32, (256, per * 128), 1)
-    lane = give % 128
-    wanted = (give // 128) * width + lane % width + jnp.where(lane >= 2 * width, 128, 0)
-    chosen = jnp.where((take == wanted) & (lane < 3 * width), 1.0, 0.0).astype(jnp.bfloat16)
     mix[...] = jnp.dot(
-        jnp.concatenate([upper, lower], axis=1), chosen, preferred_element_type=jnp.float32
+        jnp.concatenate([upper, lower], axis=1), chosen[...], preferred_element_type=jnp.float32
     ).astype(jnp.bfloat16)
     copy.wait()
 
@@ -378,9 +378,12 @@
         solution_modes.reshape(-1, nz),
         coefficient_modes.reshape(-1, nz),
     )
-    pack = call(
+    pack, select = call(
         pack_coupling,
-        jax.ShapeDtypeStruct((2, rows // 2 + 8, 128), f32),
+        [
+            jax.ShapeDtypeStruct((2, rows // 2 + 8, 128), f32),
+            jax.ShapeDtypeStruct((256, 128 // width * 128), jnp.bfloat16),
+        ],
         3,
         [],
         UNPACK_LIMIT,
@@ -440,7 +443,7 @@
         result = call(
             functools.partial(apply_kernel, geometry, blocks, slots, width, e),
             jax.ShapeDtypeStruct((tiles, local_u, 128), f32),
-            4 if e else 3,
+            5 if e else 4,
             [
                 pltpu.VMEM((rows, 128 // width * 128), jnp.bfloat16),
                 pltpu.VMEM((8, 128), jnp.int32),
@@ -451,7 +454,7 @@
             ],
             APPLY_LIMIT,
             "apply",
-        )(*(packs if e else [pack]), sources, fields)
+        )(*(packs if e else [pack]), select, sources, fields)
         parts[e] = trade(result, e) if e else result
     out = pl.pallas_call(
         functools.partial(unpack_kernel, geometry),

time: 74.7 us -> 74.6 us (level)
  no operation moved by 1% of the time
where the time goes in v6:
time: 74.6 us; the launch traced here: 74.5 us
  Pallas kernels  35.7 us (48%)
  starting transfers between devices  22.5 us (30%)
  waiting for transfers between devices  15.3 us (21%)
    pallas_call x4, Pallas kernels, on_device(): call(functools.partial(apply_kernel, geometry, blocks, slots, width, e),...  23.8 us
    ppermute x2, starting transfers between devices, on_device(): lax.ppermute(top, 'tiles', up)  9.02 us
    ppermute x6, starting transfers between devices, trade(): return lax.ppermute(value, 'modes', [(i, i ^ 2 * e) for i in range(count)])  8.28 us
    ppermute x6, waiting for transfers between devices, trade(): return lax.ppermute(value, 'modes', [(i, i ^ 2 * e) for i in range(count)])  8.2 us
    pallas_call x1, Pallas kernels, on_device(): pl.pallas_call(functools.partial(pack_kernel, geometry), out_shape=[jax.S...  4.38 us
    pallas_call x2, Pallas kernels, on_device(): call(functools.partial(prepare_kernel, geometry, width, local_u, local_a,...  4.1 us
    ppermute x2, waiting for transfers between devices, on_device(): lax.ppermute(top, 'tiles', up)  3.43 us
    pallas_call x1, Pallas kernels, on_device(): pl.pallas_call(functools.partial(unpack_kernel, geometry), out_shape=jax....  3.01 us
  transfers between devices with their start and end apart: 16, of which 7 were waited for; matrix products, arithmetic and copies ran while one was open for 1% of the time, Pallas kernels for 30%

profile of v6, /device:TPU:0, one launch (start us, length us, event | category | flops | bytes accessed | tf_op | source)
XLA Modules:
  0.0 74.5 jit_solution(6584501257333238983)
XLA Ops:
  0.0 4.4 %pack.1 = (f32[9,80,128]{2,1,0:T(8,128)}, f32[9,80,128]{2,1,0:T(8,128)}, f32[9,80,128]{2,1,0:T(8,128)}, f32[9,80,128]{2,1,0:T(8,128)}) custom-call(f32[2048,128]{1,0:T(8,128)} %bitcast.9, f32[512,128]{1,0:T(8,128)} %bitcast.10), custom_call_target="tpu_custom_call" | custom-call | tf_op jit(solution)/shard_map/pack/pallas_call | solution.py:364
  4.4 4.0 %collective-permute-start.5 = (f32[9,80,128]{2,1,0:T(8,128)}, f32[9,80,128]{2,1,0:T(8,128)S(1)}, u32[]{:S(2)}, u32[]{:S(2)}) collective-permute-start(f32[9,80,128]{2,1,0:T(8,128)} %get-tuple-element.21), channel_id=1, source_target_pairs={{0,24},{4,28},{8,16},{12,20},{16,8},{20,12},{24,0},{28,4},{1,25},{... | collective-permute-start | bytes 1105928 | tf_op jit(solution)/shard_map/ppermute | solution.py:394
  8.4 0.5 collective-permute-start
  8.9 0.1 collective-permute-start.1
  9.0 0.3 pack_coupling.1
  9.5 1.3 %collective-permute-done.9 = f32[1,264,128]{2,1,0:T(8,128)S(1)} collective-permute-done((f32[1,264,128]{2,1,0:T(8,128)S(1)}, f32[1,264,128]{2,1,0:T(8,128)S(1)}, u32[]{:S(2)}, u32[]{:S(2)}) %collective-permute-start.9) | collective-permute-done | bytes 135200 | tf_op jit(solution)/shard_map/ppermute | solution.py:397
  10.8 2.0 %collective-permute-start.10 = (f32[1,2,264,128]{3,2,0,1:T(8,128)S(1)}, f32[1,2,264,128]{3,2,0,1:T(8,128)S(1)}, u32[]{:S(2)}, u32[]{:S(2)}) collective-permute-start(f32[1,2,264,128]{3,2,0,1:T(8,128)S(1)} %maximum_bitcast_fusion), channel_id=1, source_target_pairs={{0,8},{4,20},{8,0},{12,28},{16,24},{20,4},{24,16},{28,12},{1,9},{5... | collective-permute-start | bytes 811016 | tf_op jit(solution)/shard_map/ppermute | solution.py:420
  12.8 5.2 %collective-permute-done.5.rest_1_ = f32[9,80,128]{2,1,0:T(8,128)S(1)} collective-permute-done((f32[9,80,128]{2,1,0:T(8,128)}, f32[9,80,128]{2,1,0:T(8,128)S(1)}, u32[]{:S(2)}, u32[]{:S(2)}) %collective-permute-start.5) | collective-permute-done | bytes 368672 | tf_op jit(solution)/shard_map/ppermute | solution.py:394
  18.1 1.3 %collective-permute-start.7 = (f32[4,80,128]{2,1,0:T(8,128)S(1)}, f32[4,80,128]{2,1,0:T(8,128)S(1)}, u32[]{:S(2)}, u32[]{:S(2)}) collective-permute-start(f32[4,80,128]{2,1,0:T(8,128)S(1)} %pad_maximum_fusion.6), channel_id=1, source_target_pairs={{1,0},{2,1},{3,2},{5,4},{6,5},{7,6},{9,8},{10,9},{11,10},{13,12},{... | collective-permute-start | bytes 491528 | tf_op jit(solution)/shard_map/ppermute | solution.py:407
  19.4 4.6 %collective-permute-start.6 = (f32[4,80,128]{2,1,0:T(8,128)S(1)}, f32[4,80,128]{2,1,0:T(8,128)S(1)}, u32[]{:S(2)}, u32[]{:S(2)}) collective-permute-start(f32[4,80,128]{2,1,0:T(8,128)S(1)} %pad_maximum_fusion.5), channel_id=1, source_target_pairs={{0,1},{1,2},{2,3},{4,5},{5,6},{6,7},{8,9},{9,10},{10,11},{12,13},{... | collective-permute-start | bytes 491528 | tf_op jit(solution)/shard_map/ppermute | solution.py:407
  24.0 1.3 %collective-permute-done.rest_0_ = f32[9,80,128]{2,1,0:T(8,128)S(1)} collective-permute-done((f32[9,80,128]{2,1,0:T(8,128)}, f32[9,80,128]{2,1,0:T(8,128)S(1)}, u32[]{:S(2)}, u32[]{:S(2)}) %collective-permute-start) | collective-permute-done | bytes 368672 | tf_op jit(solution)/shard_map/ppermute | solution.py:394
  25.4 1.3 %collective-permute-start.3 = (f32[4,80,128]{2,1,0:T(8,128)S(1)}, f32[4,80,128]{2,1,0:T(8,128)S(1)}, u32[]{:S(2)}, u32[]{:S(2)}) collective-permute-start(f32[4,80,128]{2,1,0:T(8,128)S(1)} %pad_maximum_fusion.4), channel_id=1, source_target_pairs={{1,0},{2,1},{3,2},{5,4},{6,5},{7,6},{9,8},{10,9},{11,10},{13,12},{... | collective-permute-start | bytes 491528 | tf_op jit(solution)/shard_map/ppermute | solution.py:407
  26.7 1.5 %collective-permute-done.10 = f32[1,2,264,128]{3,2,0,1:T(8,128)S(1)} collective-permute-done((f32[1,2,264,128]{3,2,0,1:T(8,128)S(1)}, f32[1,2,264,128]{3,2,0,1:T(8,128)S(1)}, u32[]{:S(2)}, u32[]{:S(2)}) %collective-permute-start.10) | collective-permute-done | bytes 270368 | tf_op jit(solution)/shard_map/ppermute | solution.py:420
  28.3 0.4 collective-permute-start.11
  28.7 4.4 %collective-permute-start.2 = (f32[4,80,128]{2,1,0:T(8,128)S(1)}, f32[4,80,128]{2,1,0:T(8,128)S(1)}, u32[]{:S(2)}, u32[]{:S(2)}) collective-permute-start(f32[4,80,128]{2,1,0:T(8,128)S(1)} %pad_maximum_fusion.3), channel_id=1, source_target_pairs={{0,1},{1,2},{2,3},{4,5},{5,6},{6,7},{8,9},{9,10},{10,11},{12,13},{... | collective-permute-start | bytes 491528 | tf_op jit(solution)/shard_map/ppermute | solution.py:407
  33.1 0.1 pad_maximum_fusion.1
  33.3 3.4 %collective-permute-done.2.rest_2_ = f32[4,80,128]{2,1,0:T(8,128)S(1)} collective-permute-done((f32[4,80,128]{2,1,0:T(8,128)S(1)}, f32[4,80,128]{2,1,0:T(8,128)S(1)}, u32[]{:S(2)}, u32[]{:S(2)}) %collective-permute-start.2) | collective-permute-done | bytes 163872 | tf_op jit(solution)/shard_map/ppermute | solution.py:407
  36.7 0.1 pad_maximum_fusion
  36.8 0.1 collective-permute-start.4
  36.9 0.8 %collective-permute-done.11 = f32[2,2,264,128]{3,2,0,1:T(8,128)S(1)} collective-permute-done((f32[2,2,264,128]{3,2,0,1:T(8,128)S(1)}, f32[2,2,264,128]{3,2,0,1:T(8,128)S(1)}, u32[]{:S(2)}, u32[]{:S(2)}) %collective-permute-start.11) | collective-permute-done | bytes 540704 | tf_op jit(solution)/shard_map/ppermute | solution.py:420
  37.8 0.1 slice_bitcast_fusion
  37.9 2.0 %prepare.2 = (bf16[16,96,2688]{2,1,0:T(8,128)(2,1)S(1)}, f32[128,2688]{1,0:T(8,128)S(1)}) custom-call(f32[9,80,128]{2,1,0:T(8,128)S(1)} %copy-done, f32[9,80,128]{2,1,0:T(8,128)S(1)} %collective-permute-done.5.rest_1_, f32[4,80,128]{2,1,0:T(8,128)S(1)} %collective-permute-done.6.rest_2_, f32[4,80,128]{2,1,0:T(8,128)S(1)} %collective-permute-done.7.rest_3_, ...), custom_call_target="tpu_custom_call" | custom-call | tf_op jit(solution)/shard_map/prepare/pallas_call | solution.py:427
  40.0 2.0 %prepare.3 = (bf16[16,96,2688]{2,1,0:T(8,128)(2,1)S(1)}, f32[128,2688]{1,0:T(8,128)S(1)}) custom-call(f32[9,80,128]{2,1,0:T(8,128)S(1)} %collective-permute-done.rest_0_, f32[9,80,128]{2,1,0:T(8,128)S(1)} %collective-permute-done.1.rest_1_, f32[4,80,128]{2,1,0:T(8,128)S(1)} %collective-permute-done.2.rest_2_, ...), custom_call_target="tpu_custom_call", output_to_operand_aliasing={{0}: (5, {}), {1}: (6, {})} | custom-call | tf_op jit(solution)/shard_map/prepare/pallas_call | solution.py:427
  42.1 5.9 %apply.7 = f32[8,64,128]{2,1,0:T(8,128)S(1)} custom-call(f32[4,264,128]{2,1,0:T(8,128)S(1)} %get-tuple-element.28.rest_0_, f32[4,264,128]{2,1,0:T(8,128)S(1)} %collective-permute-done.12.rest_1_, bf16[256,512]{1,0:T(8,128)(2,1)S(1)} %get-tuple-element.17.rest_1_.rest_2_, bf16[16,96,2688]{2,1,0:T(8,128)(2,1)S(1)} %get-tuple-element.24.rest_2_.rest_3_, ...), custom_call_target="tpu_custom_call" | custom-call | tf_op jit(solution)/shard_map/apply/pallas_call | solution.py:443
  48.0 1.5 %collective-permute-start.15 = (f32[8,64,128]{2,1,0:T(8,128)S(1)}, f32[8,64,128]{2,1,0:T(8,128)S(1)}, u32[]{:S(2)}, u32[]{:S(2)}) collective-permute-start(f32[8,64,128]{2,1,0:T(8,128)S(1)} %apply.7), channel_id=1, source_target_pairs={{0,24},{4,28},{8,16},{12,20},{16,8},{20,12},{24,0},{28,4},{1,25},{... | collective-permute-start | bytes 786440 | tf_op jit(solution)/shard_map/ppermute | solution.py:394
  49.5 6.1 %apply.6 = f32[8,64,128]{2,1,0:T(8,128)S(1)} custom-call(f32[4,264,128]{2,1,0:T(8,128)S(1)} %get-tuple-element.28.rest_0_, f32[4,264,128]{2,1,0:T(8,128)S(1)} %collective-permute-done.12.rest_1_, bf16[256,512]{1,0:T(8,128)(2,1)S(1)} %get-tuple-element.17.rest_1_.rest_2_, bf16[16,96,2688]{2,1,0:T(8,128)(2,1)S(1)} %get-tuple-element.24.rest_2_.rest_3_, ...), custom_call_target="tpu_custom_call" | custom-call | tf_op jit(solution)/shard_map/apply/pallas_call | solution.py:443
  55.6 1.6 %collective-permute-start.14 = (f32[8,64,128]{2,1,0:T(8,128)S(1)}, f32[8,64,128]{2,1,0:T(8,128)S(1)}, u32[]{:S(2)}, u32[]{:S(2)}) collective-permute-start(f32[8,64,128]{2,1,0:T(8,128)S(1)} %apply.6), channel_id=1, source_target_pairs={{0,16},{4,20},{8,24},{12,28},{16,0},{20,4},{24,8},{28,12},{1,17},{... | collective-permute-start | bytes 786440 | tf_op jit(solution)/shard_map/ppermute | solution.py:394
  57.2 5.9 %apply.5 = f32[8,64,128]{2,1,0:T(8,128)S(1)} custom-call(f32[4,264,128]{2,1,0:T(8,128)S(1)} %get-tuple-element.28.rest_0_, f32[4,264,128]{2,1,0:T(8,128)S(1)} %collective-permute-done.12.rest_1_, bf16[256,512]{1,0:T(8,128)(2,1)S(1)} %get-tuple-element.17.rest_1_.rest_2_, bf16[16,96,2688]{2,1,0:T(8,128)(2,1)S(1)} %get-tuple-element.24.rest_2_.rest_3_, ...), custom_call_target="tpu_custom_call" | custom-call | tf_op jit(solution)/shard_map/apply/pallas_call | solution.py:443
  63.1 0.6 collective-permute-start.13
  63.7 5.9 %apply.4.rest_0_ = f32[8,64,128]{2,1,0:T(8,128)S(1)} custom-call(f32[2,264,128]{2,1,0:T(8,128)S(1)} %get-tuple-element.16.rest_0_, bf16[256,512]{1,0:T(8,128)(2,1)S(1)} %get-tuple-element.17.rest_1_.rest_2_, bf16[16,96,2688]{2,1,0:T(8,128)(2,1)S(1)} %get-tuple-element.24.rest_2_.rest_3_, f32[128,2688]{1,0:T(8,128)S(1)} %get-tuple-element.25.rest_3_.rest_4_), custom_call_target="tpu_custom_call" | custom-call | tf_op jit(solution)/shard_map/apply/pallas_call | solution.py:443
  69.6 1.6 %collective-permute-done.13.rest_1_ = f32[8,64,128]{2,1,0:T(8,128)S(1)} collective-permute-done((f32[8,64,128]{2,1,0:T(8,128)S(1)}, f32[8,64,128]{2,1,0:T(8,128)S(1)}, u32[]{:S(2)}, u32[]{:S(2)}) %collective-permute-start.13) | collective-permute-done | bytes 262176 | tf_op jit(solution)/shard_map/ppermute | solution.py:394
  71.3 3.0 %unpack.1 = f32[2048,128]{1,0:T(8,128)} custom-call(f32[8,64,128]{2,1,0:T(8,128)S(1)} %apply.4.rest_0_, f32[8,64,128]{2,1,0:T(8,128)S(1)} %collective-permute-done.13.rest_1_, f32[8,64,128]{2,1,0:T(8,128)S(1)} %collective-permute-done.14.rest_2_, f32[8,64,128]{2,1,0:T(8,128)S(1)} %collective-permute-done.15.rest_3_), custom_call_target="tpu_custom_call" | custom-call | tf_op jit(solution)/shard_map/unpack/pallas_call | solution.py:459
  (33 shorter events, 0.5 us)
Async XLA Ops:
  0.0 9.0 %copy-start.1 = (f32[2,32,32,32]{3,2,1,0:T(8,128)S(1)}, f32[2,32,32,32]{3,2,1,0:T(8,128)}, u32[]{:S(2)}) copy-start(f32[2,32,32,32]{3,2,1,0:T(8,128)} %coupling_ref.1) | copy-start | bytes 786436
  0.0 9.0 %copy-start.2 = (s32[2,32]{1,0:T(2,128)S(1)}, s32[2,32]{1,0:T(2,128)}, u32[]{:S(2)}) copy-start(s32[2,32]{1,0:T(2,128)} %source_ref.1) | copy-start | bytes 772
  0.0 9.0 %copy-start.3 = (s32[2,32]{1,0:T(2,128)S(1)}, s32[2,32]{1,0:T(2,128)}, u32[]{:S(2)}) copy-start(s32[2,32]{1,0:T(2,128)} %expansion_ref.1) | copy-start | bytes 772
  4.4 5.1 %copy-start = (f32[9,80,128]{2,1,0:T(8,128)S(1)}, f32[9,80,128]{2,1,0:T(8,128)}, u32[]{:S(2)}) copy-start(f32[9,80,128]{2,1,0:T(8,128)} %get-tuple-element.20.rest_0_) | copy-start | bytes 1105924
  4.4 13.6 %collective-permute-start.5 = (f32[9,80,128]{2,1,0:T(8,128)}, f32[9,80,128]{2,1,0:T(8,128)S(1)}, u32[]{:S(2)}, u32[]{:S(2)}) collective-permute-start(f32[9,80,128]{2,1,0:T(8,128)} %get-tuple-element.21), channel_id=1, source_target_pairs={{0,24},{4,28},{8,16},{12,20},{16,8},{20,12},{24,0},{28,4},{1,25},{... | collective-permute-start | bytes 1105928 | tf_op jit(solution)/shard_map/ppermute | solution.py:394
  8.4 17.0 %collective-permute-start = (f32[9,80,128]{2,1,0:T(8,128)}, f32[9,80,128]{2,1,0:T(8,128)S(1)}, u32[]{:S(2)}, u32[]{:S(2)}) collective-permute-start(f32[9,80,128]{2,1,0:T(8,128)} %get-tuple-element.18), channel_id=1, source_target_pairs={{0,8},{4,12},{8,0},{12,4},{16,24},{20,28},{24,16},{28,20},{1,9},{5... | collective-permute-start | bytes 1105928 | tf_op jit(solution)/shard_map/ppermute | solution.py:394
  8.9 16.5 %collective-permute-start.1 = (f32[9,80,128]{2,1,0:T(8,128)}, f32[9,80,128]{2,1,0:T(8,128)S(1)}, u32[]{:S(2)}, u32[]{:S(2)}) collective-permute-start(f32[9,80,128]{2,1,0:T(8,128)} %get-tuple-element.19), channel_id=1, source_target_pairs={{0,16},{4,20},{8,24},{12,28},{16,0},{20,4},{24,8},{28,12},{1,17},{... | collective-permute-start | bytes 1105928 | tf_op jit(solution)/shard_map/ppermute | solution.py:394
  9.4 1.4 %collective-permute-start.9 = (f32[1,264,128]{2,1,0:T(8,128)S(1)}, f32[1,264,128]{2,1,0:T(8,128)S(1)}, u32[]{:S(2)}, u32[]{:S(2)}) collective-permute-start(f32[1,264,128]{2,1,0:T(8,128)S(1)} %get-tuple-element.38), channel_id=1, source_target_pairs={{0,4},{4,0},{8,12},{12,8},{16,20},{20,16},{24,28},{28,24},{1,5},{5... | collective-permute-start | bytes 405512 | tf_op jit(solution)/shard_map/ppermute | solution.py:397
  10.8 17.4 %collective-permute-start.10 = (f32[1,2,264,128]{3,2,0,1:T(8,128)S(1)}, f32[1,2,264,128]{3,2,0,1:T(8,128)S(1)}, u32[]{:S(2)}, u32[]{:S(2)}) collective-permute-start(f32[1,2,264,128]{3,2,0,1:T(8,128)S(1)} %maximum_bitcast_fusion), channel_id=1, source_target_pairs={{0,8},{4,20},{8,0},{12,28},{16,24},{20,4},{24,16},{28,12},{1,9},{5... | collective-permute-start | bytes 811016 | tf_op jit(solution)/shard_map/ppermute | solution.py:420
  18.1 10.2 %collective-permute-start.7 = (f32[4,80,128]{2,1,0:T(8,128)S(1)}, f32[4,80,128]{2,1,0:T(8,128)S(1)}, u32[]{:S(2)}, u32[]{:S(2)}) collective-permute-start(f32[4,80,128]{2,1,0:T(8,128)S(1)} %pad_maximum_fusion.6), channel_id=1, source_target_pairs={{1,0},{2,1},{3,2},{5,4},{6,5},{7,6},{9,8},{10,9},{11,10},{13,12},{... | collective-permute-start | bytes 491528 | tf_op jit(solution)/shard_map/ppermute | solution.py:407
  19.4 13.7 %collective-permute-start.6 = (f32[4,80,128]{2,1,0:T(8,128)S(1)}, f32[4,80,128]{2,1,0:T(8,128)S(1)}, u32[]{:S(2)}, u32[]{:S(2)}) collective-permute-start(f32[4,80,128]{2,1,0:T(8,128)S(1)} %pad_maximum_fusion.5), channel_id=1, source_target_pairs={{0,1},{1,2},{2,3},{4,5},{5,6},{6,7},{8,9},{9,10},{10,11},{12,13},{... | collective-permute-start | bytes 491528 | tf_op jit(solution)/shard_map/ppermute | solution.py:407
  25.4 7.8 %collective-permute-start.3 = (f32[4,80,128]{2,1,0:T(8,128)S(1)}, f32[4,80,128]{2,1,0:T(8,128)S(1)}, u32[]{:S(2)}, u32[]{:S(2)}) collective-permute-start(f32[4,80,128]{2,1,0:T(8,128)S(1)} %pad_maximum_fusion.4), channel_id=1, source_target_pairs={{1,0},{2,1},{3,2},{5,4},{6,5},{7,6},{9,8},{10,9},{11,10},{13,12},{... | collective-permute-start | bytes 491528 | tf_op jit(solution)/shard_map/ppermute | solution.py:407
  28.3 9.4 %collective-permute-start.11 = (f32[2,2,264,128]{3,2,0,1:T(8,128)S(1)}, f32[2,2,264,128]{3,2,0,1:T(8,128)S(1)}, u32[]{:S(2)}, u32[]{:S(2)}) collective-permute-start(f32[2,2,264,128]{3,2,0,1:T(8,128)S(1)} %pad_maximum_fusion.2), channel_id=1, source_target_pairs={{0,16},{4,12},{8,24},{12,4},{16,0},{20,28},{24,8},{28,20},{1,17},{... | collective-permute-start | bytes 1622024 | tf_op jit(solution)/shard_map/ppermute | solution.py:420
  28.7 8.0 %collective-permute-start.2 = (f32[4,80,128]{2,1,0:T(8,128)S(1)}, f32[4,80,128]{2,1,0:T(8,128)S(1)}, u32[]{:S(2)}, u32[]{:S(2)}) collective-permute-start(f32[4,80,128]{2,1,0:T(8,128)S(1)} %pad_maximum_fusion.3), channel_id=1, source_target_pairs={{0,1},{1,2},{2,3},{4,5},{5,6},{6,7},{8,9},{9,10},{10,11},{12,13},{... | collective-permute-start | bytes 491528 | tf_op jit(solution)/shard_map/ppermute | solution.py:407
  33.2 4.7 %collective-permute-start.8 = (f32[26,80,128]{2,1,0:T(8,128)S(1)}, f32[26,80,128]{2,1,0:T(8,128)S(1)}, u32[]{:S(2)}, u32[]{:S(2)}) collective-permute-start(f32[26,80,128]{2,1,0:T(8,128)S(1)} %pad_maximum_fusion.1), channel_id=1, source_target_pairs={{0,4},{4,0},{8,12},{12,8},{16,20},{20,16},{24,28},{28,24},{1,5},{5... | collective-permute-start | bytes 3194888 | tf_op jit(solution)/shard_map/ppermute | solution.py:397
  36.8 3.2 %collective-permute-start.4 = (f32[26,80,128]{2,1,0:T(8,128)S(1)}, f32[26,80,128]{2,1,0:T(8,128)S(1)}, u32[]{:S(2)}, u32[]{:S(2)}) collective-permute-start(f32[26,80,128]{2,1,0:T(8,128)S(1)} %pad_maximum_fusion), channel_id=1, source_target_pairs={{0,4},{4,0},{8,12},{12,8},{16,20},{20,16},{24,28},{28,24},{1,5},{5... | collective-permute-start | bytes 3194888 | tf_op jit(solution)/shard_map/ppermute | solution.py:397
  37.9 4.2 %collective-permute-start.12 = (f32[4,264,128]{2,1,0:T(8,128)S(1)}, f32[4,264,128]{2,1,0:T(8,128)S(1)}, u32[]{:S(2)}, u32[]{:S(2)}) collective-permute-start(f32[4,264,128]{2,1,0:T(8,128)S(1)} %get-tuple-element.27), channel_id=1, source_target_pairs={{0,4},{4,0},{8,12},{12,8},{16,20},{20,16},{24,28},{28,24},{1,5},{5... | collective-permute-start | bytes 1622024 | tf_op jit(solution)/shard_map/ppermute | solution.py:397
  48.0 21.6 %collective-permute-start.15 = (f32[8,64,128]{2,1,0:T(8,128)S(1)}, f32[8,64,128]{2,1,0:T(8,128)S(1)}, u32[]{:S(2)}, u32[]{:S(2)}) collective-permute-start(f32[8,64,128]{2,1,0:T(8,128)S(1)} %apply.7), channel_id=1, source_target_pairs={{0,24},{4,28},{8,16},{12,20},{16,8},{20,12},{24,0},{28,4},{1,25},{... | collective-permute-start | bytes 786440 | tf_op jit(solution)/shard_map/ppermute | solution.py:394
  55.6 14.0 %collective-permute-start.14 = (f32[8,64,128]{2,1,0:T(8,128)S(1)}, f32[8,64,128]{2,1,0:T(8,128)S(1)}, u32[]{:S(2)}, u32[]{:S(2)}) collective-permute-start(f32[8,64,128]{2,1,0:T(8,128)S(1)} %apply.6), channel_id=1, source_target_pairs={{0,16},{4,20},{8,24},{12,28},{16,0},{20,4},{24,8},{28,12},{1,17},{... | collective-permute-start | bytes 786440 | tf_op jit(solution)/shard_map/ppermute | solution.py:394
  63.1 8.2 %collective-permute-start.13 = (f32[8,64,128]{2,1,0:T(8,128)S(1)}, f32[8,64,128]{2,1,0:T(8,128)S(1)}, u32[]{:S(2)}, u32[]{:S(2)}) collective-permute-start(f32[8,64,128]{2,1,0:T(8,128)S(1)} %apply.5), channel_id=1, source_target_pairs={{0,8},{4,12},{8,0},{12,4},{16,24},{20,28},{24,16},{28,20},{1,9},{5... | collective-permute-start | bytes 786440 | tf_op jit(solution)/shard_map/ppermute | solution.py:394
